TPU v7x, 128 devices: a whole 4x4x4 slice. The times are simulated.
128 devices in a mesh: ball: 16 (over x, y), hid: 8 (over z, core).
Axes of the slice: x: 4, y: 4, z: 4, core: 2. Of those that a mesh axis runs over, the one named last changes fastest.
Arguments:
- points: bfloat16 [131072, 256], P(('ball', 'hid')), may hold values from -6 to 6
- tree_slot: int32 [131072], P(('ball', 'hid')), may hold values from 0 to 131071, as said below
- rotated_slot: int32 [131072], P(('ball', 'hid')), may hold values from 0 to 131071, as said below
- fine_norm: float32 [2, 2, 256], replicated, may hold values from 0.1 to 1.9
- fine_qkv: bfloat16 [2, 3, 256, 256], replicated, may hold values from -2 to 2
- fine_out: bfloat16 [2, 256, 256], replicated, may hold values from -0.375 to 0.375
- fine_gate_up: bfloat16 [2, 2, 256, 1024], replicated, may hold values from -0.375 to 0.375
- fine_down: bfloat16 [2, 1024, 256], replicated, may hold values from -0.1875 to 0.1875
- pool_weight: bfloat16 [4096, 1024], P('hid'), may hold values from -0.09375 to 0.09375
- coarse_norm: float32 [2, 1024], replicated, may hold values from 0.1 to 1.9
- coarse_qkv: bfloat16 [3, 1024, 1024], P(None, None, 'hid'), may hold values from -2 to 2
- coarse_out: bfloat16 [1024, 1024], P('hid'), may hold values from -0.1875 to 0.1875
- coarse_gate_up: bfloat16 [2, 1024, 4096], P(None, None, 'hid'), may hold values from -0.1875 to 0.1875
- coarse_down: bfloat16 [4096, 1024], P('hid'), may hold values from -0.09375 to 0.09375
- unpool_weight: bfloat16 [1024, 4096], P(None, 'hid'), may hold values from -0.1875 to 0.1875
Outputs:
- joined: bfloat16 [131072, 256], P(('ball', 'hid'))
Inputs may be any that keep to these rules, and one draw needn't show every extreme that they name: `tree_slot`: a permutation of the 131072 tree positions; the points of one device go to at most 16 positions of any one device and to exactly 16 positions of some device. `rotated_slot`: a permutation of the 131072 rotated positions; the points of one device go to at most 16 positions of any one device and to exactly 16 positions of some device.
All inputs are finite; a program needn't handle non-finite values.
Results may differ from a plain program's by a relative error of at most 0.033.
Values may be sent and summed in bfloat16 or wider, within the bound.
No kernel may reach another device: no remote copies, remote signals or barrier semaphores. Data moves between devices by JAX's collectives and lax.ppermute only.
A program may use at most 128 MiB of HBM per device.

v0:
```python
import math

import jax
import jax.numpy as jnp
from jax import lax
from jax.sharding import PartitionSpec as P

C = 256
FHEADS = 8
BALL = 256
POOL = 16
CC = 1024
CHEADS = 16
CBALL = 256


epsilon = 1e-06


def rms_scale(values, gain):
    widened = values.astype(jnp.float32)
    mean_square = jnp.mean(widened * widened, axis=-1, keepdims=True)
    return (widened * lax.rsqrt(mean_square + epsilon) * gain).astype(jnp.bfloat16)


def attend(projected, head_size, ball_size):
    row_count = projected.shape[1]
    inner_width = projected.shape[2]
    head_count = inner_width // head_size
    split_heads = projected.reshape(3, row_count // ball_size, ball_size, head_count, head_size)
    scores = jnp.einsum(
        "bqhd,bkhd->bhqk", split_heads[0], split_heads[1], preferred_element_type=jnp.float32
    ) / math.sqrt(head_size)
    weights = jax.nn.softmax(scores, axis=-1).astype(jnp.bfloat16)
    mixed = jnp.einsum(
        "bhqk,bkhd->bqhd", weights, split_heads[2], preferred_element_type=jnp.float32
    )
    return mixed.astype(jnp.bfloat16).reshape(row_count, inner_width)


def fine_block(states, block_gains, qkv_weight, out_weight, gate_up_weight, down_weight):
    normed = rms_scale(states, block_gains[0])
    projected = jnp.einsum(
        "nc,jcd->jnd", normed, qkv_weight, preferred_element_type=jnp.float32
    ).astype(jnp.bfloat16)
    mixed = attend(projected, C // FHEADS, BALL)
    attended = (
        states.astype(jnp.float32) + jnp.dot(mixed, out_weight, preferred_element_type=jnp.float32)
    ).astype(jnp.bfloat16)
    normed_again = rms_scale(attended, block_gains[1])
    gate_value = jnp.dot(normed_again, gate_up_weight[0], preferred_element_type=jnp.float32)
    upward = jnp.dot(normed_again, gate_up_weight[1], preferred_element_type=jnp.float32)
    hidden = (jax.nn.silu(gate_value) * upward).astype(jnp.bfloat16)
    return (
        attended.astype(jnp.float32)
        + jnp.dot(hidden, down_weight, preferred_element_type=jnp.float32)
    ).astype(jnp.bfloat16)


def arrange(states, target):
    row_count = states.shape[0]
    device_count = lax.axis_size("ball") * lax.axis_size("hid")
    capacity = 2 * row_count // device_count
    owners = target // row_count
    within = target % row_count
    ordering = jnp.argsort(owners, stable=True)
    owner_sorted = owners[ordering]
    matches = owner_sorted[:, None] == jnp.arange(device_count, dtype=jnp.int32)[None, :]
    tallies = jnp.sum(matches.astype(jnp.int32), axis=0)
    starts = jnp.cumsum(tallies) - tallies
    first_index = jnp.sum(jnp.where(matches, starts[None, :], 0), axis=1)
    slot_index = owner_sorted * capacity + jnp.arange(row_count, dtype=jnp.int32) - first_index
    send_rows = (
        jnp.zeros((device_count * capacity, states.shape[1]), states.dtype)
        .at[slot_index]
        .set(states[ordering])
    )
    send_place = (
        jnp.full((device_count * capacity,), row_count, jnp.int32)
        .at[slot_index]
        .set(within[ordering])
    )
    return (send_rows, send_place, ordering, slot_index)


def deliver(states, target):
    send_rows, send_place, ordering, slot_index = arrange(states, target)
    got_rows, got_place = (
        lax.all_to_all(send_rows, ("ball", "hid"), split_axis=0, concat_axis=0, tiled=True),
        lax.all_to_all(send_place, ("ball", "hid"), split_axis=0, concat_axis=0, tiled=True),
    )
    placed = jnp.zeros_like(states).at[got_place].set(got_rows, mode="drop")
    return (placed, got_place, ordering, slot_index)


def return_rows(states, got_place, ordering, slot_index):
    replies = jnp.take(states, got_place, axis=0, mode="fill", fill_value=0)
    returned = lax.all_to_all(replies, ("ball", "hid"), split_axis=0, concat_axis=0, tiled=True)
    return jnp.zeros_like(states).at[ordering].set(returned[slot_index])


def body(
    points,
    tree_slot,
    rotated_slot,
    fine_norm,
    fine_qkv,
    fine_out,
    fine_gate_up,
    fine_down,
    pool_weight,
    coarse_norm,
    coarse_qkv,
    coarse_out,
    coarse_gate_up,
    coarse_down,
    unpool_weight,
):
    ordered, _, _, _ = deliver(points, tree_slot)
    block_one = fine_block(
        ordered, fine_norm[0], fine_qkv[0], fine_out[0], fine_gate_up[0], fine_down[0]
    )
    rotated, got_place, ordering, slot_index = deliver(block_one, rotated_slot)
    second_rotated = fine_block(
        rotated, fine_norm[1], fine_qkv[1], fine_out[1], fine_gate_up[1], fine_down[1]
    )
    block_two = return_rows(second_rotated, got_place, ordering, slot_index)
    coarse_count = block_two.shape[0] // POOL
    hid_count = lax.axis_size("hid")
    grouped = block_two.reshape(coarse_count, POOL * C)
    children = lax.all_to_all(
        grouped.reshape(coarse_count, hid_count, -1), "hid", split_axis=1, concat_axis=0, tiled=True
    )
    children = children.reshape(coarse_count * hid_count, -1)
    pooled = lax.psum_scatter(
        jnp.dot(children, pool_weight, preferred_element_type=jnp.float32).astype(jnp.bfloat16),
        "hid",
        scatter_dimension=0,
        tiled=True,
    )
    coarse_head = CC // CHEADS
    normed = rms_scale(lax.all_gather(pooled, "hid", axis=0, tiled=True), coarse_norm[0])
    projected = jnp.einsum(
        "nc,jcd->jnd", normed, coarse_qkv, preferred_element_type=jnp.float32
    ).astype(jnp.bfloat16)
    mixed = attend(projected, coarse_head, CBALL)
    coarse_mid = (
        pooled.astype(jnp.float32)
        + lax.psum_scatter(
            jnp.dot(mixed, coarse_out, preferred_element_type=jnp.float32).astype(jnp.bfloat16),
            "hid",
            scatter_dimension=0,
            tiled=True,
        ).astype(jnp.float32)
    ).astype(jnp.bfloat16)
    normed = rms_scale(lax.all_gather(coarse_mid, "hid", axis=0, tiled=True), coarse_norm[1])
    gate_value = jnp.dot(normed, coarse_gate_up[0], preferred_element_type=jnp.float32)
    upward = jnp.dot(normed, coarse_gate_up[1], preferred_element_type=jnp.float32)
    hidden = (jax.nn.silu(gate_value) * upward).astype(jnp.bfloat16)
    coarse_done = (
        coarse_mid.astype(jnp.float32)
        + lax.psum_scatter(
            jnp.dot(hidden, coarse_down, preferred_element_type=jnp.float32).astype(jnp.bfloat16),
            "hid",
            scatter_dimension=0,
            tiled=True,
        ).astype(jnp.float32)
    ).astype(jnp.bfloat16)
    spread = jnp.dot(
        lax.all_gather(coarse_done, "hid", axis=0, tiled=True),
        unpool_weight,
        preferred_element_type=jnp.float32,
    ).astype(jnp.bfloat16)
    children_out = lax.all_to_all(spread, "hid", split_axis=0, concat_axis=1, tiled=True)
    restored = children_out.reshape(block_two.shape[0], block_two.shape[1])
    return (block_two.astype(jnp.float32) + restored.astype(jnp.float32)).astype(jnp.bfloat16)


def solution(mesh):
    placed = (
        P(("ball", "hid"), None),
        P(("ball", "hid")),
        P(("ball", "hid")),
        P(),
        P(),
        P(),
        P(),
        P(),
        P("hid", None),
        P(),
        P(None, None, "hid"),
        P("hid", None),
        P(None, None, "hid"),
        P("hid", None),
        P(None, "hid"),
    )
    return jax.shard_map(
        body, mesh=mesh, in_specs=placed, out_specs=P(("ball", "hid"), None), check_vma=False
    )
```

profile of v0, /device:TPU:1, one launch (start us, length us, event | category | flops | bytes accessed | tf_op | source)
XLA Modules:
  0.0 470.2 jit_solution(6584620056718369501)
XLA Ops:
  16.5 4.5 gather_fusion.3
  26.8 11.5 %all-to-all-start.1 = ((s32[128,16,1]{1,2,0:T(1,128)}), s32[128,16,1]{1,2,0:T(1,128)S(1)}, u32[]{:S(2)}, u32[]{:S(2)}) async-start(s32[128,16,1]{1,2,0:T(1,128)} %bitcast.11), calls=%async_computation.1 | async-start | bytes 131072 | tf_op jit(solution)/shard_map/all_to_all | solution.py:90
  47.3 12.7 %scatter_custom_fusion.2 = bf16[2048,256]{1,0:T(8,128)(2,1)} fusion(s32[1024]{0:T(1024)S(1)} %bitcast.172, bf16[1024,256]{1,0:T(8,128)(2,1)} %param.15, s32[1024]{0:T(1024)S(1)} %fusion.166, bf16[]{:T(256)} %constant.83.clone.1), kind=kCustom, calls=%fused_computation.126 | custom fusion | bytes 1049088 | tf_op jit(solution)/shard_map/scatter | solution.py:76
  59.9 9.8 %all-to-all-start.2 = ((bf16[128,16,256]{2,1,0:T(8,128)(2,1)}), bf16[128,16,256]{2,1,0:T(8,128)(2,1)S(1)}, u32[]{:S(2)}, u32[]{:S(2)}) async-start(bf16[128,16,256]{2,1,0:T(8,128)(2,1)} %bitcast.13), calls=%async_computation.2 | async-start | bytes 2097152 | tf_op jit(solution)/shard_map/all_to_all | solution.py:89
  81.9 7.1 %all-to-all-done.2 = bf16[128,16,256]{2,1,0:T(8,128)(2,1)S(1)} async-done(((bf16[128,16,256]{2,1,0:T(8,128)(2,1)}), bf16[128,16,256]{2,1,0:T(8,128)(2,1)S(1)}, u32[]{:S(2)}, u32[]{:S(2)}) %all-to-all-start.2) | async-done | bytes 1048608 | tf_op jit(solution)/shard_map/all_to_all | solution.py:89
  93.5 9.4 %scatter_custom_fusion.3 = bf16[1024,256]{1,0:T(8,128)(2,1)S(1)} fusion(s32[2048]{0:T(1024)S(1)} %bitcast.166, bf16[2048,256]{1,0:T(8,128)(2,1)S(1)} %bitcast.147, bf16[]{:T(256)} %constant.83.clone.1), kind=kCustom, calls=%fused_computation.177 | custom fusion | bytes 524290 | tf_op jit(solution)/shard_map/scatter | solution.py:92
  110.3 7.2 %fusion.187 = (f32[4,8,256]{2,1,0:T(8,128)S(1)}, f32[4,8,256,256]{2,3,1,0:T(8,128)}) fusion(bf16[4,256,8,32]{1,0,3,2:T(4,128)(2,1)} %squeeze.70, bf16[4,256,8,32]{1,0,3,2:T(4,128)(2,1)S(1)} %squeeze.69), kind=kOutput, calls=%fused_computation.235 | convolution fusion | flops 140509440 | bytes 9469952 | tf_op jit(solution)/shard_map/sub | solution.py:34
  131.0 9.5 %scatter_custom_fusion.4 = bf16[2048,256]{1,0:T(8,128)(2,1)} fusion(s32[1024]{0:T(1024)S(1)} %bitcast.160, bf16[1024,256]{1,0:T(8,128)(2,1)S(1)} %copy.127, s32[1024]{0:T(1024)S(1)} %get-tuple-element.28, bf16[]{:T(256)} %constant.83.clone.1), kind=kCustom, calls=%fused_computation.124 | custom fusion | bytes 1048578 | tf_op jit(solution)/shard_map/scatter | solution.py:76
  140.5 9.9 %all-to-all-start.3 = ((bf16[128,16,256]{2,1,0:T(8,128)(2,1)}), bf16[128,16,256]{2,1,0:T(8,128)(2,1)S(1)}, u32[]{:S(2)}, u32[]{:S(2)}) async-start(bf16[128,16,256]{2,1,0:T(8,128)(2,1)} %bitcast.25), calls=%async_computation.3 | async-start | bytes 2097152 | tf_op jit(solution)/shard_map/all_to_all | solution.py:89
  151.3 18.3 %all-to-all-done.3 = bf16[128,16,256]{2,1,0:T(8,128)(2,1)S(1)} async-done(((bf16[128,16,256]{2,1,0:T(8,128)(2,1)}), bf16[128,16,256]{2,1,0:T(8,128)(2,1)S(1)}, u32[]{:S(2)}, u32[]{:S(2)}) %all-to-all-start.3) | async-done | bytes 1048608 | tf_op jit(solution)/shard_map/all_to_all | solution.py:89
  169.6 9.8 %scatter_custom_fusion.5 = bf16[1024,256]{1,0:T(8,128)(2,1)S(1)} fusion(s32[2048]{0:T(1024)S(1)} %bitcast.158, bf16[2048,256]{1,0:T(8,128)(2,1)S(1)} %bitcast.148, bf16[]{:T(256)} %constant.83.clone.1), kind=kCustom, calls=%fused_computation.175 | custom fusion | bytes 524290 | tf_op jit(solution)/shard_map/scatter | solution.py:92
  186.8 7.3 %fusion.196 = (f32[4,8,256]{2,1,0:T(8,128)S(1)}, f32[4,8,256,256]{2,3,1,0:T(8,128)}) fusion(bf16[4,256,8,32]{1,0,3,2:T(4,128)(2,1)} %squeeze.78, bf16[4,256,8,32]{1,0,3,2:T(4,128)(2,1)S(1)} %squeeze.77), kind=kOutput, calls=%fused_computation.236 | convolution fusion | flops 140509440 | bytes 9469952 | tf_op jit(solution)/shard_map/sub | solution.py:34
  207.3 7.5 %gather_fusion.4 = bf16[2048,256]{1,0:T(8,128)(2,1)S(1)} fusion(bf16[1024,256]{1,0:T(8,128)(2,1)S(1)} %copy.139, s32[2048]{0:T(1024)S(1)} %broadcast_clamp_fusion), kind=kCustom, calls=%fused_computation.6 | custom fusion | bytes 2105344 | tf_op jit(solution)/shard_map/jit(_take)/gather | solution.py:97
  216.1 4.6 all-to-all-start.4
  220.9 19.2 %all-to-all-done.4 = bf16[128,16,256]{2,1,0:T(8,128)(2,1)S(1)} async-done(((bf16[128,16,256]{2,1,0:T(8,128)(2,1)}), bf16[128,16,256]{2,1,0:T(8,128)(2,1)S(1)}, u32[]{:S(2)}, u32[]{:S(2)}) %all-to-all-start.4) | async-done | bytes 1048608 | tf_op jit(solution)/shard_map/all_to_all | solution.py:98
  240.1 8.3 %scatter_custom_fusion.6 = bf16[1024,256]{1,0:T(8,128)(2,1)S(1)} fusion(s32[1024]{0:T(1024)S(1)} %get-tuple-element.29, bf16[2048,256]{1,0:T(8,128)(2,1)S(1)} %bitcast.149, s32[1024]{0:T(1024)S(1)} %broadcast_clamp_fusion.1, bf16[]{:T(256)} %constant.83.clone.1), kind=kCustom, calls=%fused_computation.122 | custom fusion | bytes 524290 | tf_op jit(solution)/shard_map/scatter | solution.py:99
  248.8 12.9 %all_to_all.88 = bf16[64,8,512]{2,0,1:T(8,128)(2,1)S(1)} all-to-all(bf16[64,8,512]{2,0,1:T(8,128)(2,1)S(1)} %copy.140), channel_id=1, replica_groups=mesh['ball'=16,'hid'=8] {'hid'}, dimensions={1} | all-to-all | bytes 1048576 | tf_op jit(solution)/shard_map/all_to_all | solution.py:131
  263.5 25.1 %reduce-scatter.4.cloned.1.call-done = bf16[64,1024]{1,0:T(8,128)(2,1)} async-done(((bf16[512,1024]{1,0:T(8,128)(2,1)}), bf16[64,1024]{1,0:T(8,128)(2,1)}) %reduce-scatter.4.cloned.1.call-update) | async-done | bytes 131088 | tf_op jit(solution)/shard_map/reduce_scatter | solution.py:135
  288.7 27.3 %all-gather.4.cloned.1.call-done = bf16[512,1024]{1,0:T(8,128)(2,1)} async-done(((bf16[64,1024]{1,0:T(8,128)(2,1)}), bf16[512,1024]{1,0:T(8,128)(2,1)}) %all-gather.4.cloned.1.call-update) | async-done | bytes 1048592 | tf_op jit(solution)/shard_map/all_gather | solution.py:142
  322.9 28.7 %reduce-scatter.6.cloned.1.call-done = bf16[64,1024]{1,0:T(8,128)(2,1)} async-done(((bf16[512,1024]{1,0:T(8,128)(2,1)}), bf16[64,1024]{1,0:T(8,128)(2,1)}) %reduce-scatter.6.cloned.1.call-update) | async-done | bytes 131088 | tf_op jit(solution)/shard_map/reduce_scatter | solution.py:149
  353.2 25.8 %all-gather.6.cloned.1.call-done = bf16[512,1024]{1,0:T(8,128)(2,1)} async-done(((bf16[64,1024]{1,0:T(8,128)(2,1)}), bf16[512,1024]{1,0:T(8,128)(2,1)}) %all-gather.6.cloned.1.call-update) | async-done | bytes 1048592 | tf_op jit(solution)/shard_map/all_gather | solution.py:156
  388.3 28.6 %reduce-scatter.8.cloned.1.call-done = bf16[64,1024]{1,0:T(8,128)(2,1)} async-done(((bf16[512,1024]{1,0:T(8,128)(2,1)}), bf16[64,1024]{1,0:T(8,128)(2,1)}) %reduce-scatter.8.cloned.1.call-update) | async-done | bytes 131088 | tf_op jit(solution)/shard_map/reduce_scatter | solution.py:162
  418.6 25.9 %all-gather.8.cloned.1.call-done = bf16[512,1024]{1,0:T(8,128)(2,1)} async-done(((bf16[64,1024]{1,0:T(8,128)(2,1)}), bf16[512,1024]{1,0:T(8,128)(2,1)}) %all-gather.8.cloned.1.call-update) | async-done | bytes 1048592 | tf_op jit(solution)/shard_map/all_gather | solution.py:170
  446.7 12.4 %all_to_all.89 = bf16[8,64,512]{2,1,0:T(8,128)(2,1)S(1)} all-to-all(bf16[8,64,512]{2,1,0:T(8,128)(2,1)S(1)} %bitcast.154), channel_id=1, replica_groups=mesh['ball'=16,'hid'=8] {'hid'}, dimensions={0} | all-to-all | bytes 1048576 | tf_op jit(solution)/shard_map/all_to_all | solution.py:174
  (150 shorter events, 112.8 us)
Async XLA Ops:
  6.5 255.2 %copy-start = (bf16[512,1024]{1,0:T(8,128)(2,1)S(1)}, bf16[512,1024]{1,0:T(8,128)(2,1)}, u32[]{:S(2)}) copy-start(bf16[512,1024]{1,0:T(8,128)(2,1)} %param.23) | copy-start | bytes 3145732
  11.7 26.6 %copy-start.8 = (s32[1024]{0:T(1024)S(1)}, s32[1024]{0:T(1024)}, u32[]{:S(2)}) copy-start(s32[1024]{0:T(1024)} %param.17) | copy-start | bytes 12292
  26.8 33.1 %all-to-all-start.1 = ((s32[128,16,1]{1,2,0:T(1,128)}), s32[128,16,1]{1,2,0:T(1,128)S(1)}, u32[]{:S(2)}, u32[]{:S(2)}) async-start(s32[128,16,1]{1,2,0:T(1,128)} %bitcast.11), calls=%async_computation.1 | async-start | bytes 131072 | tf_op jit(solution)/shard_map/all_to_all | solution.py:90
  47.3 33.2 %copy-start.9 = (f32[2,2,256]{2,1,0:T(2,128)S(1)}, f32[2,2,256]{2,1,0:T(2,128)}, u32[]{:S(2)}) copy-start(f32[2,2,256]{2,1,0:T(2,128)} %param.18) | copy-start | bytes 12292
  59.9 29.0 %all-to-all-start.2 = ((bf16[128,16,256]{2,1,0:T(8,128)(2,1)}), bf16[128,16,256]{2,1,0:T(8,128)(2,1)S(1)}, u32[]{:S(2)}, u32[]{:S(2)}) async-start(bf16[128,16,256]{2,1,0:T(8,128)(2,1)} %bitcast.13), calls=%async_computation.2 | async-start | bytes 2097152 | tf_op jit(solution)/shard_map/all_to_all | solution.py:89
  89.0 51.5 %all-to-all-start = ((s32[128,16,1]{1,2,0:T(1,128)}), s32[128,16,1]{1,2,0:T(1,128)S(1)}, u32[]{:S(2)}, u32[]{:S(2)}) async-start(s32[128,16,1]{1,2,0:T(1,128)} %bitcast.4), calls=%async_computation | async-start | bytes 131072 | tf_op jit(solution)/shard_map/all_to_all | solution.py:90
  110.3 7.3 %copy-start.4 = (bf16[4,256,8,32]{1,0,3,2:T(4,128)(2,1)S(1)}, bf16[4,256,8,32]{1,0,3,2:T(4,128)(2,1)}, u32[]{:S(2)}) copy-start(bf16[4,256,8,32]{1,0,3,2:T(4,128)(2,1)} %squeeze.68) | copy-start | bytes 1572868
  117.5 4.8 %copy-start.12 = (bf16[2,256,256]{2,1,0:T(8,128)(2,1)S(1)}, bf16[2,256,256]{2,1,0:T(8,128)(2,1)}, u32[]{:S(2)}) copy-start(bf16[2,256,256]{2,1,0:T(8,128)(2,1)} %param.20) | copy-start | bytes 786436
  140.5 29.2 %all-to-all-start.3 = ((bf16[128,16,256]{2,1,0:T(8,128)(2,1)}), bf16[128,16,256]{2,1,0:T(8,128)(2,1)S(1)}, u32[]{:S(2)}, u32[]{:S(2)}) async-start(bf16[128,16,256]{2,1,0:T(8,128)(2,1)} %bitcast.25), calls=%async_computation.3 | async-start | bytes 2097152 | tf_op jit(solution)/shard_map/all_to_all | solution.py:89
  186.8 7.3 %copy-start.5 = (bf16[4,256,8,32]{1,0,3,2:T(4,128)(2,1)S(1)}, bf16[4,256,8,32]{1,0,3,2:T(4,128)(2,1)}, u32[]{:S(2)}) copy-start(bf16[4,256,8,32]{1,0,3,2:T(4,128)(2,1)} %squeeze.76) | copy-start | bytes 1572868
  198.7 4.3 copy-start.10
  216.1 24.0 %all-to-all-start.4 = ((bf16[128,16,256]{2,1,0:T(8,128)(2,1)}), bf16[128,16,256]{2,1,0:T(8,128)(2,1)S(1)}, u32[]{:S(2)}, u32[]{:S(2)}) async-start(bf16[128,16,256]{2,1,0:T(8,128)(2,1)} %broadcast_select_fusion), calls=%async_computation.4 | async-start | bytes 2097152 | tf_op jit(solution)/shard_map/all_to_all | solution.py:98
  220.7 68.0 %copy-start.7 = (f32[2,1024]{1,0:T(2,128)S(1)}, f32[2,1024]{1,0:T(2,128)}, u32[]{:S(2)}) copy-start(f32[2,1024]{1,0:T(2,128)} %param.24) | copy-start | bytes 24580
  220.7 67.9 %reduce-scatter.4.cloned.1.call-start = ((), (), s32[]{:S(2)}) async-start(), calls=%async_computation.10 | async-start | bytes 1179648 | tf_op jit(solution)/shard_map/reduce_scatter | solution.py:135
  248.4 69.1 %copy-start.11 = (bf16[3,1024,128]{2,1,0:T(8,128)(2,1)S(1)}, bf16[3,1024,128]{2,1,0:T(8,128)(2,1)}, u32[]{:S(2)}) copy-start(bf16[3,1024,128]{2,1,0:T(8,128)(2,1)} %param.25) | copy-start | bytes 2359300
  263.4 52.6 %all-gather.4.cloned.1.call-start = ((), (), s32[]{:S(2)}) async-start(), calls=%async_computation.11 | async-start | bytes 1179648 | tf_op jit(solution)/shard_map/all_gather | solution.py:142
  288.6 62.9 %reduce-scatter.6.cloned.1.call-start = ((), (), s32[]{:S(2)}) async-start(), calls=%async_computation.12 | async-start | bytes 1179648 | tf_op jit(solution)/shard_map/reduce_scatter | solution.py:149
  319.8 1.5 copy-start.6
  320.6 30.9 %copy-start.3 = (bf16[64,1024]{1,0:T(8,128)(2,1)S(1)}, bf16[64,1024]{1,0:T(8,128)(2,1)}, u32[]{:S(2)}) copy-start(bf16[64,1024]{1,0:T(8,128)(2,1)} %reduce-scatter.4.cloned.1.call-done) | copy-start | bytes 393220
  322.8 56.2 %all-gather.6.cloned.1.call-start = ((), (), s32[]{:S(2)}) async-start(), calls=%async_computation.13 | async-start | bytes 1179648 | tf_op jit(solution)/shard_map/all_gather | solution.py:156
  353.2 63.8 %reduce-scatter.8.cloned.1.call-start = ((), (), s32[]{:S(2)}) async-start(), calls=%async_computation.14 | async-start | bytes 1179648 | tf_op jit(solution)/shard_map/reduce_scatter | solution.py:162
  379.0 4.9 %copy-start.2 = (bf16[512,1024]{1,0:T(8,128)(2,1)S(1)}, bf16[512,1024]{1,0:T(8,128)(2,1)}, u32[]{:S(2)}) copy-start(bf16[512,1024]{1,0:T(8,128)(2,1)} %all-gather.6.cloned.1.call-done) | copy-start | bytes 3145732
  383.9 33.0 %copy-start.1 = (bf16[64,1024]{1,0:T(8,128)(2,1)S(1)}, bf16[64,1024]{1,0:T(8,128)(2,1)}, u32[]{:S(2)}) copy-start(bf16[64,1024]{1,0:T(8,128)(2,1)} %add_convert_fusion.2) | copy-start | bytes 393220
  388.2 56.2 %all-gather.8.cloned.1.call-start = ((), (), s32[]{:S(2)}) async-start(), calls=%async_computation.15 | async-start | bytes 1179648 | tf_op jit(solution)/shard_map/all_gather | solution.py:170
Sparse Core Ops, SparseCore 0:
  263.5 25.0 reduce-scatter.3
  290.3 25.6 all-gather.3
  322.9 28.5 reduce-scatter.5
  353.3 25.6 all-gather.5
  388.4 28.5 reduce-scatter.7
  418.7 25.6 all-gather.7
where the time goes:
time: 479 us; the launch traced here: 470 us
  waiting for transfers between devices  206 us (43%)
  local copies, waits for them, and re-layouts  103 us (22%)
  matrix products  59.2 us (12%)
  starting transfers between devices  40.6 us (8%)
  blocking collectives  25.4 us (5%)
  other arithmetic  21.8 us (5%)
  between operations  14.3 us (3%)
    reduce_scatter x1, waiting for transfers between devices, body(): lax.psum_scatter(jnp.dot(mixed, coarse_out, preferred_element_type=jnp.fl...  28.7 us
    reduce_scatter x1, waiting for transfers between devices, body(): lax.psum_scatter(jnp.dot(hidden, coarse_down, preferred_element_type=jnp....  28.6 us
    all_gather x1, waiting for transfers between devices, body(): lax.all_gather(pooled, 'hid', axis=0, tiled=True)  27.3 us
    all_gather x1, waiting for transfers between devices, body(): lax.all_gather(coarse_done, 'hid', axis=0, tiled=True)  25.9 us
    all_gather x1, waiting for transfers between devices, body(): lax.all_gather(coarse_mid, 'hid', axis=0, tiled=True)  25.8 us
    all_to_all x2, waiting for transfers between devices, deliver(): lax.all_to_all(send_rows, ('ball', 'hid'), split_axis=0, concat_axis=0, t...  25.4 us
    reduce_scatter x1, waiting for transfers between devices, body(): lax.psum_scatter(jnp.dot(children, pool_weight, preferred_element_type=jn...  25.1 us
    scatter x2, local copies, waits for them, and re-layouts, arrange(): send_rows = jnp.zeros((device_count * capacity, states.shape[1]), states....  22.1 us
  transfers between devices with their start and end apart: 11, of which 9 were waited for; matrix products, arithmetic and copies ran while one was open for 17% of the time, Pallas kernels for 0%

commit v1 on v0

v1 whole, which is shorter than its diff:
```python
import functools
import math

import jax
import jax.numpy as jnp
from jax import lax
from jax.experimental import pallas as pl
from jax.experimental.pallas import tpu as pltpu
from jax.sharding import Mesh
from jax.sharding import PartitionSpec as P

F32 = jnp.float32
BF16 = jnp.bfloat16
I32 = jnp.int32

C = 256
FH = 1024
FHEADS = 8
BALL = 256
POOL = 16
CC = 1024
N_DEV = 128
CAP = 16
PTS = 1024
SLOTS = N_DEV * CAP
CROWS = PTS // POOL
N_BALL = 16
N_Z = 4
N_HID = 8
EPS = 1e-06
LOG2E = 1.4426950408889634
ALL = ("ball", "z", "core")
VMEM_LIMIT = 56 * 2**20

NT = (((1,), (1,)), ((), ()))


def params():
    return pltpu.CompilerParams(vmem_limit_bytes=VMEM_LIMIT)


def iota(shape, dim):
    return lax.broadcasted_iota(I32, shape, dim)


def onehot(mask):
    return jnp.where(mask, 1.0, 0.0).astype(BF16)


def mm(a, b):
    return jnp.dot(a, b, preferred_element_type=F32)


def mm_nt(a, b):
    return lax.dot_general(a, b, NT, preferred_element_type=F32)


def rms(values, gain):
    mean_square = jnp.mean(values * values, axis=-1, keepdims=True)
    return (values * lax.rsqrt(mean_square + EPS) * gain).astype(BF16)


def silu(v):
    return 0.5 * v * (1.0 + jnp.tanh(0.5 * v))


def prep_kernel(points, tree, rot, send, place, slots):
    upper = onehot(iota((PTS, PTS), 0) < iota((PTS, PTS), 1))
    device = iota((N_DEV, PTS), 0)
    placed = jnp.zeros((N_DEV, N_DEV), F32)
    for which, ref in ((0, tree), (1, rot)):
        target = ref[...]
        owner = target >> 10
        within = (target & (PTS - 1)) + 1
        match = jnp.where(device == owner, 1.0, 0.0)
        match_16 = match.astype(BF16)
        before = mm(match_16, upper)
        rank = jnp.sum(match * before, axis=0, keepdims=True).astype(I32)
        slots[which : which + 1, :] = owner * CAP + rank
        column = device - 2 * CAP * which
        high = (within >> 5).astype(F32)
        low = (within & 31).astype(F32)
        spread = jnp.where(
            column == rank, high, jnp.where(column == rank + CAP, low, 0.0)
        ).astype(BF16)
        placed = placed + mm_nt(match_16, spread)
    place[...] = placed
    pack(slots[0:1, :], points, send)


def pack(slot_row, source, send):
    for chunk in range(SLOTS // 256):
        pick = onehot(iota((256, PTS), 0) + chunk * 256 == slot_row)
        send[chunk * 256 : (chunk + 1) * 256, :] = mm(pick, source[...]).astype(BF16)


def fine_ball(x_16, gains, qkv, out, gate_up, down):
    x = x_16.astype(F32)
    normed = rms(x, gains[0, 0:1, :])
    q = mm(normed, qkv[0, 0]).astype(BF16)
    k = mm(normed, qkv[0, 1]).astype(BF16)
    v = mm(normed, qkv[0, 2]).astype(BF16)
    width = C // FHEADS
    head_of = iota((BALL, C), 1) // width
    scale = LOG2E / math.sqrt(width)
    mixed = jnp.zeros((BALL, C), F32)
    inverse = jnp.zeros((BALL, C), F32)
    zero = jnp.zeros((BALL, C), BF16)
    for head in range(FHEADS):
        mine = head_of == head
        scores = mm_nt(q, jnp.where(mine, k, zero))
        top = jnp.max(scores, axis=-1, keepdims=True)
        weights = jnp.exp2((scores - top) * scale)
        total = jnp.sum(weights, axis=-1, keepdims=True)
        mixed = mixed + mm(weights.astype(BF16), jnp.where(mine, v, zero))
        inverse = jnp.where(mine, 1.0 / total, inverse)
    mixed = (mixed * inverse).astype(BF16)
    attended = (x + mm(mixed, out[0])).astype(BF16).astype(F32)
    normed = rms(attended, gains[0, 1:2, :])
    hidden = (silu(mm(normed, gate_up[0, 0])) * mm(normed, gate_up[0, 1])).astype(BF16)
    return (attended + mm(hidden, down[0])).astype(BF16)


def fine_kernel(which, rows, place, slots, gains, qkv, out, gate_up, down, send, place_row, states):
    base = 2 * CAP * which
    got = place[...]
    got_t = jnp.transpose(got)[base : base + 2 * CAP].astype(BF16)
    source = onehot(iota((N_DEV, SLOTS), 0) == (iota((N_DEV, SLOTS), 1) >> 4))
    spread = mm(got_t, source)
    row = iota((2 * CAP, SLOTS), 0)
    lane = iota((2 * CAP, SLOTS), 1)
    factor = jnp.where((row & 15) == (lane & 15), jnp.where(row < CAP, 32.0, 1.0), 0.0)
    place_row[0:1, :] = jnp.sum(spread * factor, axis=0, keepdims=True).astype(I32) - 1

    def one_ball(ball, carry):
        start = pl.multiple_of(ball * BALL, BALL)
        pick = onehot(iota((BALL, SLOTS), 0) + ball * BALL == place_row[0:1, :])
        x = mm(pick, rows[...]).astype(BF16)
        states[pl.ds(start, BALL), :] = fine_ball(x, gains, qkv, out, gate_up, down)
        return carry

    lax.fori_loop(0, PTS // BALL, one_ball, 0)

    if which == 0:
        pack(slots[1:2, :], states, send)
        return
    got_16 = got.astype(BF16)
    for chunk in range(SLOTS // 256):
        slot = iota((256, N_DEV), 0) + chunk * 256
        col = iota((256, N_DEV), 1)
        spread = mm(onehot(col == (slot >> 4)), got_16)
        inside = col - base
        hit = ((inside & 15) == (slot & 15)) & (inside >= 0) & (inside < 2 * CAP)
        factor = jnp.where(hit, jnp.where(inside < CAP, 32.0, 1.0), 0.0)
        at = jnp.sum(spread * factor, axis=1, keepdims=True).astype(I32) - 1
        pick = onehot(iota((256, PTS), 1) == at)
        send[chunk * 256 : (chunk + 1) * 256, :] = mm(pick, states[...]).astype(BF16)


def pool_kernel(returned, slots, pool, block_two, coarse, total):
    step = pl.program_id(0)
    slot = slots[1:2, :]
    high = (slot >> 5).astype(F32)
    low = (slot & 31).astype(F32)
    row = iota((8, PTS), 0)
    digits = jnp.where(row == 0, high, jnp.where(row == 1, low, 0.0)).astype(BF16)
    child = iota((128, PTS), 0)
    order = onehot(iota((128, PTS), 1) == POOL * (child & 63) + 2 * step + (child >> 6))
    found = mm_nt(order, digits)
    at = (found[:, 0:1] * 32.0 + found[:, 1:2]).astype(I32)
    pick = onehot(iota((128, SLOTS), 1) == at)
    two = mm(pick, returned[...]).astype(BF16)
    block_two[...] = two
    part = mm(two[:CROWS], pool[0, :C]) + mm(two[CROWS:], pool[0, C:])

    @pl.when(step == 0)
    def _():
        total[...] = part

    @pl.when(step > 0)
    def _():
        total[...] += part

    @pl.when(step == N_HID - 1)
    def _():
        coarse[...] = total[...].astype(BF16)


def attn_kernel(own, other_z, pair, gains, qkv, out, mid, normed_mid, keys, total):
    step = pl.program_id(0)

    @pl.when(step == 0)
    def _():
        gain = gains[0:1, :]
        keys[0:64, :] = rms(own[...].astype(F32), gain)
        keys[64:128, :] = rms(other_z[...].astype(F32), gain)
        keys[128:256, :] = rms(pair[...].astype(F32), gain)
        total[...] = own[...].astype(F32)

    q = mm(keys[0:64, :], qkv[0, 0]).astype(BF16)
    k = mm(keys[...], qkv[0, 1]).astype(BF16)
    v = mm(keys[...], qkv[0, 2]).astype(BF16)
    head_of = iota((BALL, 128), 1) // 64
    scale = LOG2E / math.sqrt(64)
    mixed = jnp.zeros((CROWS, 128), F32)
    inverse = jnp.zeros((CROWS, 128), F32)
    zero = jnp.zeros((BALL, 128), BF16)
    for head in range(2):
        mine = head_of == head
        scores = mm_nt(q, jnp.where(mine, k, zero))
        top = jnp.max(scores, axis=-1, keepdims=True)
        weights = jnp.exp2((scores - top) * scale)
        sums = jnp.sum(weights, axis=-1, keepdims=True)
        mixed = mixed + mm(weights.astype(BF16), jnp.where(mine, v, zero))
        inverse = jnp.where(mine[:CROWS], 1.0 / sums, inverse)
    mixed = (mixed * inverse).astype(BF16)
    total[...] += mm(mixed, out[0])

    @pl.when(step == N_HID - 1)
    def _():
        done = total[...].astype(BF16)
        mid[...] = done
        normed_mid[...] = rms(done.astype(F32), gains[1:2, :])


def mlp_kernel(own, pair, weights, kept, sent, total):
    step = pl.program_id(0)
    rows = jnp.concatenate([own[...], pair[...]], axis=0)
    gate = mm(rows, weights[:, 0, 0, :64, :].reshape(CC, 512))
    up = mm(rows, weights[:, 0, 1, :64, :].reshape(CC, 512))
    hidden = (silu(gate) * up).astype(BF16)
    left = mm(hidden, weights[:, 0, 0, 64:, :].reshape(512, 512))
    right = mm(hidden, weights[:, 0, 1, 64:, :].reshape(512, 512))

    @pl.when(step == 0)
    def _():
        total[:, :512] = left
        total[:, 512:] = right

    @pl.when(step > 0)
    def _():
        total[:, :512] += left
        total[:, 512:] += right

    @pl.when(step == N_Z - 1)
    def _():
        kept[...] = total[:CROWS, :]
        sent[...] = total[CROWS:, :].astype(BF16)


def unpool_kernel(mid, kept, got, block_two, unpool, joined, done, children):
    step = pl.program_id(0)

    @pl.when(step == 0)
    def _():
        done[...] = (mid[...].astype(F32) + kept[...] + got[...].astype(F32)).astype(BF16)

    spread = mm(done[...], unpool[0]).astype(BF16).astype(F32)
    start = pl.multiple_of(step * 128, 128)
    two = block_two[...].astype(F32)
    children[pl.ds(start, CROWS), :] = (two[:CROWS] + spread[:, :C]).astype(BF16)
    children[pl.ds(start + CROWS, CROWS), :] = (two[CROWS:] + spread[:, C:]).astype(BF16)

    @pl.when(step == N_HID - 1)
    def _():
        for chunk in range(4):
            point = iota((256, PTS), 0) + chunk * 256
            child = iota((256, PTS), 1)
            order = onehot(point == POOL * (child & 63) + (child >> 6))
            joined[chunk * 256 : (chunk + 1) * 256, :] = mm(order, children[...]).astype(BF16)


def shape(dims, dtype):
    return jax.ShapeDtypeStruct(dims, dtype)


def whole(dims):
    zeros = (0,) * len(dims)
    return pl.BlockSpec(dims, lambda *_: zeros)


def layer(dims, which):
    index = (which,) + (0,) * (len(dims) - 1)
    return pl.BlockSpec((1,) + dims[1:], lambda *_: index)


def along(dims):
    rest = (0,) * (len(dims) - 1)
    return pl.BlockSpec((1,) + dims[1:], lambda i: (i,) + rest)


def exchange(values):
    return lax.all_to_all(values, ALL, split_axis=0, concat_axis=0, tiled=True)


def other_core(values):
    return lax.ppermute(values, "core", [(0, 1), (1, 0)])


def other_z(values):
    return lax.ppermute(values, "z", [(0, 1), (1, 0), (2, 3), (3, 2)])


def fine(which, rows, place, slots, norm, qkv, out, gate_up, down):
    return pl.pallas_call(
        functools.partial(fine_kernel, which),
        grid=(1,),
        out_shape=shape((SLOTS, C), BF16),
        in_specs=[
            whole((SLOTS, C)),
            whole((N_DEV, N_DEV)),
            whole((2, PTS)),
            layer(norm.shape, which),
            layer(qkv.shape, which),
            layer(out.shape, which),
            layer(gate_up.shape, which),
            layer(down.shape, which),
        ],
        out_specs=whole((SLOTS, C)),
        scratch_shapes=[pltpu.VMEM((8, SLOTS), I32), pltpu.VMEM((PTS, C), BF16)],
        compiler_params=params(),
        cost_estimate=pl.CostEstimate(flops=8 * 10**9, bytes_accessed=4 * 2**20, transcendentals=0),
        name=f"fine_block_{which}",
    )(rows, place, slots, norm, qkv, out, gate_up, down)


def body(
    points,
    tree_slot,
    rotated_slot,
    fine_norm,
    fine_qkv,
    fine_out,
    fine_gate_up,
    fine_down,
    pool_weight,
    coarse_norm,
    coarse_qkv,
    coarse_out,
    coarse_gate_up,
    coarse_down,
    unpool_weight,
):
    hid = ("z", "core")
    pool_out = lax.all_gather(jnp.concatenate([pool_weight, coarse_out], axis=0), hid)
    at_ball = lax.axis_index("ball")
    gate_slice = lax.dynamic_slice_in_dim(coarse_gate_up, at_ball * 64, 64, axis=1)
    down_slice = lax.dynamic_slice_in_dim(coarse_down, at_ball * 32, 32, axis=0)
    mlp_slice = jnp.concatenate(
        [gate_slice, jnp.stack([down_slice[:, :512], down_slice[:, 512:]])], axis=1
    )
    mlp_weights = lax.all_gather(lax.all_gather(mlp_slice, "z"), "ball")
    qkv_all = lax.all_gather(coarse_qkv, hid)
    unpool_all = lax.all_gather(unpool_weight, hid)

    send, place, slots = pl.pallas_call(
        prep_kernel,
        out_shape=(shape((SLOTS, C), BF16), shape((N_DEV, N_DEV), F32), shape((2, PTS), I32)),
        compiler_params=params(),
        name="prep",
    )(points, tree_slot.reshape(1, PTS), rotated_slot.reshape(1, PTS))
    rows = exchange(send)
    place = exchange(place)
    fine_weights = (fine_norm, fine_qkv, fine_out, fine_gate_up, fine_down)
    rows = exchange(fine(0, rows, place, slots, *fine_weights))
    returned = exchange(fine(1, rows, place, slots, *fine_weights))

    block_two, coarse = pl.pallas_call(
        pool_kernel,
        grid=(N_HID,),
        out_shape=(shape((PTS, C), BF16), shape((CROWS, CC), BF16)),
        in_specs=[
            whole((SLOTS, C)),
            whole((2, PTS)),
            pl.BlockSpec((1, 512, CC), lambda i: (i, 0, 0)),
        ],
        out_specs=(pl.BlockSpec((128, C), lambda i: (i, 0)), whole((CROWS, CC))),
        scratch_shapes=[pltpu.VMEM((CROWS, CC), F32)],
        compiler_params=params(),
        name="pool",
    )(returned, slots, pool_out)

    from_z = other_z(coarse)
    from_pair = other_core(jnp.concatenate([coarse, from_z], axis=0))

    mid, normed = pl.pallas_call(
        attn_kernel,
        grid=(N_HID,),
        out_shape=(shape((CROWS, CC), BF16), shape((CROWS, CC), BF16)),
        in_specs=[
            whole((CROWS, CC)),
            whole((CROWS, CC)),
            whole((2 * CROWS, CC)),
            whole((2, CC)),
            along((N_HID, 3, CC, 128)),
            pl.BlockSpec((1, 128, CC), lambda i: (i, 4, 0)),
        ],
        out_specs=(whole((CROWS, CC)), whole((CROWS, CC))),
        scratch_shapes=[pltpu.VMEM((4 * CROWS, CC), BF16), pltpu.VMEM((CROWS, CC), F32)],
        compiler_params=params(),
        name="attn",
    )(coarse, from_z, from_pair, coarse_norm, qkv_all, pool_out)

    kept, sent = pl.pallas_call(
        mlp_kernel,
        grid=(N_Z,),
        out_shape=(shape((CROWS, CC), F32), shape((CROWS, CC), BF16)),
        in_specs=[
            whole((CROWS, CC)),
            whole((CROWS, CC)),
            pl.BlockSpec((N_BALL, 1, 2, 96, 512), lambda i: (0, i, 0, 0, 0)),
        ],
        out_specs=(whole((CROWS, CC)), whole((CROWS, CC))),
        scratch_shapes=[pltpu.VMEM((2 * CROWS, CC), F32)],
        compiler_params=params(),
        name="mlp",
    )(normed, other_core(normed), mlp_weights)

    return pl.pallas_call(
        unpool_kernel,
        grid=(N_HID,),
        out_shape=shape((PTS, C), BF16),
        in_specs=[
            whole((CROWS, CC)),
            whole((CROWS, CC)),
            whole((CROWS, CC)),
            pl.BlockSpec((128, C), lambda i: (i, 0)),
            along((N_HID, CC, 512)),
        ],
        out_specs=whole((PTS, C)),
        scratch_shapes=[pltpu.VMEM((CROWS, CC), BF16), pltpu.VMEM((PTS, C), BF16)],
        compiler_params=params(),
        name="unpool",
    )(mid, kept, other_core(sent), block_two, unpool_all)


def solution(mesh):
    split = Mesh(mesh.devices.reshape(N_BALL, N_Z, 2), ALL)
    hid = ("z", "core")
    placed = (
        P(ALL, None),
        P(ALL),
        P(ALL),
        P(),
        P(),
        P(),
        P(),
        P(),
        P(hid, None),
        P(),
        P(None, None, hid),
        P(hid, None),
        P(None, None, hid),
        P(hid, None),
        P(None, hid),
    )
    return jax.shard_map(
        body, mesh=split, in_specs=placed, out_specs=P(ALL, None), check_vma=False
    )
```

time: 479 us -> 300 us (0.63); the launches traced: 470 us -> 299 us
  waiting for transfers between devices: 206 us -> 85.2 us
  local copies, waits for them, and re-layouts: 103 us -> 2.17 us
  blocking collectives: 25.4 us -> 114 us
  Pallas kernels: 0 us -> 76.3 us
  matrix products: 59.2 us -> 0 us
  starting transfers between devices: 40.6 us -> 4.5 us
  other arithmetic: 21.8 us -> 3.58 us
    reduce_scatter x3 -> x0, waiting for transfers between devices: 82.4 us -> none  [the longest x1 28.7 us: body(): lax.psum_scatter(jnp.dot(mixed, coarse_out, preferred_element_type=jnp.fl...]
    pallas_call x0 -> x7, Pallas kernels: none -> 76.3 us  [the longest x2 33.7 us: fine(): pl.pallas_call(functools.partial(fine_kernel, which), grid=(1,), out_shap...]
    all_to_all x2 -> x4, blocking collectives: 25.4 us -> 99.2 us  [exchange(): return lax.all_to_all(values, ALL, split_axis=0, concat_axis=0, tiled=True)]
    scatter x9 -> x0, local copies, waits for them, and re-layouts: 58.8 us -> none  [the longest x2 22.1 us: arrange(): send_rows = jnp.zeros((device_count * capacity, states.shape[1]), states....]
    all_to_all x5 -> x0, waiting for transfers between devices: 44.6 us -> none  [the longest x2 25.4 us: deliver(): lax.all_to_all(send_rows, ('ball', 'hid'), split_axis=0, concat_axis=0, t...]
    dot_general x18 -> x0, matrix products: 44.3 us -> none  [the longest x3 8.78 us: attend(): jnp.einsum('bhqk,bkhd->bqhd', weights, split_heads[2], preferred_element_...]
    all_to_all x5 -> x0, starting transfers between devices: 40.2 us -> none  [the longest x2 19.6 us: deliver(): lax.all_to_all(send_rows, ('ball', 'hid'), split_axis=0, concat_axis=0, t...]
    gather x5 -> x0, local copies, waits for them, and re-layouts: 25.6 us -> none  [the longest x2 9.05 us: arrange(): within[ordering]]
  transfers between devices with their start and end apart: 11 -> 8, of which waited for: 9 -> 5; matrix products, arithmetic and copies ran while one was open for 17% -> 1% of each run, Pallas kernels for 0% -> 23%
where the time goes in v1:
time: 300 us; the launch traced here: 299 us
  blocking collectives  114 us (38%)
  waiting for transfers between devices  85.2 us (28%)
  Pallas kernels  76.3 us (25%)
  between operations  13.2 us (4%)
  starting transfers between devices  4.5 us (2%)
  other arithmetic  3.58 us (1%)
    all_to_all x4, blocking collectives, exchange(): return lax.all_to_all(values, ALL, split_axis=0, concat_axis=0, tiled=True)  99.2 us
    all_gather x1, waiting for transfers between devices, body(): unpool_all = lax.all_gather(unpool_weight, hid)  43.7 us
    all_gather x1, waiting for transfers between devices, body(): mlp_weights = lax.all_gather(lax.all_gather(mlp_slice, 'z'), 'ball')  33.9 us
    pallas_call x2, Pallas kernels, fine(): pl.pallas_call(functools.partial(fine_kernel, which), grid=(1,), out_shap...  33.7 us
    all_gather x1, blocking collectives, body(): mlp_weights = lax.all_gather(lax.all_gather(mlp_slice, 'z'), 'ball')  14.8 us
    pallas_call x1, Pallas kernels, body(): pl.pallas_call(pool_kernel, grid=(N_HID,), out_shape=(shape((PTS, C), BF1...  12 us
    pallas_call x1, Pallas kernels, body(): pl.pallas_call(attn_kernel, grid=(N_HID,), out_shape=(shape((CROWS, CC),...  10.6 us
    pallas_call x1, Pallas kernels, body(): pl.pallas_call(unpool_kernel, grid=(N_HID,), out_shape=shape((PTS, C), BF...  8.51 us
  transfers between devices with their start and end apart: 8, of which 5 were waited for; matrix products, arithmetic and copies ran while one was open for 1% of the time, Pallas kernels for 23%

profile of v1, /device:TPU:1, one launch (start us, length us, event | category | flops | bytes accessed | tf_op | source)
XLA Modules:
  0.0 299.0 jit_solution(13363550357429311044)
XLA Ops:
  6.5 2.6 pad_maximum_fusion
  9.2 0.7 all-gather.12.cloned.1.call-update
  10.0 0.8 dynamic-slice_bitcast_fusion.1
  10.8 14.8 %all-gather.2 = bf16[8,96,512]{2,1,0:T(8,128)(2,1)} all-gather(bf16[2,96,512]{2,1,0:T(8,128)(2,1)S(1)} %maximum_maximum_fusion), channel_id=4, replica_groups=mesh['ball'=16,'z'=4,'core'=2] {'z'}, dimensions={0}, use_global_device_ids=true | all-gather | bytes 983040 | tf_op jit(solution)/shard_map/all_gather | solution.py:352
  26.2 4.2 %prep.1 = (bf16[2048,256]{1,0:T(8,128)(2,1)}, f32[128,128]{1,0:T(8,128)}, s32[2,1024]{1,0:T(2,128)}) custom-call(bf16[1024,256]{1,0:T(8,128)(2,1)} %points.1, s32[1,1024]{1,0:T(1,128)} %bitcast.36, s32[1,1024]{1,0:T(1,128)} %bitcast.37), custom_call_target="tpu_custom_call" | custom-call | tf_op jit(solution)/shard_map/prep/pallas_call | solution.py:356
  30.4 22.2 %all_to_all.44 = f32[128,1,128]{2,1,0:T(1,128)} all-to-all(f32[128,1,128]{2,1,0:T(1,128)} %bitcast.35), channel_id=1, replica_groups=mesh['ball'=16,'z'=4,'core'=2] {'ball','z','core'}, dimensions={0} | all-to-all | bytes 131072 | tf_op jit(solution)/shard_map/all_to_all | solution.py:293
  52.6 25.0 %all_to_all.45 = bf16[128,16,256]{2,1,0:T(8,128)(2,1)} all-to-all(bf16[128,16,256]{2,1,0:T(8,128)(2,1)} %bitcast.28), channel_id=1, replica_groups=mesh['ball'=16,'z'=4,'core'=2] {'ball','z','core'}, dimensions={0} | all-to-all | bytes 2097152 | tf_op jit(solution)/shard_map/all_to_all | solution.py:293
  77.6 16.5 %fine_block_0.1 = bf16[2048,256]{1,0:T(8,128)(2,1)} custom-call(bf16[2048,256]{1,0:T(8,128)(2,1)} %bitcast.29, f32[128,128]{1,0:T(8,128)} %bitcast.33, s32[2,1024]{1,0:T(2,128)} %get-tuple-element.16.slots, f32[2,2,256]{2,1,0:T(2,128)} %gains.4, bf16[2,3,256,256]{3,2,1,0:T(8,128)(2,1)} %qkv.3, bf16[2,256,256]{2,1,0:T(8,128)(2,1)} %out.3, ...), custom_call_target="tpu_custom_call" | custom-call | flops 8000000000 | bytes 4194304 | tf_op jit(solution)/shard_map/fine_block_0/pallas_call | solution.py:305
  94.0 24.9 %all_to_all.46 = bf16[128,16,256]{2,1,0:T(8,128)(2,1)} all-to-all(bf16[128,16,256]{2,1,0:T(8,128)(2,1)} %bitcast.32), channel_id=1, replica_groups=mesh['ball'=16,'z'=4,'core'=2] {'ball','z','core'}, dimensions={0} | all-to-all | bytes 2097152 | tf_op jit(solution)/shard_map/all_to_all | solution.py:293
  119.0 17.3 %fine_block_1.1 = bf16[2048,256]{1,0:T(8,128)(2,1)} custom-call(bf16[2048,256]{1,0:T(8,128)(2,1)} %bitcast.30, f32[128,128]{1,0:T(8,128)} %bitcast.34, s32[2,1024]{1,0:T(2,128)} %get-tuple-element.16.slots, f32[2,2,256]{2,1,0:T(2,128)} %gains.4, bf16[2,3,256,256]{3,2,1,0:T(8,128)(2,1)} %qkv.3, bf16[2,256,256]{2,1,0:T(8,128)(2,1)} %out.3, ...), custom_call_target="tpu_custom_call" | custom-call | flops 8000000000 | bytes 4194304 | tf_op jit(solution)/shard_map/fine_block_1/pallas_call | solution.py:305
  136.2 27.1 %all_to_all.47 = bf16[128,16,256]{2,1,0:T(8,128)(2,1)} all-to-all(bf16[128,16,256]{2,1,0:T(8,128)(2,1)} %bitcast.31), channel_id=1, replica_groups=mesh['ball'=16,'z'=4,'core'=2] {'ball','z','core'}, dimensions={0} | all-to-all | bytes 2097152 | tf_op jit(solution)/shard_map/all_to_all | solution.py:293
  163.3 12.0 %pool.1 = (bf16[1024,256]{1,0:T(8,128)(2,1)}, bf16[64,1024]{1,0:T(8,128)(2,1)}) custom-call(bf16[2048,256]{1,0:T(8,128)(2,1)} %bitcast.26, s32[2,1024]{1,0:T(2,128)} %get-tuple-element.16.slots, bf16[8,640,1024]{2,1,0:T(8,128)(2,1)} %bitcast.21), custom_call_target="tpu_custom_call" | custom-call | tf_op jit(solution)/shard_map/pool/pallas_call | solution.py:368
  175.3 4.0 %collective-permute-done.other_z = bf16[64,1024]{1,0:T(8,128)(2,1)S(1)} collective-permute-done((bf16[64,1024]{1,0:T(8,128)(2,1)}, bf16[64,1024]{1,0:T(8,128)(2,1)S(1)}, u32[]{:S(2)}, u32[]{:S(2)}) %collective-permute-start) | collective-permute-done | bytes 131104 | tf_op jit(solution)/shard_map/ppermute | solution.py:301
  179.4 1.0 pad_maximum_fusion.1
  180.3 3.3 %collective-permute-start.1 = (bf16[128,1024]{1,0:T(8,128)(2,1)S(1)}, bf16[128,1024]{1,0:T(8,128)(2,1)S(1)}, u32[]{:S(2)}, u32[]{:S(2)}) collective-permute-start(bf16[128,1024]{1,0:T(8,128)(2,1)S(1)} %pad_maximum_fusion.1), channel_id=1, source_target_pairs={{0,1},{1,0},{2,3},{3,2},{4,5},{5,4},{6,7},{7,6},{8,9},{9,8},{10,11... | collective-permute-start | bytes 786440 | tf_op jit(solution)/shard_map/ppermute | solution.py:297
  183.7 1.2 collective-permute-done.1.pair
  184.8 0.7 copy-done.2
  185.5 10.6 %attn.1 = (bf16[64,1024]{1,0:T(8,128)(2,1)}, bf16[64,1024]{1,0:T(8,128)(2,1)}) custom-call(bf16[64,1024]{1,0:T(8,128)(2,1)} %get-tuple-element.17.own, bf16[64,1024]{1,0:T(8,128)(2,1)} %copy-done.1, bf16[128,1024]{1,0:T(8,128)(2,1)} %copy-done.2, f32[2,1024]{1,0:T(2,128)} %gains.5, bf16[8,3,1024,128]{3,2,1,0:T(8,128)(2,1)} %bitcast.25, ...), custom_call_target="tpu_custom_call" | custom-call | tf_op jit(solution)/shard_map/attn/pallas_call | solution.py:386
  196.5 1.2 collective-permute-done.2.pair
  197.7 33.9 %all-gather.14.cloned.1.call-done = bf16[64,2,96,512]{3,2,1,0:T(8,128)(2,1)} async-done(((bf16[4,2,96,512]{3,2,1,0:T(8,128)(2,1)}), bf16[64,2,96,512]{3,2,1,0:T(8,128)(2,1)}) %all-gather.14.cloned.1.call-update) | async-done | bytes 12582928 | tf_op jit(solution)/shard_map/all_gather | solution.py:352
  231.6 7.4 %mlp.1 = (f32[64,1024]{1,0:T(8,128)}, bf16[64,1024]{1,0:T(8,128)(2,1)}) custom-call(bf16[64,1024]{1,0:T(8,128)(2,1)} %get-tuple-element.19.own, bf16[64,1024]{1,0:T(8,128)(2,1)} %copy-done.4, bf16[16,4,2,96,512]{4,3,2,1,0:T(8,128)(2,1)} %bitcast.23), custom_call_target="tpu_custom_call" | custom-call | tf_op jit(solution)/shard_map/mlp/pallas_call | solution.py:404
  239.0 0.7 collective-permute-start.3
  239.6 43.7 %all-gather.16.cloned.1.call-done = bf16[8192,512]{1,0:T(8,128)(2,1)} async-done(((bf16[1024,512]{1,0:T(8,128)(2,1)}), bf16[8192,512]{1,0:T(8,128)(2,1)}) %all-gather.16.cloned.1.call-update) | async-done | bytes 8388624 | tf_op jit(solution)/shard_map/all_gather | solution.py:354
  284.0 8.5 %unpool.1 = bf16[1024,256]{1,0:T(8,128)(2,1)} custom-call(bf16[64,1024]{1,0:T(8,128)(2,1)} %get-tuple-element.18.mid, f32[64,1024]{1,0:T(8,128)} %get-tuple-element.20.kept, bf16[64,1024]{1,0:T(8,128)(2,1)} %copy-done.3, bf16[1024,256]{1,0:T(8,128)(2,1)} %get-tuple-element.22.block_two, bf16[8,1024,512]{2,1,0:T(8,128)(2,1)} %bitcast.24), custom_call_target="tpu_custom_call" | custom-call | tf_op jit(solution)/shard_map/unpool/pallas_call | solution.py:419
  (23 shorter events, 1.7 us)
Async XLA Ops:
  6.5 4.2 %copy-start = (bf16[2,1024,512]{2,1,0:T(8,128)(2,1)S(1)}, bf16[2,1024,512]{2,1,0:T(8,128)(2,1)}, u32[]{:S(2)}) copy-start(bf16[2,1024,512]{2,1,0:T(8,128)(2,1)} %param.27) | copy-start | bytes 6291460
  6.5 156.8 %all-gather.10.cloned.1.call-start = ((), (), s32[]{:S(2)}) async-start(), calls=%async_computation.4 | async-start | bytes 11796480 | tf_op jit(solution)/shard_map/all_gather | solution.py:345
  9.2 174.5 %all-gather.12.cloned.1.call-start = ((), (), s32[]{:S(2)}) async-start(), calls=%async_computation.5 | async-start | bytes 7077888 | tf_op jit(solution)/shard_map/all_gather | solution.py:353
  9.9 221.7 %all-gather.14.cloned.1.call-start = ((), (), s32[]{:S(2)}) async-start(), calls=%async_computation.6 | async-start | bytes 13369344 | tf_op jit(solution)/shard_map/all_gather | solution.py:352
  25.6 257.7 %all-gather.16.cloned.1.call-start = ((), (), s32[]{:S(2)}) async-start(), calls=%async_computation.7 | async-start | bytes 9437184 | tf_op jit(solution)/shard_map/all_gather | solution.py:354
  175.3 4.0 %collective-permute-start = (bf16[64,1024]{1,0:T(8,128)(2,1)}, bf16[64,1024]{1,0:T(8,128)(2,1)S(1)}, u32[]{:S(2)}, u32[]{:S(2)}) collective-permute-start(bf16[64,1024]{1,0:T(8,128)(2,1)} %get-tuple-element.17.own), channel_id=1, source_target_pairs={{0,2},{2,0},{4,6},{6,4},{1,3},{3,1},{5,7},{7,5},{8,10},{10,8},{12,... | collective-permute-start | bytes 393224 | tf_op jit(solution)/shard_map/ppermute | solution.py:301
  179.4 5.5 %copy-start.1 = (bf16[64,1024]{1,0:T(8,128)(2,1)}, bf16[64,1024]{1,0:T(8,128)(2,1)S(1)}, u32[]{:S(2)}) copy-start(bf16[64,1024]{1,0:T(8,128)(2,1)S(1)} %collective-permute-done.other_z) | copy-start | bytes 393220
  180.3 4.5 %collective-permute-start.1 = (bf16[128,1024]{1,0:T(8,128)(2,1)S(1)}, bf16[128,1024]{1,0:T(8,128)(2,1)S(1)}, u32[]{:S(2)}, u32[]{:S(2)}) collective-permute-start(bf16[128,1024]{1,0:T(8,128)(2,1)S(1)} %pad_maximum_fusion.1), channel_id=1, source_target_pairs={{0,1},{1,0},{2,3},{3,2},{4,5},{5,4},{6,7},{7,6},{8,9},{9,8},{10,11... | collective-permute-start | bytes 786440 | tf_op jit(solution)/shard_map/ppermute | solution.py:297
  184.8 0.7 copy-start.2
  196.1 1.6 collective-permute-start.2
  197.7 33.9 %copy-start.4 = (bf16[64,1024]{1,0:T(8,128)(2,1)}, bf16[64,1024]{1,0:T(8,128)(2,1)S(1)}, u32[]{:S(2)}) copy-start(bf16[64,1024]{1,0:T(8,128)(2,1)S(1)} %collective-permute-done.2.pair) | copy-start | bytes 393220
  239.0 44.3 %collective-permute-start.3 = (bf16[64,1024]{1,0:T(8,128)(2,1)}, bf16[64,1024]{1,0:T(8,128)(2,1)S(1)}, u32[]{:S(2)}, u32[]{:S(2)}) collective-permute-start(bf16[64,1024]{1,0:T(8,128)(2,1)} %get-tuple-element.21), channel_id=1, source_target_pairs={{0,1},{1,0},{2,3},{3,2},{4,5},{5,4},{6,7},{7,6},{8,9},{9,8},{10,11... | collective-permute-start | bytes 393224 | tf_op jit(solution)/shard_map/ppermute | solution.py:297
  283.3 0.7 copy-start.3
Sparse Core Ops, SparseCore 0:
  9.3 74.3 all-gather.9
  85.3 52.4 all-gather.11
  140.1 91.5 all-gather.13
  233.2 50.0 all-gather.15

commit v2 on v1

v2 whole, which is shorter than its diff:
```python
import functools
import math

import jax
import jax.numpy as jnp
from jax import lax
from jax.experimental import pallas as pl
from jax.experimental.pallas import tpu as pltpu
from jax.sharding import Mesh
from jax.sharding import PartitionSpec as P

F32 = jnp.float32
BF16 = jnp.bfloat16
I32 = jnp.int32

C = 256
FH = 1024
FHEADS = 8
BALL = 256
POOL = 16
CC = 1024
N_DEV = 128
CAP = 16
PTS = 1024
SLOTS = N_DEV * CAP
CROWS = PTS // POOL
N_BALL = 16
N_Z = 4
N_HID = 8
EPS = 1e-06
LOG2E = 1.4426950408889634
ALL = ("ball", "z", "core")
VMEM_LIMIT = 56 * 2**20

NT = (((1,), (1,)), ((), ()))


def params():
    return pltpu.CompilerParams(vmem_limit_bytes=VMEM_LIMIT)


def iota(shape, dim):
    return lax.broadcasted_iota(I32, shape, dim)


def onehot(mask):
    return jnp.where(mask, 1.0, 0.0).astype(BF16)


def mm(a, b):
    return jnp.dot(a, b, preferred_element_type=F32)


def mm_nt(a, b):
    return lax.dot_general(a, b, NT, preferred_element_type=F32)


def rms(values, gain):
    mean_square = jnp.mean(values * values, axis=-1, keepdims=True)
    return (values * lax.rsqrt(mean_square + EPS) * gain).astype(BF16)


def silu(v):
    return 0.5 * v * (1.0 + jnp.tanh(0.5 * v))


def slice_kernel(at_ball, gate_up, down, pool, unpool, qkv, out, piece):
    piece[0:64, :] = gate_up[0]
    piece[64:128, :] = gate_up[1]
    piece[128:160, :] = down[:, :512]
    piece[160:192, :] = down[:, 512:]
    piece[192:224, :] = pool[:, :512]
    piece[224:256, :] = pool[:, 512:]
    piece[256:320, :] = unpool[...]
    for part in range(4):
        rows = slice(16 * part, 16 * part + 16)
        lanes = slice(128 * part, 128 * part + 128)
        for which in range(3):
            piece[320 + 16 * which : 336 + 16 * which, lanes] = qkv[which, rows, :]
        piece[368:384, lanes] = out[rows, :]


def prep_kernel(points, tree, rot, send, slots):
    upper = onehot(iota((PTS, PTS), 0) < iota((PTS, PTS), 1))
    device = iota((N_DEV, PTS), 0)
    digits = []
    for which, ref in ((0, tree), (1, rot)):
        target = ref[...]
        owner = target >> 10
        within = (target & (PTS - 1)) + 1
        match = jnp.where(device == owner, 1.0, 0.0)
        before = mm(match.astype(BF16), upper)
        rank = jnp.sum(match * before, axis=0, keepdims=True).astype(I32)
        slots[which : which + 1, :] = owner * CAP + rank
        row = device - 2 * which
        high = (within >> 5).astype(F32)
        low = (within & 31).astype(F32)
        digits.append(jnp.where(row == 0, high, jnp.where(row == 1, low, 0.0)).astype(BF16))
    for chunk in range(SLOTS // 256):
        rows = slice(chunk * 256, (chunk + 1) * 256)
        slot = iota((256, PTS), 0) + chunk * 256
        tree_pick = onehot(slot == slots[0:1, :])
        rot_pick = onehot(slot == slots[1:2, :])
        send[rows, :C] = mm(tree_pick, points[...]).astype(BF16)
        send[rows, C:] = (mm_nt(tree_pick, digits[0]) + mm_nt(rot_pick, digits[1])).astype(BF16)


def pack(slot_row, source, send):
    for chunk in range(SLOTS // 256):
        pick = onehot(iota((256, PTS), 0) + chunk * 256 == slot_row)
        send[chunk * 256 : (chunk + 1) * 256, :] = mm(pick, source[...]).astype(BF16)


def fine_ball(x_16, gains, qkv, out, gate_up, down):
    x = x_16.astype(F32)
    normed = rms(x, gains[0, 0:1, :])
    q = mm(normed, qkv[0, 0]).astype(BF16)
    k = mm(normed, qkv[0, 1]).astype(BF16)
    v = mm(normed, qkv[0, 2]).astype(BF16)
    width = C // FHEADS
    head_of = iota((BALL, C), 1) // width
    scale = LOG2E / math.sqrt(width)
    mixed = jnp.zeros((BALL, C), F32)
    inverse = jnp.zeros((BALL, C), F32)
    zero = jnp.zeros((BALL, C), BF16)
    for head in range(FHEADS):
        mine = head_of == head
        scores = mm_nt(q, jnp.where(mine, k, zero))
        top = jnp.max(scores, axis=-1, keepdims=True)
        weights = jnp.exp2((scores - top) * scale)
        total = jnp.sum(weights, axis=-1, keepdims=True)
        mixed = mixed + mm(weights.astype(BF16), jnp.where(mine, v, zero))
        inverse = jnp.where(mine, 1.0 / total, inverse)
    mixed = (mixed * inverse).astype(BF16)
    attended = (x + mm(mixed, out[0])).astype(BF16).astype(F32)
    normed = rms(attended, gains[0, 1:2, :])
    hidden = (silu(mm(normed, gate_up[0, 0])) * mm(normed, gate_up[0, 1])).astype(BF16)
    return (attended + mm(hidden, down[0])).astype(BF16)


def fine_kernel(which, rows, place, slots, gains, qkv, out, gate_up, down, send, place_row, states):
    row = iota((8, N_DEV), 0)
    lane = iota((8, N_DEV), 1)
    digit = jnp.where(row == 0, jnp.where(lane == 2 * which, 32.0, 0.0), 0.0)
    digit = jnp.where((row == 0) & (lane == 2 * which + 1), 1.0, digit).astype(BF16)
    place_row[...] = mm_nt(digit, place[...]).astype(I32) - 1

    def one_ball(ball, carry):
        start = pl.multiple_of(ball * BALL, BALL)
        pick = onehot(iota((BALL, SLOTS), 0) + ball * BALL == place_row[0:1, :])
        x = mm(pick, rows[...]).astype(BF16)
        states[pl.ds(start, BALL), :] = fine_ball(x, gains, qkv, out, gate_up, down)
        return carry

    lax.fori_loop(0, PTS // BALL, one_ball, 0)

    if which == 0:
        pack(slots[1:2, :], states, send)
        return
    for chunk in range(SLOTS // 256):
        digits = place[chunk * 256 : (chunk + 1) * 256, :].astype(F32)
        at = (digits[:, 2:3] * 32.0 + digits[:, 3:4]).astype(I32) - 1
        pick = onehot(iota((256, PTS), 1) == at)
        send[chunk * 256 : (chunk + 1) * 256, :] = mm(pick, states[...]).astype(BF16)


def pool_kernel(returned, slots, pool, block_two, coarse, total):
    step = pl.program_id(0)
    slot = slots[1:2, :]
    high = (slot >> 5).astype(F32)
    low = (slot & 31).astype(F32)
    row = iota((8, PTS), 0)
    digits = jnp.where(row == 0, high, jnp.where(row == 1, low, 0.0)).astype(BF16)
    child = iota((128, PTS), 0)
    order = onehot(iota((128, PTS), 1) == POOL * (child & 63) + 2 * step + (child >> 6))
    found = mm_nt(order, digits)
    at = (found[:, 0:1] * 32.0 + found[:, 1:2]).astype(I32)
    pick = onehot(iota((128, SLOTS), 1) == at)
    two = mm(pick, returned[...]).astype(BF16)
    block_two[...] = two

    @pl.when(step == 0)
    def _():
        total[...] = jnp.zeros_like(total)

    for half in range(2):
        rows = slice(32 * half, 32 * half + 32)
        lanes = slice(512 * half, 512 * half + 512)
        weight = pool[:, 0, rows, :].reshape(512, 512)
        total[:, lanes] += mm(two[:CROWS], weight[:C]) + mm(two[CROWS:], weight[C:])

    @pl.when(step == N_HID - 1)
    def _():
        coarse[...] = total[...].astype(BF16)


def coarse_kernel(
    own, from_z, pair, gains, heads, gate, up, down, unpool, block_two, joined, keys, total, normed, out, children
):
    step = pl.program_id(0)

    @pl.when(step == 0)
    def _():
        gain = gains[0:1, :]
        keys[0:64, :] = rms(own[...].astype(F32), gain)
        keys[64:128, :] = rms(from_z[...].astype(F32), gain)
        keys[128:256, :] = rms(pair[...].astype(F32), gain)
        total[...] = own[...].astype(F32)

    @pl.when(step < N_HID)
    def _():
        def weight(which):
            rows = slice(16 * which, 16 * which + 16)
            return jnp.stack(
                [heads[:, 0, rows, 128 * part : 128 * part + 128] for part in range(4)], axis=1
            ).reshape(CC, 128)

        for ball in range(N_BALL):
            lanes = slice(128 * (ball % 8), 128 * (ball % 8) + 128)
            for part in range(4):
                top = 64 * (ball // 8) + 16 * part
                out[top : top + 16, lanes] = heads[ball, 0, 48:64, 128 * part : 128 * part + 128]

        q = mm(keys[0:64, :], weight(0)).astype(BF16)
        k = mm(keys[...], weight(1)).astype(BF16)
        v = mm(keys[...], weight(2)).astype(BF16)
        head_of = iota((BALL, 128), 1) // 64
        scale = LOG2E / math.sqrt(64)
        mixed = jnp.zeros((CROWS, 128), F32)
        inverse = jnp.zeros((CROWS, 128), F32)
        zero = jnp.zeros((BALL, 128), BF16)
        for head in range(2):
            mine = head_of == head
            scores = mm_nt(q, jnp.where(mine, k, zero))
            top = jnp.max(scores, axis=-1, keepdims=True)
            weights = jnp.exp2((scores - top) * scale)
            sums = jnp.sum(weights, axis=-1, keepdims=True)
            mixed = mixed + mm(weights.astype(BF16), jnp.where(mine, v, zero))
            inverse = jnp.where(mine[:CROWS], 1.0 / sums, inverse)
        total[...] += mm((mixed * inverse).astype(BF16), out[...])

    @pl.when(step == N_HID)
    def _():
        mid = total[...].astype(BF16).astype(F32)
        total[...] = mid
        normed[...] = rms(mid, gains[1:2, :])

    @pl.when((step >= N_HID) & (step < 2 * N_HID))
    def _():
        rows = normed[...]
        hidden = silu(mm(rows, gate[...].reshape(CC, 512))) * mm(rows, up[...].reshape(CC, 512))
        hidden = hidden.astype(BF16)
        total[:, :512] += mm(hidden, down[:, 0, :32, :].reshape(512, 512))
        total[:, 512:] += mm(hidden, down[:, 0, 32:, :].reshape(512, 512))

    @pl.when(step == 2 * N_HID)
    def _():
        normed[...] = total[...].astype(BF16)

    @pl.when(step >= 2 * N_HID)
    def _():
        spread = mm(normed[...], unpool[...].reshape(CC, 512)).astype(BF16).astype(F32)
        start = pl.multiple_of((step - 2 * N_HID) * 128, 128)
        two = block_two[...].astype(F32)
        children[pl.ds(start, CROWS), :] = (two[:CROWS] + spread[:, :C]).astype(BF16)
        children[pl.ds(start + CROWS, CROWS), :] = (two[CROWS:] + spread[:, C:]).astype(BF16)

    @pl.when(step == 3 * N_HID - 1)
    def _():
        for chunk in range(4):
            point = iota((256, PTS), 0) + chunk * 256
            child = iota((256, PTS), 1)
            order = onehot(point == POOL * (child & 63) + (child >> 6))
            joined[chunk * 256 : (chunk + 1) * 256, :] = mm(order, children[...]).astype(BF16)


def shape(dims, dtype):
    return jax.ShapeDtypeStruct(dims, dtype)


def whole(dims):
    zeros = (0,) * len(dims)
    return pl.BlockSpec(dims, lambda *_: zeros)


def layer(dims, which):
    index = (which,) + (0,) * (len(dims) - 1)
    return pl.BlockSpec((1,) + dims[1:], lambda *_: index)


def unit(which, first):
    return pl.BlockSpec(
        (N_BALL, 1, 64, 512), lambda i: (0, jnp.clip(i - first, 0, N_HID - 1), which, 0)
    )


def exchange(values):
    return lax.all_to_all(values, ALL, split_axis=0, concat_axis=0, tiled=True)


def other_core(values):
    return lax.ppermute(values, "core", [(0, 1), (1, 0)])


def other_z(values):
    return lax.ppermute(values, "z", [(0, 1), (1, 0), (2, 3), (3, 2)])


def fine(which, rows, place, slots, norm, qkv, out, gate_up, down):
    return pl.pallas_call(
        functools.partial(fine_kernel, which),
        grid=(1,),
        out_shape=shape((SLOTS, C), BF16),
        in_specs=[
            whole((SLOTS, C)),
            pl.BlockSpec((SLOTS, N_DEV), lambda i: (0, 2)),
            whole((2, PTS)),
            layer(norm.shape, which),
            layer(qkv.shape, which),
            layer(out.shape, which),
            layer(gate_up.shape, which),
            layer(down.shape, which),
        ],
        out_specs=whole((SLOTS, C)),
        scratch_shapes=[pltpu.VMEM((8, SLOTS), I32), pltpu.VMEM((PTS, C), BF16)],
        compiler_params=params(),
        cost_estimate=pl.CostEstimate(flops=8 * 10**9, bytes_accessed=4 * 2**20, transcendentals=0),
        name=f"fine_block_{which}",
    )(rows, place, slots, norm, qkv, out, gate_up, down)


def body(
    points,
    tree_slot,
    rotated_slot,
    fine_norm,
    fine_qkv,
    fine_out,
    fine_gate_up,
    fine_down,
    pool_weight,
    coarse_norm,
    coarse_qkv,
    coarse_out,
    coarse_gate_up,
    coarse_down,
    unpool_weight,
):
    piece = pl.pallas_call(
        slice_kernel,
        grid_spec=pltpu.PrefetchScalarGridSpec(
            num_scalar_prefetch=1,
            grid=(1,),
            in_specs=[
                pl.BlockSpec((2, 64, 512), lambda i, at: (0, at[0], 0)),
                pl.BlockSpec((32, CC), lambda i, at: (at[0], 0)),
                pl.BlockSpec((32, CC), lambda i, at: (at[0], 0)),
                pl.BlockSpec((64, 512), lambda i, at: (at[0], 0)),
                pl.BlockSpec((3, 64, 128), lambda i, at: (0, at[0], 0)),
                pl.BlockSpec((64, 128), lambda i, at: (at[0] // 8, at[0] % 8)),
            ],
            out_specs=pl.BlockSpec((384, 512), lambda i, at: (0, 0)),
        ),
        out_shape=shape((384, 512), BF16),
        compiler_params=params(),
        name="cut",
    )(
        lax.axis_index("ball").reshape(1),
        coarse_gate_up,
        coarse_down,
        pool_weight,
        unpool_weight,
        coarse_qkv,
        coarse_out,
    )
    weights = lax.all_gather(piece, ALL).reshape(N_BALL, N_HID, 384, 512)

    send, slots = pl.pallas_call(
        prep_kernel,
        out_shape=(shape((SLOTS, C + N_DEV), BF16), shape((2, PTS), I32)),
        compiler_params=params(),
        name="prep",
    )(points, tree_slot.reshape(1, PTS), rotated_slot.reshape(1, PTS))
    first = exchange(send)
    fine_weights = (fine_norm, fine_qkv, fine_out, fine_gate_up, fine_down)
    rows = exchange(fine(0, first, first, slots, *fine_weights))
    returned = exchange(fine(1, rows, first, slots, *fine_weights))

    block_two, coarse = pl.pallas_call(
        pool_kernel,
        grid=(N_HID,),
        out_shape=(shape((PTS, C), BF16), shape((CROWS, CC), BF16)),
        in_specs=[whole((SLOTS, C)), whole((2, PTS)), unit(3, 0)],
        out_specs=(pl.BlockSpec((128, C), lambda i: (i, 0)), whole((CROWS, CC))),
        scratch_shapes=[pltpu.VMEM((CROWS, CC), F32)],
        compiler_params=params(),
        name="pool",
    )(returned, slots, weights)

    from_z = other_z(coarse)
    from_pair = other_core(jnp.concatenate([coarse, from_z], axis=0))

    return pl.pallas_call(
        coarse_kernel,
        grid=(3 * N_HID,),
        out_shape=shape((PTS, C), BF16),
        in_specs=[
            whole((CROWS, CC)),
            whole((CROWS, CC)),
            whole((2 * CROWS, CC)),
            whole((2, CC)),
            unit(5, 0),
            unit(0, N_HID),
            unit(1, N_HID),
            unit(2, N_HID),
            unit(4, 2 * N_HID),
            pl.BlockSpec((128, C), lambda i: (jnp.clip(i - 2 * N_HID, 0, N_HID - 1), 0)),
        ],
        out_specs=whole((PTS, C)),
        scratch_shapes=[
            pltpu.VMEM((4 * CROWS, CC), BF16),
            pltpu.VMEM((CROWS, CC), F32),
            pltpu.VMEM((CROWS, CC), BF16),
            pltpu.VMEM((128, CC), BF16),
            pltpu.VMEM((PTS, C), BF16),
        ],
        compiler_params=params(),
        name="coarse",
    )(coarse, from_z, from_pair, coarse_norm, *[weights] * 5, block_two)


def solution(mesh):
    split = Mesh(mesh.devices.reshape(N_BALL, N_Z, 2), ALL)
    hid = ("z", "core")
    placed = (
        P(ALL, None),
        P(ALL),
        P(ALL),
        P(),
        P(),
        P(),
        P(),
        P(),
        P(hid, None),
        P(),
        P(None, None, hid),
        P(hid, None),
        P(None, None, hid),
        P(hid, None),
        P(None, hid),
    )
    return jax.shard_map(
        body, mesh=split, in_specs=placed, out_specs=P(ALL, None), check_vma=False
    )
```

time: 300 us -> 235 us (0.78)
  waiting for transfers between devices: 85.2 us -> 33.1 us
  blocking collectives: 114 us -> 102 us
  Pallas kernels: 76.3 us -> 83.1 us
  starting transfers between devices: 4.5 us -> 1.15 us
    all_gather x4 -> x1, waiting for transfers between devices: 77.6 us -> 26.8 us  [body(): weights = lax.all_gather(piece, ALL).reshape(N_BALL, N_HID, 384, 512)]
    all_gather x1 -> x0, blocking collectives: 14.8 us -> none  [body(): mlp_weights = lax.all_gather(lax.all_gather(mlp_slice, 'z'), 'ball')]
    pallas_call x4 -> x3, Pallas kernels: 30.6 us -> 38.3 us  [the longest x1 30.4 us: body(): pl.pallas_call(coarse_kernel, grid=(3 * N_HID,), out_shape=shape((PTS, C)...]
    ppermute x3 -> x1, starting transfers between devices: 4.38 us -> 1.14 us  [other_core(): return lax.ppermute(values, 'core', [(0, 1), (1, 0)])]
    all_to_all x4 -> x3, blocking collectives: 99.2 us -> 102 us  [exchange(): return lax.all_to_all(values, ALL, split_axis=0, concat_axis=0, tiled=True)]
  transfers between devices with their start and end apart: 8 -> 3, of which waited for: 5 -> 3; matrix products, arithmetic and copies ran while one was open for 1% -> 0% of each run, Pallas kernels for 23% -> 17%
where the time goes in v2:
time: 235 us; the launch traced here: 234 us
  blocking collectives  102 us (43%)
  Pallas kernels  83.1 us (35%)
  waiting for transfers between devices  33.1 us (14%)
  between operations  13.4 us (6%)
    all_to_all x3, blocking collectives, exchange(): return lax.all_to_all(values, ALL, split_axis=0, concat_axis=0, tiled=True)  102 us
    pallas_call x2, Pallas kernels, fine(): pl.pallas_call(functools.partial(fine_kernel, which), grid=(1,), out_shap...  32.8 us
    pallas_call x1, Pallas kernels, body(): pl.pallas_call(coarse_kernel, grid=(3 * N_HID,), out_shape=shape((PTS, C)...  30.4 us
    all_gather x1, waiting for transfers between devices, body(): weights = lax.all_gather(piece, ALL).reshape(N_BALL, N_HID, 384, 512)  26.8 us
    pallas_call x1, Pallas kernels, body(): pl.pallas_call(pool_kernel, grid=(N_HID,), out_shape=(shape((PTS, C), BF1...  12 us
    pallas_call x1, Pallas kernels, body(): pl.pallas_call(prep_kernel, out_shape=(shape((SLOTS, C + N_DEV), BF16), s...  6.22 us
    ppermute x1, waiting for transfers between devices, other_z(): return lax.ppermute(values, 'z', [(0, 1), (1, 0), (2, 3), (3, 2)])  5.05 us
  transfers between devices with their start and end apart: 3, of which 3 were waited for; matrix products, arithmetic and copies ran while one was open for 0% of the time, Pallas kernels for 17%

profile of v2, /device:TPU:1, one launch (start us, length us, event | category | flops | bytes accessed | tf_op | source)
XLA Modules:
  0.0 234.4 jit_solution(11325562166148004481)
XLA Ops:
  6.5 0.0 all-gather.3.cloned.1.call-start
  6.5 1.7 cut.1
  8.3 0.0 all-gather.3.cloned.1.call-update
  8.3 6.2 %prep.1 = (bf16[2048,384]{1,0:T(8,128)(2,1)}, s32[2,1024]{1,0:T(2,128)}) custom-call(bf16[1024,256]{1,0:T(8,128)(2,1)} %points.1, s32[1,1024]{1,0:T(1,128)} %bitcast.24, s32[1,1024]{1,0:T(1,128)} %bitcast.25), custom_call_target="tpu_custom_call" | custom-call | tf_op jit(solution)/shard_map/prep/pallas_call | solution.py:378
  14.5 39.6 %all_to_all.33 = bf16[128,16,384]{2,1,0:T(8,128)(2,1)} all-to-all(bf16[128,16,384]{2,1,0:T(8,128)(2,1)} %bitcast.20), channel_id=1, replica_groups=mesh['ball'=16,'z'=4,'core'=2] {'ball','z','core'}, dimensions={0} | all-to-all | bytes 3145728 | tf_op jit(solution)/shard_map/all_to_all | solution.py:298
  54.2 16.3 %fine_block_0.1 = bf16[2048,256]{1,0:T(8,128)(2,1)} custom-call(bf16[2048,384]{1,0:T(8,128)(2,1)} %bitcast.17, bf16[2048,384]{1,0:T(8,128)(2,1)} %bitcast.18, s32[2,1024]{1,0:T(2,128)} %get-tuple-element.10.slots, f32[2,2,256]{2,1,0:T(2,128)} %gains.4, bf16[2,3,256,256]{3,2,1,0:T(8,128)(2,1)} %qkv.4, bf16[2,256,256]{2,1,0:T(8,128)(2,1)} %out.4, ...), custom_call_target="tpu_custom_call" | custom-call | flops 8000000000 | bytes 4194304 | tf_op jit(solution)/shard_map/fine_block_0/pallas_call | solution.py:310
  70.5 25.0 %all_to_all.34 = bf16[128,16,256]{2,1,0:T(8,128)(2,1)} all-to-all(bf16[128,16,256]{2,1,0:T(8,128)(2,1)} %bitcast.23), channel_id=1, replica_groups=mesh['ball'=16,'z'=4,'core'=2] {'ball','z','core'}, dimensions={0} | all-to-all | bytes 2097152 | tf_op jit(solution)/shard_map/all_to_all | solution.py:298
  95.5 16.5 %fine_block_1.1 = bf16[2048,256]{1,0:T(8,128)(2,1)} custom-call(bf16[2048,256]{1,0:T(8,128)(2,1)} %bitcast.21, bf16[2048,384]{1,0:T(8,128)(2,1)} %bitcast.19, s32[2,1024]{1,0:T(2,128)} %get-tuple-element.10.slots, f32[2,2,256]{2,1,0:T(2,128)} %gains.4, bf16[2,3,256,256]{3,2,1,0:T(8,128)(2,1)} %qkv.4, bf16[2,256,256]{2,1,0:T(8,128)(2,1)} %out.4, ...), custom_call_target="tpu_custom_call" | custom-call | flops 8000000000 | bytes 4194304 | tf_op jit(solution)/shard_map/fine_block_1/pallas_call | solution.py:310
  112.0 37.4 %all_to_all.35 = bf16[128,16,256]{2,1,0:T(8,128)(2,1)} all-to-all(bf16[128,16,256]{2,1,0:T(8,128)(2,1)} %bitcast.22), channel_id=1, replica_groups=mesh['ball'=16,'z'=4,'core'=2] {'ball','z','core'}, dimensions={0} | all-to-all | bytes 2097152 | tf_op jit(solution)/shard_map/all_to_all | solution.py:298
  149.3 26.8 %all-gather.3.cloned.1.call-done = bf16[49152,512]{1,0:T(8,128)(2,1)} async-done(((bf16[384,512]{1,0:T(8,128)(2,1)}), bf16[49152,512]{1,0:T(8,128)(2,1)}) %all-gather.3.cloned.1.call-update) | async-done | bytes 50331664 | tf_op jit(solution)/shard_map/all_gather | solution.py:376
  176.2 12.0 %pool.3 = (bf16[1024,256]{1,0:T(8,128)(2,1)}, bf16[64,1024]{1,0:T(8,128)(2,1)}) custom-call(bf16[2048,256]{1,0:T(8,128)(2,1)} %bitcast.16, s32[2,1024]{1,0:T(2,128)} %get-tuple-element.10.slots, bf16[16,8,384,512]{3,2,1,0:T(8,128)(2,1)} %bitcast.10), custom_call_target="tpu_custom_call" | custom-call | tf_op jit(solution)/shard_map/pool/pallas_call | solution.py:389
  188.1 0.0 collective-permute-start
  188.1 5.1 %collective-permute-done.from_z = bf16[64,1024]{1,0:T(8,128)(2,1)S(1)} collective-permute-done((bf16[64,1024]{1,0:T(8,128)(2,1)}, bf16[64,1024]{1,0:T(8,128)(2,1)S(1)}, u32[]{:S(2)}, u32[]{:S(2)}) %collective-permute-start) | collective-permute-done | bytes 131104 | tf_op jit(solution)/shard_map/ppermute | solution.py:306
  193.2 0.0 copy-start
  193.2 1.0 pad_maximum_fusion
  194.2 1.1 collective-permute-start.1
  195.3 1.2 collective-permute-done.1.pair
  196.5 0.0 copy-start.1
  196.5 0.0 copy-done
  196.5 0.7 copy-done.1
  197.2 30.4 %coarse.1 = bf16[1024,256]{1,0:T(8,128)(2,1)} custom-call(bf16[64,1024]{1,0:T(8,128)(2,1)} %get-tuple-element.11.own, bf16[64,1024]{1,0:T(8,128)(2,1)} %copy-done, bf16[128,1024]{1,0:T(8,128)(2,1)} %copy-done.1, f32[2,1024]{1,0:T(2,128)} %gains.5, bf16[16,8,384,512]{3,2,1,0:T(8,128)(2,1)} %bitcast.11, bf16[16,8,384,512]{3,2,1,0:T(8,128)(2,1)} %bitcast.12, ...), custom_call_target="tpu_custom_call" | custom-call | tf_op jit(solution)/shard_map/coarse/pallas_call | solution.py:403
Async XLA Ops:
  6.5 169.6 %all-gather.3.cloned.1.call-start = ((), (), s32[]{:S(2)}) async-start(), calls=%async_computation.3 | async-start | bytes 50724864 | tf_op jit(solution)/shard_map/all_gather | solution.py:376
  188.1 5.1 %collective-permute-start = (bf16[64,1024]{1,0:T(8,128)(2,1)}, bf16[64,1024]{1,0:T(8,128)(2,1)S(1)}, u32[]{:S(2)}, u32[]{:S(2)}) collective-permute-start(bf16[64,1024]{1,0:T(8,128)(2,1)} %get-tuple-element.11.own), channel_id=1, source_target_pairs={{0,2},{2,0},{4,6},{6,4},{1,3},{3,1},{5,7},{7,5},{8,10},{10,8},{12,... | collective-permute-start | bytes 393224 | tf_op jit(solution)/shard_map/ppermute | solution.py:306
  193.2 3.3 %copy-start = (bf16[64,1024]{1,0:T(8,128)(2,1)}, bf16[64,1024]{1,0:T(8,128)(2,1)S(1)}, u32[]{:S(2)}) copy-start(bf16[64,1024]{1,0:T(8,128)(2,1)S(1)} %collective-permute-done.from_z) | copy-start | bytes 393220
  194.2 2.3 collective-permute-start.1
  196.5 0.7 copy-start.1
Sparse Core Ops, SparseCore 0:
  10.4 165.7 all-gather.2

commit v3 on v2

--- a/solution.py
+++ b/solution.py
@@ -64,20 +64,16 @@
     return 0.5 * v * (1.0 + jnp.tanh(0.5 * v))
 
 
-def slice_kernel(at_ball, gate_up, down, pool, unpool, qkv, out, piece):
-    piece[0:64, :] = gate_up[0]
-    piece[64:128, :] = gate_up[1]
-    piece[128:160, :] = down[:, :512]
-    piece[160:192, :] = down[:, 512:]
-    piece[192:224, :] = pool[:, :512]
-    piece[224:256, :] = pool[:, 512:]
-    piece[256:320, :] = unpool[...]
+def slice_kernel(at_ball, pool, unpool, qkv, out, piece):
+    piece[0:32, :] = pool[:, :512]
+    piece[32:64, :] = pool[:, 512:]
+    piece[64:128, :] = unpool[...]
     for part in range(4):
         rows = slice(16 * part, 16 * part + 16)
         lanes = slice(128 * part, 128 * part + 128)
         for which in range(3):
-            piece[320 + 16 * which : 336 + 16 * which, lanes] = qkv[which, rows, :]
-        piece[368:384, lanes] = out[rows, :]
+            piece[128 + 16 * which : 144 + 16 * which, lanes] = qkv[which, rows, :]
+        piece[176:192, lanes] = out[rows, :]
 
 
 def prep_kernel(points, tree, rot, send, slots):
@@ -195,17 +191,33 @@
 
 
 def coarse_kernel(
-    own, from_z, pair, gains, heads, gate, up, down, unpool, block_two, joined, keys, total, normed, out, children
+    own,
+    from_z,
+    pair,
+    pair_z,
+    gains,
+    heads,
+    own_gate_up,
+    own_down,
+    far_gate_up,
+    far_down,
+    mid,
+    kept,
+    kept_z,
+    sent,
+    normed,
+    total,
+    out,
 ):
     step = pl.program_id(0)
+    sources = (own, from_z, pair, pair_z)
 
     @pl.when(step == 0)
     def _():
-        gain = gains[0:1, :]
-        keys[0:64, :] = rms(own[...].astype(F32), gain)
-        keys[64:128, :] = rms(from_z[...].astype(F32), gain)
-        keys[128:256, :] = rms(pair[...].astype(F32), gain)
-        total[...] = own[...].astype(F32)
+        for at, ref in enumerate(sources):
+            values = ref[...].astype(F32)
+            normed[CROWS * at : CROWS * at + CROWS, :] = rms(values, gains[0:1, :])
+            total[CROWS * at : CROWS * at + CROWS, :] = values
 
     @pl.when(step < N_HID)
     def _():
@@ -221,13 +233,14 @@
                 top = 64 * (ball // 8) + 16 * part
                 out[top : top + 16, lanes] = heads[ball, 0, 48:64, 128 * part : 128 * part + 128]
 
-        q = mm(keys[0:64, :], weight(0)).astype(BF16)
-        k = mm(keys[...], weight(1)).astype(BF16)
-        v = mm(keys[...], weight(2)).astype(BF16)
+        rows = normed[...]
+        q = mm(rows, weight(0)).astype(BF16)
+        k = mm(rows, weight(1)).astype(BF16)
+        v = mm(rows, weight(2)).astype(BF16)
         head_of = iota((BALL, 128), 1) // 64
         scale = LOG2E / math.sqrt(64)
-        mixed = jnp.zeros((CROWS, 128), F32)
-        inverse = jnp.zeros((CROWS, 128), F32)
+        mixed = jnp.zeros((BALL, 128), F32)
+        inverse = jnp.zeros((BALL, 128), F32)
         zero = jnp.zeros((BALL, 128), BF16)
         for head in range(2):
             mine = head_of == head
@@ -236,36 +249,51 @@
             weights = jnp.exp2((scores - top) * scale)
             sums = jnp.sum(weights, axis=-1, keepdims=True)
             mixed = mixed + mm(weights.astype(BF16), jnp.where(mine, v, zero))
-            inverse = jnp.where(mine[:CROWS], 1.0 / sums, inverse)
+            inverse = jnp.where(mine, 1.0 / sums, inverse)
         total[...] += mm((mixed * inverse).astype(BF16), out[...])
 
     @pl.when(step == N_HID)
     def _():
-        mid = total[...].astype(BF16).astype(F32)
-        total[...] = mid
-        normed[...] = rms(mid, gains[1:2, :])
-
-    @pl.when((step >= N_HID) & (step < 2 * N_HID))
-    def _():
+        values = total[...].astype(BF16)
+        mid[...] = values[:CROWS]
+        normed[...] = rms(values.astype(F32), gains[1:2, :])
+        total[...] = jnp.zeros_like(total)
+
+    def mlp(gate_up, down):
         rows = normed[...]
-        hidden = silu(mm(rows, gate[...].reshape(CC, 512))) * mm(rows, up[...].reshape(CC, 512))
-        hidden = hidden.astype(BF16)
-        total[:, :512] += mm(hidden, down[:, 0, :32, :].reshape(512, 512))
-        total[:, 512:] += mm(hidden, down[:, 0, 32:, :].reshape(512, 512))
-
-    @pl.when(step == 2 * N_HID)
-    def _():
-        normed[...] = total[...].astype(BF16)
-
-    @pl.when(step >= 2 * N_HID)
-    def _():
-        spread = mm(normed[...], unpool[...].reshape(CC, 512)).astype(BF16).astype(F32)
-        start = pl.multiple_of((step - 2 * N_HID) * 128, 128)
-        two = block_two[...].astype(F32)
-        children[pl.ds(start, CROWS), :] = (two[:CROWS] + spread[:, :C]).astype(BF16)
-        children[pl.ds(start + CROWS, CROWS), :] = (two[CROWS:] + spread[:, C:]).astype(BF16)
-
-    @pl.when(step == 3 * N_HID - 1)
+        hidden = (silu(mm(rows, gate_up[0])) * mm(rows, gate_up[1])).astype(BF16)
+        total[...] += mm(hidden, down[...])
+
+    @pl.when((step >= N_HID) & (step < N_HID + 2))
+    def _():
+        mlp(own_gate_up, own_down)
+
+    @pl.when(step >= N_HID + 2)
+    def _():
+        mlp(far_gate_up, far_down)
+
+    @pl.when(step == N_HID + 3)
+    def _():
+        kept[...] = total[:CROWS, :]
+        kept_z[...] = total[CROWS : 2 * CROWS, :]
+        sent[...] = total[2 * CROWS :, :].astype(BF16)
+
+
+def unpool_kernel(mid, kept, got, got_z, unpool, block_two, joined, done, children):
+    step = pl.program_id(0)
+
+    @pl.when(step == 0)
+    def _():
+        parts = kept[...] + got[...].astype(F32) + got_z[...].astype(F32)
+        done[...] = (mid[...].astype(F32) + parts).astype(BF16)
+
+    spread = mm(done[...], unpool[...].reshape(CC, 512)).astype(BF16).astype(F32)
+    start = pl.multiple_of(step * 128, 128)
+    two = block_two[...].astype(F32)
+    children[pl.ds(start, CROWS), :] = (two[:CROWS] + spread[:, :C]).astype(BF16)
+    children[pl.ds(start + CROWS, CROWS), :] = (two[CROWS:] + spread[:, C:]).astype(BF16)
+
+    @pl.when(step == N_HID - 1)
     def _():
         for chunk in range(4):
             point = iota((256, PTS), 0) + chunk * 256
@@ -288,10 +316,16 @@
     return pl.BlockSpec((1,) + dims[1:], lambda *_: index)
 
 
-def unit(which, first):
+def unit(which):
     return pl.BlockSpec(
-        (N_BALL, 1, 64, 512), lambda i: (0, jnp.clip(i - first, 0, N_HID - 1), which, 0)
+        (N_BALL, 1, 64, 512), lambda i: (0, jnp.minimum(i, N_HID - 1), which, 0)
     )
+
+
+def hidden_half(first, gate_up):
+    if gate_up:
+        return pl.BlockSpec((2, CC, 256), lambda i: (0, 0, jnp.clip(i - first, 0, 1)))
+    return pl.BlockSpec((256, CC), lambda i: (jnp.clip(i - first, 0, 1), 0))
 
 
 def exchange(values):
@@ -304,6 +338,10 @@
 
 def other_z(values):
     return lax.ppermute(values, "z", [(0, 1), (1, 0), (2, 3), (3, 2)])
+
+
+def far_z(values):
+    return lax.ppermute(values, "z", [(0, 2), (2, 0), (1, 3), (3, 1)])
 
 
 def fine(which, rows, place, slots, norm, qkv, out, gate_up, down):
@@ -352,28 +390,26 @@
             num_scalar_prefetch=1,
             grid=(1,),
             in_specs=[
-                pl.BlockSpec((2, 64, 512), lambda i, at: (0, at[0], 0)),
-                pl.BlockSpec((32, CC), lambda i, at: (at[0], 0)),
                 pl.BlockSpec((32, CC), lambda i, at: (at[0], 0)),
                 pl.BlockSpec((64, 512), lambda i, at: (at[0], 0)),
                 pl.BlockSpec((3, 64, 128), lambda i, at: (0, at[0], 0)),
                 pl.BlockSpec((64, 128), lambda i, at: (at[0] // 8, at[0] % 8)),
             ],
-            out_specs=pl.BlockSpec((384, 512), lambda i, at: (0, 0)),
+            out_specs=pl.BlockSpec((192, 512), lambda i, at: (0, 0)),
         ),
-        out_shape=shape((384, 512), BF16),
+        out_shape=shape((192, 512), BF16),
         compiler_params=params(),
         name="cut",
     )(
         lax.axis_index("ball").reshape(1),
-        coarse_gate_up,
-        coarse_down,
         pool_weight,
         unpool_weight,
         coarse_qkv,
         coarse_out,
     )
-    weights = lax.all_gather(piece, ALL).reshape(N_BALL, N_HID, 384, 512)
+    weights = lax.all_gather(piece, ALL).reshape(N_BALL, N_HID, 192, 512)
+    far_gate_up = far_z(coarse_gate_up)
+    far_down = far_z(coarse_down)
 
     send, slots = pl.pallas_call(
         prep_kernel,
@@ -390,7 +426,7 @@
         pool_kernel,
         grid=(N_HID,),
         out_shape=(shape((PTS, C), BF16), shape((CROWS, CC), BF16)),
-        in_specs=[whole((SLOTS, C)), whole((2, PTS)), unit(3, 0)],
+        in_specs=[whole((SLOTS, C)), whole((2, PTS)), unit(0)],
         out_specs=(pl.BlockSpec((128, C), lambda i: (i, 0)), whole((CROWS, CC))),
         scratch_shapes=[pltpu.VMEM((CROWS, CC), F32)],
         compiler_params=params(),
@@ -398,35 +434,68 @@
     )(returned, slots, weights)
 
     from_z = other_z(coarse)
-    from_pair = other_core(jnp.concatenate([coarse, from_z], axis=0))
-
-    return pl.pallas_call(
+    rows_64 = whole((CROWS, CC))
+    mid, kept, kept_z, sent = pl.pallas_call(
         coarse_kernel,
-        grid=(3 * N_HID,),
-        out_shape=shape((PTS, C), BF16),
+        grid=(N_HID + 4,),
+        out_shape=(
+            shape((CROWS, CC), BF16),
+            shape((CROWS, CC), F32),
+            shape((CROWS, CC), F32),
+            shape((2 * CROWS, CC), BF16),
+        ),
         in_specs=[
-            whole((CROWS, CC)),
-            whole((CROWS, CC)),
-            whole((2 * CROWS, CC)),
+            rows_64,
+            rows_64,
+            rows_64,
+            rows_64,
             whole((2, CC)),
-            unit(5, 0),
-            unit(0, N_HID),
-            unit(1, N_HID),
-            unit(2, N_HID),
-            unit(4, 2 * N_HID),
-            pl.BlockSpec((128, C), lambda i: (jnp.clip(i - 2 * N_HID, 0, N_HID - 1), 0)),
+            unit(2),
+            hidden_half(N_HID, True),
+            hidden_half(N_HID, False),
+            hidden_half(N_HID + 2, True),
+            hidden_half(N_HID + 2, False),
         ],
-        out_specs=whole((PTS, C)),
+        out_specs=(rows_64, rows_64, rows_64, whole((2 * CROWS, CC))),
         scratch_shapes=[
             pltpu.VMEM((4 * CROWS, CC), BF16),
-            pltpu.VMEM((CROWS, CC), F32),
-            pltpu.VMEM((CROWS, CC), BF16),
+            pltpu.VMEM((4 * CROWS, CC), F32),
             pltpu.VMEM((128, CC), BF16),
-            pltpu.VMEM((PTS, C), BF16),
         ],
         compiler_params=params(),
         name="coarse",
-    )(coarse, from_z, from_pair, coarse_norm, *[weights] * 5, block_two)
+    )(
+        coarse,
+        from_z,
+        other_core(coarse),
+        other_core(from_z),
+        coarse_norm,
+        weights,
+        coarse_gate_up,
+        coarse_down,
+        far_gate_up,
+        far_down,
+    )
+
+    got = other_core(sent)
+    got_z = other_z((kept_z + got[CROWS:].astype(F32)).astype(BF16))
+    return pl.pallas_call(
+        unpool_kernel,
+        grid=(N_HID,),
+        out_shape=shape((PTS, C), BF16),
+        in_specs=[
+            rows_64,
+            rows_64,
+            rows_64,
+            rows_64,
+            unit(1),
+            pl.BlockSpec((128, C), lambda i: (i, 0)),
+        ],
+        out_specs=whole((PTS, C)),
+        scratch_shapes=[pltpu.VMEM((CROWS, CC), BF16), pltpu.VMEM((PTS, C), BF16)],
+        compiler_params=params(),
+        name="unpool",
+    )(mid, kept, got, got_z, weights, block_two)
 
 
 def solution(mesh):

time: 235 us -> 266 us (1.13)
  waiting for transfers between devices: 33.1 us -> 112 us
  blocking collectives: 102 us -> 38 us
  starting transfers between devices: 1.15 us -> 19.7 us
  Pallas kernels: 83.1 us -> 78.4 us
    all_to_all x0 -> x2, waiting for transfers between devices: none -> 75 us  [exchange(): return lax.all_to_all(values, ALL, split_axis=0, concat_axis=0, tiled=True)]
    all_to_all x3 -> x1, blocking collectives: 102 us -> 38 us  [exchange(): return lax.all_to_all(values, ALL, split_axis=0, concat_axis=0, tiled=True)]
    all_to_all x0 -> x2, starting transfers between devices: none -> 10.7 us  [exchange(): return lax.all_to_all(values, ALL, split_axis=0, concat_axis=0, tiled=True)]
    ppermute x0 -> x2, starting transfers between devices: none -> 7.18 us  [far_z(): return lax.ppermute(values, 'z', [(0, 2), (2, 0), (1, 3), (3, 1)])]
    pallas_call x1 -> x2, Pallas kernels: 30.4 us -> 25.6 us  [the longest x1 17.1 us: body(): pl.pallas_call(coarse_kernel, grid=(N_HID + 4,), out_shape=(shape((CROWS,...]
    ppermute x1 -> x2, waiting for transfers between devices: 5.05 us -> 9.43 us  [other_z(): return lax.ppermute(values, 'z', [(0, 1), (1, 0), (2, 3), (3, 2)])]
  transfers between devices with their start and end apart: 3 -> 10, of which waited for: 3 -> 7; matrix products, arithmetic and copies ran while one was open for 0% -> 0% of each run, Pallas kernels for 17% -> 19%
where the time goes in v3:
time: 266 us; the launch traced here: 265 us
  waiting for transfers between devices  112 us (42%)
  Pallas kernels  78.4 us (29%)
  blocking collectives  38 us (14%)
  starting transfers between devices  19.7 us (7%)
  between operations  13.5 us (5%)
    all_to_all x2, waiting for transfers between devices, exchange(): return lax.all_to_all(values, ALL, split_axis=0, concat_axis=0, tiled=True)  75 us
    all_to_all x1, blocking collectives, exchange(): return lax.all_to_all(values, ALL, split_axis=0, concat_axis=0, tiled=True)  38 us
    pallas_call x2, Pallas kernels, fine(): pl.pallas_call(functools.partial(fine_kernel, which), grid=(1,), out_shap...  32.9 us
    all_gather x1, waiting for transfers between devices, body(): weights = lax.all_gather(piece, ALL).reshape(N_BALL, N_HID, 192, 512)  25.1 us
    pallas_call x1, Pallas kernels, body(): pl.pallas_call(coarse_kernel, grid=(N_HID + 4,), out_shape=(shape((CROWS,...  17.1 us
    pallas_call x1, Pallas kernels, body(): pl.pallas_call(pool_kernel, grid=(N_HID,), out_shape=(shape((PTS, C), BF1...  12 us
    all_to_all x2, starting transfers between devices, exchange(): return lax.all_to_all(values, ALL, split_axis=0, concat_axis=0, tiled=True)  10.7 us
    ppermute x2, waiting for transfers between devices, other_z(): return lax.ppermute(values, 'z', [(0, 1), (1, 0), (2, 3), (3, 2)])  9.43 us
  transfers between devices with their start and end apart: 10, of which 7 were waited for; matrix products, arithmetic and copies ran while one was open for 0% of the time, Pallas kernels for 19%

profile of v3, /device:TPU:1, one launch (start us, length us, event | category | flops | bytes accessed | tf_op | source)
XLA Modules:
  0.0 264.9 jit_solution(1897529829180221912)
XLA Ops:
  6.5 1.6 cut.1
  8.1 6.3 %prep.1 = (bf16[2048,384]{1,0:T(8,128)(2,1)}, s32[2,1024]{1,0:T(2,128)}) custom-call(bf16[1024,256]{1,0:T(8,128)(2,1)} %points.1, s32[1,1024]{1,0:T(1,128)} %bitcast.21, s32[1,1024]{1,0:T(1,128)} %bitcast.22), custom_call_target="tpu_custom_call" | custom-call | tf_op jit(solution)/shard_map/prep/pallas_call | solution.py:414
  14.4 38.0 %all_to_all.33 = bf16[128,16,384]{2,1,0:T(8,128)(2,1)} all-to-all(bf16[128,16,384]{2,1,0:T(8,128)(2,1)} %bitcast.17), channel_id=1, replica_groups=mesh['ball'=16,'z'=4,'core'=2] {'ball','z','core'}, dimensions={0} | all-to-all | bytes 3145728 | tf_op jit(solution)/shard_map/all_to_all | solution.py:332
  52.4 16.4 %fine_block_0.1 = bf16[2048,256]{1,0:T(8,128)(2,1)} custom-call(bf16[2048,384]{1,0:T(8,128)(2,1)} %bitcast.14, bf16[2048,384]{1,0:T(8,128)(2,1)} %bitcast.15, s32[2,1024]{1,0:T(2,128)} %get-tuple-element.14.slots, f32[2,2,256]{2,1,0:T(2,128)} %gains.4, bf16[2,3,256,256]{3,2,1,0:T(8,128)(2,1)} %qkv.4, bf16[2,256,256]{2,1,0:T(8,128)(2,1)} %out.4, ...), custom_call_target="tpu_custom_call" | custom-call | flops 8000000000 | bytes 4194304 | tf_op jit(solution)/shard_map/fine_block_0/pallas_call | solution.py:348
  68.8 4.6 %all-to-all-start.1 = ((bf16[128,16,256]{2,1,0:T(8,128)(2,1)}), bf16[128,16,256]{2,1,0:T(8,128)(2,1)S(1)}, u32[]{:S(2)}, u32[]{:S(2)}) async-start(bf16[128,16,256]{2,1,0:T(8,128)(2,1)} %bitcast.20), calls=%async_computation.1 | async-start | bytes 2097152 | tf_op jit(solution)/shard_map/all_to_all | solution.py:332
  73.5 3.7 %collective-permute-start.3 = (bf16[2,1024,512]{2,1,0:T(8,128)(2,1)S(1)}, bf16[2,1024,512]{2,1,0:T(8,128)(2,1)}, u32[]{:S(2)}, u32[]{:S(2)}) collective-permute-start(bf16[2,1024,512]{2,1,0:T(8,128)(2,1)S(1)} %copy-done.1), channel_id=1, source_target_pairs={{0,4},{4,0},{2,6},{6,2},{1,5},{5,1},{3,7},{7,3},{8,12},{12,8},{10,... | collective-permute-start | bytes 6291464 | tf_op jit(solution)/shard_map/ppermute | solution.py:344
  77.2 22.2 %all-to-all-done.1 = bf16[128,16,256]{2,1,0:T(8,128)(2,1)S(1)} async-done(((bf16[128,16,256]{2,1,0:T(8,128)(2,1)}), bf16[128,16,256]{2,1,0:T(8,128)(2,1)S(1)}, u32[]{:S(2)}, u32[]{:S(2)}) %all-to-all-start.1) | async-done | bytes 1048608 | tf_op jit(solution)/shard_map/all_to_all | solution.py:332
  99.4 1.0 copy-done.2
  100.4 16.5 %fine_block_1.1 = bf16[2048,256]{1,0:T(8,128)(2,1)} custom-call(bf16[2048,256]{1,0:T(8,128)(2,1)} %bitcast.18, bf16[2048,384]{1,0:T(8,128)(2,1)} %bitcast.16, s32[2,1024]{1,0:T(2,128)} %get-tuple-element.14.slots, f32[2,2,256]{2,1,0:T(2,128)} %gains.4, bf16[2,3,256,256]{3,2,1,0:T(8,128)(2,1)} %qkv.4, bf16[2,256,256]{2,1,0:T(8,128)(2,1)} %out.4, ...), custom_call_target="tpu_custom_call" | custom-call | flops 8000000000 | bytes 4194304 | tf_op jit(solution)/shard_map/fine_block_1/pallas_call | solution.py:348
  116.9 6.1 %all-to-all-start.2 = ((bf16[128,16,256]{2,1,0:T(8,128)(2,1)}), bf16[128,16,256]{2,1,0:T(8,128)(2,1)S(1)}, u32[]{:S(2)}, u32[]{:S(2)}) async-start(bf16[128,16,256]{2,1,0:T(8,128)(2,1)} %bitcast.19), calls=%async_computation.2 | async-start | bytes 2097152 | tf_op jit(solution)/shard_map/all_to_all | solution.py:332
  123.0 3.5 %collective-permute-start.4 = (bf16[512,1024]{1,0:T(8,128)(2,1)}, bf16[512,1024]{1,0:T(8,128)(2,1)}, u32[]{:S(2)}, u32[]{:S(2)}) collective-permute-start(bf16[512,1024]{1,0:T(8,128)(2,1)} %own_down.1), channel_id=1, source_target_pairs={{0,4},{4,0},{2,6},{6,2},{1,5},{5,1},{3,7},{7,3},{8,12},{12,8},{10,... | collective-permute-start | bytes 3145736 | tf_op jit(solution)/shard_map/ppermute | solution.py:344
  126.5 52.8 %all-to-all-done.2 = bf16[128,16,256]{2,1,0:T(8,128)(2,1)S(1)} async-done(((bf16[128,16,256]{2,1,0:T(8,128)(2,1)}), bf16[128,16,256]{2,1,0:T(8,128)(2,1)S(1)}, u32[]{:S(2)}, u32[]{:S(2)}) %all-to-all-start.2) | async-done | bytes 1048608 | tf_op jit(solution)/shard_map/all_to_all | solution.py:332
  179.2 25.1 %all-gather.3.cloned.1.call-done = bf16[24576,512]{1,0:T(8,128)(2,1)} async-done(((bf16[192,512]{1,0:T(8,128)(2,1)}), bf16[24576,512]{1,0:T(8,128)(2,1)}) %all-gather.3.cloned.1.call-update) | async-done | bytes 25165840 | tf_op jit(solution)/shard_map/all_gather | solution.py:410
  204.4 12.0 %pool.3 = (bf16[1024,256]{1,0:T(8,128)(2,1)}, bf16[64,1024]{1,0:T(8,128)(2,1)}) custom-call(bf16[2048,256]{1,0:T(8,128)(2,1)} %bitcast.13, s32[2,1024]{1,0:T(2,128)} %get-tuple-element.14.slots, bf16[16,8,192,512]{3,2,1,0:T(8,128)(2,1)} %bitcast.10), custom_call_target="tpu_custom_call" | custom-call | tf_op jit(solution)/shard_map/pool/pallas_call | solution.py:425
  216.7 4.7 %collective-permute-done.from_z = bf16[64,1024]{1,0:T(8,128)(2,1)S(1)} collective-permute-done((bf16[64,1024]{1,0:T(8,128)(2,1)}, bf16[64,1024]{1,0:T(8,128)(2,1)S(1)}, u32[]{:S(2)}, u32[]{:S(2)}) %collective-permute-start) | collective-permute-done | bytes 131104 | tf_op jit(solution)/shard_map/ppermute | solution.py:340
  221.4 1.1 collective-permute-start.2
  222.5 1.0 collective-permute-done.2.pair_z
  223.5 0.7 copy-done.6
  224.1 17.1 %coarse.1 = (bf16[64,1024]{1,0:T(8,128)(2,1)}, f32[64,1024]{1,0:T(8,128)}, f32[64,1024]{1,0:T(8,128)}, bf16[128,1024]{1,0:T(8,128)(2,1)}) custom-call(bf16[64,1024]{1,0:T(8,128)(2,1)} %get-tuple-element.15.own, bf16[64,1024]{1,0:T(8,128)(2,1)} %copy-done.4, bf16[64,1024]{1,0:T(8,128)(2,1)} %copy-done.5, bf16[64,1024]{1,0:T(8,128)(2,1)} %copy-done.6, ...), custom_call_target="tpu_custom_call" | custom-call | tf_op jit(solution)/shard_map/coarse/pallas_call | solution.py:438
  241.6 1.4 collective-permute-done.5.got
  242.9 1.1 add_convert_fusion
  244.1 4.7 %collective-permute-done.6.got_z = bf16[64,1024]{1,0:T(8,128)(2,1)S(1)} collective-permute-done((bf16[64,1024]{1,0:T(8,128)(2,1)S(1)}, bf16[64,1024]{1,0:T(8,128)(2,1)S(1)}, u32[]{:S(2)}, u32[]{:S(2)}) %collective-permute-start.6) | collective-permute-done | bytes 131104 | tf_op jit(solution)/shard_map/ppermute | solution.py:340
  248.8 0.7 copy-done.7
  249.5 8.6 %unpool.3 = bf16[1024,256]{1,0:T(8,128)(2,1)} custom-call(bf16[64,1024]{1,0:T(8,128)(2,1)} %get-tuple-element.16.mid, f32[64,1024]{1,0:T(8,128)} %get-tuple-element.17.kept, bf16[128,1024]{1,0:T(8,128)(2,1)} %copy-done.3, bf16[64,1024]{1,0:T(8,128)(2,1)} %copy-done.7, bf16[16,8,192,512]{3,2,1,0:T(8,128)(2,1)} %bitcast.12, ...), custom_call_target="tpu_custom_call" | custom-call | tf_op jit(solution)/shard_map/unpool/pallas_call | solution.py:482
  (22 shorter events, 0.8 us)
Async XLA Ops:
  6.5 197.8 %all-gather.3.cloned.1.call-start = ((), (), s32[]{:S(2)}) async-start(), calls=%async_computation.3 | async-start | bytes 25362432 | tf_op jit(solution)/shard_map/all_gather | solution.py:410
  68.8 4.7 %copy-start.1 = (bf16[2,1024,512]{2,1,0:T(8,128)(2,1)S(1)}, bf16[2,1024,512]{2,1,0:T(8,128)(2,1)}, u32[]{:S(2)}) copy-start(bf16[2,1024,512]{2,1,0:T(8,128)(2,1)} %own_gate_up.1) | copy-start | bytes 6291460
  68.8 30.6 %all-to-all-start.1 = ((bf16[128,16,256]{2,1,0:T(8,128)(2,1)}), bf16[128,16,256]{2,1,0:T(8,128)(2,1)S(1)}, u32[]{:S(2)}, u32[]{:S(2)}) async-start(bf16[128,16,256]{2,1,0:T(8,128)(2,1)} %bitcast.20), calls=%async_computation.1 | async-start | bytes 2097152 | tf_op jit(solution)/shard_map/all_to_all | solution.py:332
  73.5 149.0 %collective-permute-start.3 = (bf16[2,1024,512]{2,1,0:T(8,128)(2,1)S(1)}, bf16[2,1024,512]{2,1,0:T(8,128)(2,1)}, u32[]{:S(2)}, u32[]{:S(2)}) collective-permute-start(bf16[2,1024,512]{2,1,0:T(8,128)(2,1)S(1)} %copy-done.1), channel_id=1, source_target_pairs={{0,4},{4,0},{2,6},{6,2},{1,5},{5,1},{3,7},{7,3},{8,12},{12,8},{10,... | collective-permute-start | bytes 6291464 | tf_op jit(solution)/shard_map/ppermute | solution.py:344
  99.4 1.0 copy-start.2
  116.9 62.3 %all-to-all-start.2 = ((bf16[128,16,256]{2,1,0:T(8,128)(2,1)}), bf16[128,16,256]{2,1,0:T(8,128)(2,1)S(1)}, u32[]{:S(2)}, u32[]{:S(2)}) async-start(bf16[128,16,256]{2,1,0:T(8,128)(2,1)} %bitcast.19), calls=%async_computation.2 | async-start | bytes 2097152 | tf_op jit(solution)/shard_map/all_to_all | solution.py:332
  123.0 99.5 %collective-permute-start.4 = (bf16[512,1024]{1,0:T(8,128)(2,1)}, bf16[512,1024]{1,0:T(8,128)(2,1)}, u32[]{:S(2)}, u32[]{:S(2)}) collective-permute-start(bf16[512,1024]{1,0:T(8,128)(2,1)} %own_down.1), channel_id=1, source_target_pairs={{0,4},{4,0},{2,6},{6,2},{1,5},{5,1},{3,7},{7,3},{8,12},{12,8},{10,... | collective-permute-start | bytes 3145736 | tf_op jit(solution)/shard_map/ppermute | solution.py:344
  179.2 25.1 %copy-start = (bf16[128,16,256]{2,1,0:T(8,128)(2,1)}, bf16[128,16,256]{2,1,0:T(8,128)(2,1)S(1)}, u32[]{:S(2)}) copy-start(bf16[128,16,256]{2,1,0:T(8,128)(2,1)S(1)} %all-to-all-done.2) | copy-start | bytes 3145732
  216.3 5.1 %collective-permute-start = (bf16[64,1024]{1,0:T(8,128)(2,1)}, bf16[64,1024]{1,0:T(8,128)(2,1)S(1)}, u32[]{:S(2)}, u32[]{:S(2)}) collective-permute-start(bf16[64,1024]{1,0:T(8,128)(2,1)} %get-tuple-element.15.own), channel_id=1, source_target_pairs={{0,2},{2,0},{4,6},{6,4},{1,3},{3,1},{5,7},{7,5},{8,10},{10,8},{12,... | collective-permute-start | bytes 393224 | tf_op jit(solution)/shard_map/ppermute | solution.py:340
  216.3 6.1 %collective-permute-start.1 = (bf16[64,1024]{1,0:T(8,128)(2,1)}, bf16[64,1024]{1,0:T(8,128)(2,1)S(1)}, u32[]{:S(2)}, u32[]{:S(2)}) collective-permute-start(bf16[64,1024]{1,0:T(8,128)(2,1)} %get-tuple-element.15.own), channel_id=1, source_target_pairs={{0,1},{1,0},{2,3},{3,2},{4,5},{5,4},{6,7},{7,6},{8,9},{9,8},{10,11... | collective-permute-start | bytes 393224 | tf_op jit(solution)/shard_map/ppermute | solution.py:336
  221.4 2.1 copy-start.4
  221.4 2.1 collective-permute-start.2
  222.5 1.0 copy-start.5
  223.5 0.7 copy-start.6
  241.2 1.7 collective-permute-start.5
  242.9 5.9 %copy-start.3 = (bf16[128,1024]{1,0:T(8,128)(2,1)}, bf16[128,1024]{1,0:T(8,128)(2,1)S(1)}, u32[]{:S(2)}) copy-start(bf16[128,1024]{1,0:T(8,128)(2,1)S(1)} %collective-permute-done.5.got) | copy-start | bytes 786436
  244.0 4.8 %collective-permute-start.6 = (bf16[64,1024]{1,0:T(8,128)(2,1)S(1)}, bf16[64,1024]{1,0:T(8,128)(2,1)S(1)}, u32[]{:S(2)}, u32[]{:S(2)}) collective-permute-start(bf16[64,1024]{1,0:T(8,128)(2,1)S(1)} %add_convert_fusion), channel_id=1, source_target_pairs={{0,2},{2,0},{4,6},{6,4},{1,3},{3,1},{5,7},{7,5},{8,10},{10,8},{12,... | collective-permute-start | bytes 393224 | tf_op jit(solution)/shard_map/ppermute | solution.py:340
  248.8 0.7 copy-start.7
Sparse Core Ops, SparseCore 0:
  10.4 193.9 all-gather.2

commit v4 on v3

--- a/solution.py
+++ b/solution.py
@@ -64,7 +64,11 @@
     return 0.5 * v * (1.0 + jnp.tanh(0.5 * v))
 
 
-def slice_kernel(at_ball, pool, unpool, qkv, out, piece):
+def slice_kernel(at_ball, gate_up, down, pool, unpool, qkv, out, mlp, piece):
+    mlp[0:64, :] = gate_up[0]
+    mlp[64:128, :] = gate_up[1]
+    mlp[128:160, :] = down[:, :512]
+    mlp[160:192, :] = down[:, 512:]
     piece[0:32, :] = pool[:, :512]
     piece[32:64, :] = pool[:, 512:]
     piece[64:128, :] = unpool[...]
@@ -199,7 +203,8 @@
     heads,
     own_gate_up,
     own_down,
-    far_gate_up,
+    far_gate,
+    far_up,
     far_down,
     mid,
     kept,
@@ -259,18 +264,19 @@
         normed[...] = rms(values.astype(F32), gains[1:2, :])
         total[...] = jnp.zeros_like(total)
 
-    def mlp(gate_up, down):
+    def hidden_of(gate, up):
         rows = normed[...]
-        hidden = (silu(mm(rows, gate_up[0])) * mm(rows, gate_up[1])).astype(BF16)
-        total[...] += mm(hidden, down[...])
+        return (silu(mm(rows, gate)) * mm(rows, up)).astype(BF16)
 
     @pl.when((step >= N_HID) & (step < N_HID + 2))
     def _():
-        mlp(own_gate_up, own_down)
+        total[...] += mm(hidden_of(own_gate_up[0], own_gate_up[1]), own_down[...])
 
     @pl.when(step >= N_HID + 2)
     def _():
-        mlp(far_gate_up, far_down)
+        hidden = hidden_of(far_gate[...].reshape(CC, 256), far_up[...].reshape(CC, 256))
+        total[:, :512] += mm(hidden, far_down[:, :32, :].reshape(256, 512))
+        total[:, 512:] += mm(hidden, far_down[:, 32:, :].reshape(256, 512))
 
     @pl.when(step == N_HID + 3)
     def _():
@@ -326,6 +332,17 @@
     if gate_up:
         return pl.BlockSpec((2, CC, 256), lambda i: (0, 0, jnp.clip(i - first, 0, 1)))
     return pl.BlockSpec((256, CC), lambda i: (jnp.clip(i - first, 0, 1), 0))
+
+
+def far_halves(first):
+    def half(i):
+        return jnp.clip(i - first, 0, 1)
+
+    return (
+        pl.BlockSpec((N_BALL, 64, 256), lambda i: (0, 0, half(i))),
+        pl.BlockSpec((N_BALL, 64, 256), lambda i: (0, 1, half(i))),
+        pl.BlockSpec((N_BALL // 2, 64, 512), lambda i: (half(i), 2, 0)),
+    )
 
 
 def exchange(values):
@@ -384,39 +401,44 @@
     coarse_down,
     unpool_weight,
 ):
-    piece = pl.pallas_call(
+    mlp_piece, piece = pl.pallas_call(
         slice_kernel,
         grid_spec=pltpu.PrefetchScalarGridSpec(
             num_scalar_prefetch=1,
             grid=(1,),
             in_specs=[
+                pl.BlockSpec((2, 64, 512), lambda i, at: (0, at[0], 0)),
+                pl.BlockSpec((32, CC), lambda i, at: (at[0], 0)),
                 pl.BlockSpec((32, CC), lambda i, at: (at[0], 0)),
                 pl.BlockSpec((64, 512), lambda i, at: (at[0], 0)),
                 pl.BlockSpec((3, 64, 128), lambda i, at: (0, at[0], 0)),
                 pl.BlockSpec((64, 128), lambda i, at: (at[0] // 8, at[0] % 8)),
             ],
-            out_specs=pl.BlockSpec((192, 512), lambda i, at: (0, 0)),
+            out_specs=(pl.BlockSpec((192, 512), lambda i, at: (0, 0)),) * 2,
         ),
-        out_shape=shape((192, 512), BF16),
+        out_shape=(shape((192, 512), BF16),) * 2,
         compiler_params=params(),
         name="cut",
     )(
         lax.axis_index("ball").reshape(1),
+        coarse_gate_up,
+        coarse_down,
         pool_weight,
         unpool_weight,
         coarse_qkv,
         coarse_out,
     )
     weights = lax.all_gather(piece, ALL).reshape(N_BALL, N_HID, 192, 512)
-    far_gate_up = far_z(coarse_gate_up)
-    far_down = far_z(coarse_down)
 
     send, slots = pl.pallas_call(
         prep_kernel,
         out_shape=(shape((SLOTS, C + N_DEV), BF16), shape((2, PTS), I32)),
         compiler_params=params(),
+        cost_estimate=pl.CostEstimate(flops=6 * 10**9, bytes_accessed=2 * 2**20, transcendentals=0),
         name="prep",
     )(points, tree_slot.reshape(1, PTS), rotated_slot.reshape(1, PTS))
+    far_piece, send = lax.optimization_barrier((far_z(mlp_piece), send))
+    far_mlp = lax.all_gather(far_piece, "ball")
     first = exchange(send)
     fine_weights = (fine_norm, fine_qkv, fine_out, fine_gate_up, fine_down)
     rows = exchange(fine(0, first, first, slots, *fine_weights))
@@ -453,8 +475,7 @@
             unit(2),
             hidden_half(N_HID, True),
             hidden_half(N_HID, False),
-            hidden_half(N_HID + 2, True),
-            hidden_half(N_HID + 2, False),
+            *far_halves(N_HID + 2),
         ],
         out_specs=(rows_64, rows_64, rows_64, whole((2 * CROWS, CC))),
         scratch_shapes=[
@@ -473,8 +494,9 @@
         weights,
         coarse_gate_up,
         coarse_down,
-        far_gate_up,
-        far_down,
+        far_mlp,
+        far_mlp,
+        far_mlp,
     )
 
     got = other_core(sent)

time: 266 us -> 220 us (0.83)
  waiting for transfers between devices: 112 us -> 21.8 us
  blocking collectives: 38 us -> 91.6 us
  starting transfers between devices: 19.7 us -> 10.6 us
    all_to_all x2 -> x0, waiting for transfers between devices: 75 us -> none  [exchange(): return lax.all_to_all(values, ALL, split_axis=0, concat_axis=0, tiled=True)]
    all_to_all x1 -> x3, blocking collectives: 38 us -> 91.6 us  [exchange(): return lax.all_to_all(values, ALL, split_axis=0, concat_axis=0, tiled=True)]
    all_gather x1, waiting for transfers between devices: 25.1 us -> 0.01 us  [body(): weights = lax.all_gather(piece, ALL).reshape(N_BALL, N_HID, 192, 512)]
    all_gather x0 -> x1, waiting for transfers between devices: none -> 14.2 us  [body(): far_mlp = lax.all_gather(far_piece, 'ball')]
    all_to_all x2 -> x0, starting transfers between devices: 10.7 us -> none  [exchange(): return lax.all_to_all(values, ALL, split_axis=0, concat_axis=0, tiled=True)]
    ppermute x2, waiting for transfers between devices: 9.43 us -> 6.1 us  [other_z(): return lax.ppermute(values, 'z', [(0, 1), (1, 0), (2, 3), (3, 2)])]
    ppermute x3, starting transfers between devices: 1.76 us -> 4.67 us  [other_core(): return lax.ppermute(values, 'core', [(0, 1), (1, 0)])]
    ppermute x2 -> x1, starting transfers between devices: 7.18 us -> 4.51 us  [far_z(): return lax.ppermute(values, 'z', [(0, 2), (2, 0), (1, 3), (3, 1)])]
  transfers between devices with their start and end apart: 10 -> 8, of which waited for: 7 -> 4; matrix products, arithmetic and copies ran while one was open for 0% -> 0% of each run, Pallas kernels for 19% -> 23%
where the time goes in v4:
time: 220 us; the launch traced here: 219 us
  blocking collectives  91.6 us (42%)
  Pallas kernels  78.8 us (36%)
  waiting for transfers between devices  21.8 us (10%)
  between operations  13.4 us (6%)
  starting transfers between devices  10.6 us (5%)
    all_to_all x3, blocking collectives, exchange(): return lax.all_to_all(values, ALL, split_axis=0, concat_axis=0, tiled=True)  91.6 us
    pallas_call x2, Pallas kernels, fine(): pl.pallas_call(functools.partial(fine_kernel, which), grid=(1,), out_shap...  33 us
    pallas_call x1, Pallas kernels, body(): pl.pallas_call(coarse_kernel, grid=(N_HID + 4,), out_shape=(shape((CROWS,...  17.2 us
    all_gather x1, waiting for transfers between devices, body(): far_mlp = lax.all_gather(far_piece, 'ball')  14.2 us
    pallas_call x1, Pallas kernels, body(): pl.pallas_call(pool_kernel, grid=(N_HID,), out_shape=(shape((PTS, C), BF1...  12 us
    pallas_call x1, Pallas kernels, body(): pl.pallas_call(unpool_kernel, grid=(N_HID,), out_shape=shape((PTS, C), BF...  8.56 us
    pallas_call x1, Pallas kernels, body(): pl.pallas_call(prep_kernel, out_shape=(shape((SLOTS, C + N_DEV), BF16), s...  6.23 us
    ppermute x2, waiting for transfers between devices, other_z(): return lax.ppermute(values, 'z', [(0, 1), (1, 0), (2, 3), (3, 2)])  6.1 us
  transfers between devices with their start and end apart: 8, of which 4 were waited for; matrix products, arithmetic and copies ran while one was open for 0% of the time, Pallas kernels for 23%

profile of v4, /device:TPU:1, one launch (start us, length us, event | category | flops | bytes accessed | tf_op | source)
XLA Modules:
  0.0 219.2 jit_solution(16802109659179521767)
XLA Ops:
  6.5 1.7 cut.1
  8.3 4.5 %collective-permute-start = (bf16[192,512]{1,0:T(8,128)(2,1)}, bf16[192,512]{1,0:T(8,128)(2,1)S(1)}, u32[]{:S(2)}, u32[]{:S(2)}) collective-permute-start(bf16[192,512]{1,0:T(8,128)(2,1)} %get-tuple-element.17), channel_id=1, source_target_pairs={{0,4},{4,0},{2,6},{6,2},{1,5},{5,1},{3,7},{7,3},{8,12},{12,8},{10,... | collective-permute-start | bytes 589832 | tf_op jit(solution)/shard_map/ppermute | solution.py:361
  12.8 6.2 %prep.1 = (bf16[2048,384]{1,0:T(8,128)(2,1)}, s32[2,1024]{1,0:T(2,128)}) custom-call(bf16[1024,256]{1,0:T(8,128)(2,1)} %points.1, s32[1,1024]{1,0:T(1,128)} %bitcast.25, s32[1,1024]{1,0:T(1,128)} %bitcast.26), custom_call_target="tpu_custom_call" | custom-call | flops 6000000000 | bytes 2097152 | tf_op jit(solution)/shard_map/prep/pallas_call | solution.py:433
  19.1 0.7 copy-done.1
  19.8 34.8 %all_to_all.33 = bf16[128,16,384]{2,1,0:T(8,128)(2,1)} all-to-all(bf16[128,16,384]{2,1,0:T(8,128)(2,1)} %bitcast.18), channel_id=1, replica_groups=mesh['ball'=16,'z'=4,'core'=2] {'ball','z','core'}, dimensions={0} | all-to-all | bytes 3145728 | tf_op jit(solution)/shard_map/all_to_all | solution.py:349
  54.6 16.4 %fine_block_0.1 = bf16[2048,256]{1,0:T(8,128)(2,1)} custom-call(bf16[2048,384]{1,0:T(8,128)(2,1)} %bitcast.19, bf16[2048,384]{1,0:T(8,128)(2,1)} %bitcast.20, s32[2,1024]{1,0:T(2,128)} %get-tuple-element.20.slots, f32[2,2,256]{2,1,0:T(2,128)} %gains.4, bf16[2,3,256,256]{3,2,1,0:T(8,128)(2,1)} %qkv.5, bf16[2,256,256]{2,1,0:T(8,128)(2,1)} %out.5, ...), custom_call_target="tpu_custom_call" | custom-call | flops 8000000000 | bytes 4194304 | tf_op jit(solution)/shard_map/fine_block_0/pallas_call | solution.py:365
  71.0 31.0 %all_to_all.34 = bf16[128,16,256]{2,1,0:T(8,128)(2,1)} all-to-all(bf16[128,16,256]{2,1,0:T(8,128)(2,1)} %bitcast.24), channel_id=1, replica_groups=mesh['ball'=16,'z'=4,'core'=2] {'ball','z','core'}, dimensions={0} | all-to-all | bytes 2097152 | tf_op jit(solution)/shard_map/all_to_all | solution.py:349
  101.9 16.7 %fine_block_1.1 = bf16[2048,256]{1,0:T(8,128)(2,1)} custom-call(bf16[2048,256]{1,0:T(8,128)(2,1)} %bitcast.22, bf16[2048,384]{1,0:T(8,128)(2,1)} %bitcast.21, s32[2,1024]{1,0:T(2,128)} %get-tuple-element.20.slots, f32[2,2,256]{2,1,0:T(2,128)} %gains.4, bf16[2,3,256,256]{3,2,1,0:T(8,128)(2,1)} %qkv.5, bf16[2,256,256]{2,1,0:T(8,128)(2,1)} %out.5, ...), custom_call_target="tpu_custom_call" | custom-call | flops 8000000000 | bytes 4194304 | tf_op jit(solution)/shard_map/fine_block_1/pallas_call | solution.py:365
  118.6 25.8 %all_to_all.35 = bf16[128,16,256]{2,1,0:T(8,128)(2,1)} all-to-all(bf16[128,16,256]{2,1,0:T(8,128)(2,1)} %bitcast.23), channel_id=1, replica_groups=mesh['ball'=16,'z'=4,'core'=2] {'ball','z','core'}, dimensions={0} | all-to-all | bytes 2097152 | tf_op jit(solution)/shard_map/all_to_all | solution.py:349
  144.4 12.0 %pool.3 = (bf16[1024,256]{1,0:T(8,128)(2,1)}, bf16[64,1024]{1,0:T(8,128)(2,1)}) custom-call(bf16[2048,256]{1,0:T(8,128)(2,1)} %bitcast.17, s32[2,1024]{1,0:T(2,128)} %get-tuple-element.20.slots, bf16[16,8,192,512]{3,2,1,0:T(8,128)(2,1)} %bitcast.11), custom_call_target="tpu_custom_call" | custom-call | tf_op jit(solution)/shard_map/pool/pallas_call | solution.py:447
  156.4 1.4 collective-permute-start.2
  157.8 2.7 %collective-permute-done.1.from_z = bf16[64,1024]{1,0:T(8,128)(2,1)S(1)} collective-permute-done((bf16[64,1024]{1,0:T(8,128)(2,1)}, bf16[64,1024]{1,0:T(8,128)(2,1)S(1)}, u32[]{:S(2)}, u32[]{:S(2)}) %collective-permute-start.1) | collective-permute-done | bytes 131104 | tf_op jit(solution)/shard_map/ppermute | solution.py:357
  160.4 2.3 %collective-permute-start.3 = (bf16[64,1024]{1,0:T(8,128)(2,1)S(1)}, bf16[64,1024]{1,0:T(8,128)(2,1)S(1)}, u32[]{:S(2)}, u32[]{:S(2)}) collective-permute-start(bf16[64,1024]{1,0:T(8,128)(2,1)S(1)} %collective-permute-done.1.from_z), channel_id=1, source_target_pairs={{0,1},{1,0},{2,3},{3,2},{4,5},{5,4},{6,7},{7,6},{8,9},{9,8},{10,11... | collective-permute-start | bytes 393224 | tf_op jit(solution)/shard_map/ppermute | solution.py:353
  162.7 14.2 %all-gather.7.cloned.1.call-done = bf16[3072,512]{1,0:T(8,128)(2,1)} async-done(((bf16[192,512]{1,0:T(8,128)(2,1)}), bf16[3072,512]{1,0:T(8,128)(2,1)}) %all-gather.7.cloned.1.call-update) | async-done | bytes 3145744 | tf_op jit(solution)/shard_map/all_gather | solution.py:441
  177.0 0.6 copy-done.3
  177.6 0.1 copy-done.4
  177.7 17.2 %coarse.1 = (bf16[64,1024]{1,0:T(8,128)(2,1)}, f32[64,1024]{1,0:T(8,128)}, f32[64,1024]{1,0:T(8,128)}, bf16[128,1024]{1,0:T(8,128)(2,1)}) custom-call(bf16[64,1024]{1,0:T(8,128)(2,1)} %get-tuple-element.22.own, bf16[64,1024]{1,0:T(8,128)(2,1)} %copy-done.2, bf16[64,1024]{1,0:T(8,128)(2,1)} %copy-done.3, bf16[64,1024]{1,0:T(8,128)(2,1)} %copy-done.4, ...), custom_call_target="tpu_custom_call" | custom-call | tf_op jit(solution)/shard_map/coarse/pallas_call | solution.py:460
  194.9 1.0 collective-permute-start.4
  196.0 1.4 collective-permute-done.4.got
  197.3 1.1 add_convert_fusion
  198.4 1.4 collective-permute-start.5
  199.8 3.4 %collective-permute-done.5.got_z = bf16[64,1024]{1,0:T(8,128)(2,1)S(1)} collective-permute-done((bf16[64,1024]{1,0:T(8,128)(2,1)S(1)}, bf16[64,1024]{1,0:T(8,128)(2,1)S(1)}, u32[]{:S(2)}, u32[]{:S(2)}) %collective-permute-start.5) | collective-permute-done | bytes 131104 | tf_op jit(solution)/shard_map/ppermute | solution.py:357
  203.2 0.6 copy-done.5
  203.8 8.6 %unpool.3 = bf16[1024,256]{1,0:T(8,128)(2,1)} custom-call(bf16[64,1024]{1,0:T(8,128)(2,1)} %get-tuple-element.24.mid, f32[64,1024]{1,0:T(8,128)} %get-tuple-element.25.kept, bf16[128,1024]{1,0:T(8,128)(2,1)} %copy-done, bf16[64,1024]{1,0:T(8,128)(2,1)} %copy-done.5, bf16[16,8,192,512]{3,2,1,0:T(8,128)(2,1)} %bitcast.13, ...), custom_call_target="tpu_custom_call" | custom-call | tf_op jit(solution)/shard_map/unpool/pallas_call | solution.py:504
  (17 shorter events, 0.1 us)
Async XLA Ops:
  6.5 137.9 %all-gather.5.cloned.1.call-start = ((), (), s32[]{:S(2)}) async-start(), calls=%async_computation.3 | async-start | bytes 25362432 | tf_op jit(solution)/shard_map/all_gather | solution.py:431
  8.3 168.7 %all-gather.7.cloned.1.call-start = ((), (), s32[]{:S(2)}) async-start(), calls=%async_computation.4 | async-start | bytes 3342336 | tf_op jit(solution)/shard_map/all_gather | solution.py:441
  8.3 10.7 %collective-permute-start = (bf16[192,512]{1,0:T(8,128)(2,1)}, bf16[192,512]{1,0:T(8,128)(2,1)S(1)}, u32[]{:S(2)}, u32[]{:S(2)}) collective-permute-start(bf16[192,512]{1,0:T(8,128)(2,1)} %get-tuple-element.17), channel_id=1, source_target_pairs={{0,4},{4,0},{2,6},{6,2},{1,5},{5,1},{3,7},{7,3},{8,12},{12,8},{10,... | collective-permute-start | bytes 589832 | tf_op jit(solution)/shard_map/ppermute | solution.py:361
  19.1 0.7 copy-start.1
  156.4 4.0 %collective-permute-start.1 = (bf16[64,1024]{1,0:T(8,128)(2,1)}, bf16[64,1024]{1,0:T(8,128)(2,1)S(1)}, u32[]{:S(2)}, u32[]{:S(2)}) collective-permute-start(bf16[64,1024]{1,0:T(8,128)(2,1)} %get-tuple-element.22.own), channel_id=1, source_target_pairs={{0,2},{2,0},{4,6},{6,4},{1,3},{3,1},{5,7},{7,5},{8,10},{10,8},{12,... | collective-permute-start | bytes 393224 | tf_op jit(solution)/shard_map/ppermute | solution.py:357
  156.4 20.6 %collective-permute-start.2 = (bf16[64,1024]{1,0:T(8,128)(2,1)}, bf16[64,1024]{1,0:T(8,128)(2,1)S(1)}, u32[]{:S(2)}, u32[]{:S(2)}) collective-permute-start(bf16[64,1024]{1,0:T(8,128)(2,1)} %get-tuple-element.22.own), channel_id=1, source_target_pairs={{0,1},{1,0},{2,3},{3,2},{4,5},{5,4},{6,7},{7,6},{8,9},{9,8},{10,11... | collective-permute-start | bytes 393224 | tf_op jit(solution)/shard_map/ppermute | solution.py:353
  160.4 16.6 %copy-start.2 = (bf16[64,1024]{1,0:T(8,128)(2,1)}, bf16[64,1024]{1,0:T(8,128)(2,1)S(1)}, u32[]{:S(2)}) copy-start(bf16[64,1024]{1,0:T(8,128)(2,1)S(1)} %collective-permute-done.1.from_z) | copy-start | bytes 393220
  160.4 16.6 %collective-permute-start.3 = (bf16[64,1024]{1,0:T(8,128)(2,1)S(1)}, bf16[64,1024]{1,0:T(8,128)(2,1)S(1)}, u32[]{:S(2)}, u32[]{:S(2)}) collective-permute-start(bf16[64,1024]{1,0:T(8,128)(2,1)S(1)} %collective-permute-done.1.from_z), channel_id=1, source_target_pairs={{0,1},{1,0},{2,3},{3,2},{4,5},{5,4},{6,7},{7,6},{8,9},{9,8},{10,11... | collective-permute-start | bytes 393224 | tf_op jit(solution)/shard_map/ppermute | solution.py:353
  177.0 0.6 copy-start.3
  177.0 0.7 copy-start.4
  194.9 2.4 %collective-permute-start.4 = (bf16[128,1024]{1,0:T(8,128)(2,1)}, bf16[128,1024]{1,0:T(8,128)(2,1)S(1)}, u32[]{:S(2)}, u32[]{:S(2)}) collective-permute-start(bf16[128,1024]{1,0:T(8,128)(2,1)} %get-tuple-element.26), channel_id=1, source_target_pairs={{0,1},{1,0},{2,3},{3,2},{4,5},{5,4},{6,7},{7,6},{8,9},{9,8},{10,11... | collective-permute-start | bytes 786440 | tf_op jit(solution)/shard_map/ppermute | solution.py:353
  197.3 5.9 %copy-start = (bf16[128,1024]{1,0:T(8,128)(2,1)}, bf16[128,1024]{1,0:T(8,128)(2,1)S(1)}, u32[]{:S(2)}) copy-start(bf16[128,1024]{1,0:T(8,128)(2,1)S(1)} %collective-permute-done.4.got) | copy-start | bytes 786436
  198.4 4.8 %collective-permute-start.5 = (bf16[64,1024]{1,0:T(8,128)(2,1)S(1)}, bf16[64,1024]{1,0:T(8,128)(2,1)S(1)}, u32[]{:S(2)}, u32[]{:S(2)}) collective-permute-start(bf16[64,1024]{1,0:T(8,128)(2,1)S(1)} %add_convert_fusion), channel_id=1, source_target_pairs={{0,2},{2,0},{4,6},{6,4},{1,3},{3,1},{5,7},{7,5},{8,10},{10,8},{12,... | collective-permute-start | bytes 393224 | tf_op jit(solution)/shard_map/ppermute | solution.py:357
  203.2 0.6 copy-start.5
Sparse Core Ops, SparseCore 0:
  10.4 119.0 all-gather.4
  131.7 45.2 all-gather.6

commit v5 on v3

--- a/solution.py
+++ b/solution.py
@@ -199,7 +199,8 @@
     heads,
     own_gate_up,
     own_down,
-    far_gate_up,
+    far_gate,
+    far_up,
     far_down,
     mid,
     kept,
@@ -259,18 +260,17 @@
         normed[...] = rms(values.astype(F32), gains[1:2, :])
         total[...] = jnp.zeros_like(total)
 
-    def mlp(gate_up, down):
+    def hidden_of(gate, up):
         rows = normed[...]
-        hidden = (silu(mm(rows, gate_up[0])) * mm(rows, gate_up[1])).astype(BF16)
-        total[...] += mm(hidden, down[...])
+        return (silu(mm(rows, gate)) * mm(rows, up)).astype(BF16)
 
     @pl.when((step >= N_HID) & (step < N_HID + 2))
     def _():
-        mlp(own_gate_up, own_down)
+        total[...] += mm(hidden_of(own_gate_up[0], own_gate_up[1]), own_down[...])
 
     @pl.when(step >= N_HID + 2)
     def _():
-        mlp(far_gate_up, far_down)
+        total[...] += mm(hidden_of(far_gate[...], far_up[...]), far_down[...])
 
     @pl.when(step == N_HID + 3)
     def _():
@@ -322,10 +322,15 @@
     )
 
 
-def hidden_half(first, gate_up):
-    if gate_up:
-        return pl.BlockSpec((2, CC, 256), lambda i: (0, 0, jnp.clip(i - first, 0, 1)))
-    return pl.BlockSpec((256, CC), lambda i: (jnp.clip(i - first, 0, 1), 0))
+def hidden_half(first, kind):
+    def half(i):
+        return jnp.clip(i - first, 0, 1)
+
+    if kind == "both":
+        return pl.BlockSpec((2, CC, 256), lambda i: (0, 0, half(i)))
+    if kind == "in":
+        return pl.BlockSpec((CC, 256), lambda i: (0, half(i)))
+    return pl.BlockSpec((256, CC), lambda i: (half(i), 0))
 
 
 def exchange(values):
@@ -341,7 +346,7 @@
 
 
 def far_z(values):
-    return lax.ppermute(values, "z", [(0, 2), (2, 0), (1, 3), (3, 1)])
+    return lax.ppermute(values, "z", [(0, 3), (3, 0), (1, 2), (2, 1)])
 
 
 def fine(which, rows, place, slots, norm, qkv, out, gate_up, down):
@@ -408,19 +413,21 @@
         coarse_out,
     )
     weights = lax.all_gather(piece, ALL).reshape(N_BALL, N_HID, 192, 512)
-    far_gate_up = far_z(coarse_gate_up)
-    far_down = far_z(coarse_down)
 
     send, slots = pl.pallas_call(
         prep_kernel,
         out_shape=(shape((SLOTS, C + N_DEV), BF16), shape((2, PTS), I32)),
         compiler_params=params(),
+        cost_estimate=pl.CostEstimate(flops=6 * 10**9, bytes_accessed=2 * 2**20, transcendentals=0),
         name="prep",
     )(points, tree_slot.reshape(1, PTS), rotated_slot.reshape(1, PTS))
     first = exchange(send)
+    far_gate, first = lax.optimization_barrier((far_z(coarse_gate_up[0]), first))
     fine_weights = (fine_norm, fine_qkv, fine_out, fine_gate_up, fine_down)
     rows = exchange(fine(0, first, first, slots, *fine_weights))
+    far_up, rows = lax.optimization_barrier((far_z(coarse_gate_up[1]), rows))
     returned = exchange(fine(1, rows, first, slots, *fine_weights))
+    far_down, returned = lax.optimization_barrier((far_z(coarse_down), returned))
 
     block_two, coarse = pl.pallas_call(
         pool_kernel,
@@ -451,10 +458,11 @@
             rows_64,
             whole((2, CC)),
             unit(2),
-            hidden_half(N_HID, True),
-            hidden_half(N_HID, False),
-            hidden_half(N_HID + 2, True),
-            hidden_half(N_HID + 2, False),
+            hidden_half(N_HID, "both"),
+            hidden_half(N_HID, "out"),
+            hidden_half(N_HID + 2, "in"),
+            hidden_half(N_HID + 2, "in"),
+            hidden_half(N_HID + 2, "out"),
         ],
         out_specs=(rows_64, rows_64, rows_64, whole((2 * CROWS, CC))),
         scratch_shapes=[
@@ -473,7 +481,8 @@
         weights,
         coarse_gate_up,
         coarse_down,
-        far_gate_up,
+        far_gate,
+        far_up,
         far_down,
     )
 

time: 266 us -> 243 us (0.914)
  blocking collectives: 38 us -> 0 us
  starting transfers between devices: 19.7 us -> 33.7 us
    ppermute x2 -> x3, waiting for transfers between devices: 0.01 us -> 98.1 us  [far_z(): return lax.ppermute(values, 'z', [(0, 3), (3, 0), (1, 2), (2, 1)])]
    all_to_all x2 -> x3, waiting for transfers between devices: 75 us -> 2.44 us  [exchange(): return lax.all_to_all(values, ALL, split_axis=0, concat_axis=0, tiled=True)]
    all_to_all x1 -> x0, blocking collectives: 38 us -> none  [exchange(): return lax.all_to_all(values, ALL, split_axis=0, concat_axis=0, tiled=True)]
    all_gather x1, waiting for transfers between devices: 25.1 us -> 0.01 us  [body(): weights = lax.all_gather(piece, ALL).reshape(N_BALL, N_HID, 192, 512)]
    all_to_all x2 -> x3, starting transfers between devices: 10.7 us -> 24.5 us  [exchange(): return lax.all_to_all(values, ALL, split_axis=0, concat_axis=0, tiled=True)]
    ppermute x2 -> x3, starting transfers between devices: 7.18 us -> 6.81 us  [far_z(): return lax.ppermute(values, 'z', [(0, 3), (3, 0), (1, 2), (2, 1)])]
  transfers between devices with their start and end apart: 10 -> 12, of which waited for: 7 -> 9; matrix products, arithmetic and copies ran while one was open for 0% -> 0% of each run, Pallas kernels for 19% -> 16%
where the time goes in v5:
time: 243 us; the launch traced here: 242 us
  waiting for transfers between devices  112 us (46%)
  Pallas kernels  78.8 us (32%)
  starting transfers between devices  33.7 us (14%)
  between operations  13.5 us (6%)
  local copies, waits for them, and re-layouts  3.44 us (1%)
    ppermute x3, waiting for transfers between devices, far_z(): return lax.ppermute(values, 'z', [(0, 3), (3, 0), (1, 2), (2, 1)])  98.1 us
    pallas_call x2, Pallas kernels, fine(): pl.pallas_call(functools.partial(fine_kernel, which), grid=(1,), out_shap...  33.4 us
    all_to_all x3, starting transfers between devices, exchange(): return lax.all_to_all(values, ALL, split_axis=0, concat_axis=0, tiled=True)  24.5 us
    pallas_call x1, Pallas kernels, body(): pl.pallas_call(coarse_kernel, grid=(N_HID + 4,), out_shape=(shape((CROWS,...  17.1 us
    pallas_call x1, Pallas kernels, body(): pl.pallas_call(pool_kernel, grid=(N_HID,), out_shape=(shape((PTS, C), BF1...  12 us
    ppermute x2, waiting for transfers between devices, other_z(): return lax.ppermute(values, 'z', [(0, 1), (1, 0), (2, 3), (3, 2)])  8.95 us
    pallas_call x1, Pallas kernels, body(): pl.pallas_call(unpool_kernel, grid=(N_HID,), out_shape=shape((PTS, C), BF...  8.56 us
    ppermute x3, starting transfers between devices, far_z(): return lax.ppermute(values, 'z', [(0, 3), (3, 0), (1, 2), (2, 1)])  6.81 us
  transfers between devices with their start and end apart: 12, of which 9 were waited for; matrix products, arithmetic and copies ran while one was open for 0% of the time, Pallas kernels for 16%

profile of v5, /device:TPU:1, one launch (start us, length us, event | category | flops | bytes accessed | tf_op | source)
XLA Modules:
  0.0 242.4 jit_solution(6243133859521213632)
XLA Ops:
  6.5 1.6 cut.1
  8.1 6.2 %prep.1 = (bf16[2048,384]{1,0:T(8,128)(2,1)}, s32[2,1024]{1,0:T(2,128)}) custom-call(bf16[1024,256]{1,0:T(8,128)(2,1)} %points.1, s32[1,1024]{1,0:T(1,128)} %bitcast.21, s32[1,1024]{1,0:T(1,128)} %bitcast.22), custom_call_target="tpu_custom_call" | custom-call | flops 6000000000 | bytes 2097152 | tf_op jit(solution)/shard_map/prep/pallas_call | solution.py:417
  14.4 11.9 %all-to-all-start = ((bf16[128,16,384]{2,1,0:T(8,128)(2,1)}), bf16[128,16,384]{2,1,0:T(8,128)(2,1)}, u32[]{:S(2)}, u32[]{:S(2)}) async-start(bf16[128,16,384]{2,1,0:T(8,128)(2,1)} %bitcast.18), calls=%async_computation | async-start | bytes 3145728 | tf_op jit(solution)/shard_map/all_to_all | solution.py:337
  26.3 1.1 slice_bitcast_fusion
  27.4 3.3 %collective-permute-start.2 = (bf16[1024,512]{1,0:T(8,128)(2,1)S(1)}, bf16[1024,512]{1,0:T(8,128)(2,1)S(1)}, u32[]{:S(2)}, u32[]{:S(2)}) collective-permute-start(bf16[1024,512]{1,0:T(8,128)(2,1)S(1)} %get-tuple-element.33), channel_id=1, source_target_pairs={{0,6},{6,0},{2,4},{4,2},{1,7},{7,1},{3,5},{5,3},{8,14},{14,8},{10,... | collective-permute-start | bytes 3145736 | tf_op jit(solution)/shard_map/ppermute | solution.py:349
  30.7 48.8 %collective-permute-done.2.far_gate = bf16[1024,512]{1,0:T(8,128)(2,1)S(1)} collective-permute-done((bf16[1024,512]{1,0:T(8,128)(2,1)S(1)}, bf16[1024,512]{1,0:T(8,128)(2,1)S(1)}, u32[]{:S(2)}, u32[]{:S(2)}) %collective-permute-start.2) | collective-permute-done | bytes 1048608 | tf_op jit(solution)/shard_map/ppermute | solution.py:349
  79.5 16.8 %fine_block_0.1 = bf16[2048,256]{1,0:T(8,128)(2,1)} custom-call(bf16[2048,384]{1,0:T(8,128)(2,1)} %bitcast.5.rows.place, bf16[2048,384]{1,0:T(8,128)(2,1)} %bitcast.5.rows.place, s32[2,1024]{1,0:T(2,128)} %get-tuple-element.21.slots, f32[2,2,256]{2,1,0:T(2,128)} %gains.4, bf16[2,3,256,256]{3,2,1,0:T(8,128)(2,1)} %qkv.4, bf16[2,256,256]{2,1,0:T(8,128)(2,1)} %out.4, ...), custom_call_target="tpu_custom_call" | custom-call | flops 8000000000 | bytes 4194304 | tf_op jit(solution)/shard_map/fine_block_0/pallas_call | solution.py:353
  96.2 7.0 %all-to-all-start.1 = ((bf16[128,16,256]{2,1,0:T(8,128)(2,1)}), bf16[128,16,256]{2,1,0:T(8,128)(2,1)}, u32[]{:S(2)}, u32[]{:S(2)}) async-start(bf16[128,16,256]{2,1,0:T(8,128)(2,1)} %bitcast.19), calls=%async_computation.1 | async-start | bytes 2097152 | tf_op jit(solution)/shard_map/all_to_all | solution.py:337
  103.2 3.5 %collective-permute-start = (bf16[512,1024]{1,0:T(8,128)(2,1)S(1)}, bf16[512,1024]{1,0:T(8,128)(2,1)S(1)}, u32[]{:S(2)}, u32[]{:S(2)}) collective-permute-start(bf16[512,1024]{1,0:T(8,128)(2,1)S(1)} %copy-done.2), channel_id=1, source_target_pairs={{0,6},{6,0},{2,4},{4,2},{1,7},{7,1},{3,5},{5,3},{8,14},{14,8},{10,... | collective-permute-start | bytes 3145736 | tf_op jit(solution)/shard_map/ppermute | solution.py:349
  106.8 19.8 %collective-permute-done.1.far_up = bf16[1024,512]{1,0:T(8,128)(2,1)S(1)} collective-permute-done((bf16[1024,512]{1,0:T(8,128)(2,1)}, bf16[1024,512]{1,0:T(8,128)(2,1)S(1)}, u32[]{:S(2)}, u32[]{:S(2)}) %collective-permute-start.1) | collective-permute-done | bytes 1048608 | tf_op jit(solution)/shard_map/ppermute | solution.py:349
  126.5 1.9 all-to-all-done.1
  128.4 16.6 %fine_block_1.1 = bf16[2048,256]{1,0:T(8,128)(2,1)} custom-call(bf16[2048,256]{1,0:T(8,128)(2,1)} %bitcast.7.rows, bf16[2048,384]{1,0:T(8,128)(2,1)} %bitcast.5.rows.place, s32[2,1024]{1,0:T(2,128)} %get-tuple-element.21.slots, f32[2,2,256]{2,1,0:T(2,128)} %gains.4, bf16[2,3,256,256]{3,2,1,0:T(8,128)(2,1)} %qkv.4, bf16[2,256,256]{2,1,0:T(8,128)(2,1)} %out.4, ...), custom_call_target="tpu_custom_call" | custom-call | flops 8000000000 | bytes 4194304 | tf_op jit(solution)/shard_map/fine_block_1/pallas_call | solution.py:353
  145.0 5.6 %all-to-all-start.2 = ((bf16[128,16,256]{2,1,0:T(8,128)(2,1)}), bf16[128,16,256]{2,1,0:T(8,128)(2,1)S(1)}, u32[]{:S(2)}, u32[]{:S(2)}) async-start(bf16[128,16,256]{2,1,0:T(8,128)(2,1)} %bitcast.20), calls=%async_computation.2 | async-start | bytes 2097152 | tf_op jit(solution)/shard_map/all_to_all | solution.py:337
  150.7 29.6 %collective-permute-done.far_down = bf16[512,1024]{1,0:T(8,128)(2,1)S(1)} collective-permute-done((bf16[512,1024]{1,0:T(8,128)(2,1)S(1)}, bf16[512,1024]{1,0:T(8,128)(2,1)S(1)}, u32[]{:S(2)}, u32[]{:S(2)}) %collective-permute-start) | collective-permute-done | bytes 1048608 | tf_op jit(solution)/shard_map/ppermute | solution.py:349
  180.8 1.0 copy-done.1
  181.8 12.0 %pool.3 = (bf16[1024,256]{1,0:T(8,128)(2,1)}, bf16[64,1024]{1,0:T(8,128)(2,1)}) custom-call(bf16[2048,256]{1,0:T(8,128)(2,1)} %bitcast.17, s32[2,1024]{1,0:T(2,128)} %get-tuple-element.21.slots, bf16[16,8,192,512]{3,2,1,0:T(8,128)(2,1)} %bitcast.14), custom_call_target="tpu_custom_call" | custom-call | tf_op jit(solution)/shard_map/pool/pallas_call | solution.py:432
  194.4 4.2 %collective-permute-done.3.from_z = bf16[64,1024]{1,0:T(8,128)(2,1)S(1)} collective-permute-done((bf16[64,1024]{1,0:T(8,128)(2,1)}, bf16[64,1024]{1,0:T(8,128)(2,1)S(1)}, u32[]{:S(2)}, u32[]{:S(2)}) %collective-permute-start.3) | collective-permute-done | bytes 131104 | tf_op jit(solution)/shard_map/ppermute | solution.py:345
  198.6 1.3 collective-permute-start.5
  199.9 1.0 collective-permute-done.5.pair_z
  201.6 17.1 %coarse.1 = (bf16[64,1024]{1,0:T(8,128)(2,1)}, f32[64,1024]{1,0:T(8,128)}, f32[64,1024]{1,0:T(8,128)}, bf16[128,1024]{1,0:T(8,128)(2,1)}) custom-call(bf16[64,1024]{1,0:T(8,128)(2,1)} %get-tuple-element.24.own, bf16[64,1024]{1,0:T(8,128)(2,1)} %copy-done.7, bf16[64,1024]{1,0:T(8,128)(2,1)} %copy-done.8, bf16[64,1024]{1,0:T(8,128)(2,1)} %copy-done.9, ...), custom_call_target="tpu_custom_call" | custom-call | tf_op jit(solution)/shard_map/coarse/pallas_call | solution.py:445
  219.1 1.4 collective-permute-done.6.got
  220.5 1.1 add_convert_fusion
  221.7 4.7 %collective-permute-done.7.got_z = bf16[64,1024]{1,0:T(8,128)(2,1)S(1)} collective-permute-done((bf16[64,1024]{1,0:T(8,128)(2,1)S(1)}, bf16[64,1024]{1,0:T(8,128)(2,1)S(1)}, u32[]{:S(2)}, u32[]{:S(2)}) %collective-permute-start.7) | collective-permute-done | bytes 131104 | tf_op jit(solution)/shard_map/ppermute | solution.py:345
  227.0 8.6 %unpool.3 = bf16[1024,256]{1,0:T(8,128)(2,1)} custom-call(bf16[64,1024]{1,0:T(8,128)(2,1)} %get-tuple-element.28.mid, f32[64,1024]{1,0:T(8,128)} %get-tuple-element.29.kept, bf16[128,1024]{1,0:T(8,128)(2,1)} %copy-done.6, bf16[64,1024]{1,0:T(8,128)(2,1)} %copy-done.10, bf16[16,8,192,512]{3,2,1,0:T(8,128)(2,1)} %bitcast.16, ...), custom_call_target="tpu_custom_call" | custom-call | tf_op jit(solution)/shard_map/unpool/pallas_call | solution.py:491
  (32 shorter events, 3.1 us)
Async XLA Ops:
  6.5 174.3 %all-gather.3.cloned.1.call-start = ((), (), s32[]{:S(2)}) async-start(), calls=%async_computation.3 | async-start | bytes 25362432 | tf_op jit(solution)/shard_map/all_gather | solution.py:415
  14.4 11.9 %copy-start = (bf16[2,1024,512]{2,1,0:T(8,128)(2,1)S(1)}, bf16[2,1024,512]{2,1,0:T(8,128)(2,1)}, u32[]{:S(2)}) copy-start(bf16[2,1024,512]{2,1,0:T(8,128)(2,1)} %own_gate_up.1) | copy-start | bytes 6291460
  14.4 65.1 %all-to-all-start = ((bf16[128,16,384]{2,1,0:T(8,128)(2,1)}), bf16[128,16,384]{2,1,0:T(8,128)(2,1)}, u32[]{:S(2)}, u32[]{:S(2)}) async-start(bf16[128,16,384]{2,1,0:T(8,128)(2,1)} %bitcast.18), calls=%async_computation | async-start | bytes 3145728 | tf_op jit(solution)/shard_map/all_to_all | solution.py:337
  27.4 52.1 %collective-permute-start.2 = (bf16[1024,512]{1,0:T(8,128)(2,1)S(1)}, bf16[1024,512]{1,0:T(8,128)(2,1)S(1)}, u32[]{:S(2)}, u32[]{:S(2)}) collective-permute-start(bf16[1024,512]{1,0:T(8,128)(2,1)S(1)} %get-tuple-element.33), channel_id=1, source_target_pairs={{0,6},{6,0},{2,4},{4,2},{1,7},{7,1},{3,5},{5,3},{8,14},{14,8},{10,... | collective-permute-start | bytes 3145736 | tf_op jit(solution)/shard_map/ppermute | solution.py:349
  30.7 95.9 %collective-permute-start.1 = (bf16[1024,512]{1,0:T(8,128)(2,1)}, bf16[1024,512]{1,0:T(8,128)(2,1)S(1)}, u32[]{:S(2)}, u32[]{:S(2)}) collective-permute-start(bf16[1024,512]{1,0:T(8,128)(2,1)} %get-tuple-element.34), channel_id=1, source_target_pairs={{0,6},{6,0},{2,4},{4,2},{1,7},{7,1},{3,5},{5,3},{8,14},{14,8},{10,... | collective-permute-start | bytes 3145736 | tf_op jit(solution)/shard_map/ppermute | solution.py:349
  79.5 16.8 %copy-start.3 = (bf16[1024,512]{1,0:T(8,128)(2,1)}, bf16[1024,512]{1,0:T(8,128)(2,1)S(1)}, u32[]{:S(2)}) copy-start(bf16[1024,512]{1,0:T(8,128)(2,1)S(1)} %collective-permute-done.2.far_gate) | copy-start | bytes 3145732
  96.2 7.0 %copy-start.2 = (bf16[512,1024]{1,0:T(8,128)(2,1)S(1)}, bf16[512,1024]{1,0:T(8,128)(2,1)}, u32[]{:S(2)}) copy-start(bf16[512,1024]{1,0:T(8,128)(2,1)} %own_down.1) | copy-start | bytes 3145732
  96.2 32.2 %all-to-all-start.1 = ((bf16[128,16,256]{2,1,0:T(8,128)(2,1)}), bf16[128,16,256]{2,1,0:T(8,128)(2,1)}, u32[]{:S(2)}, u32[]{:S(2)}) async-start(bf16[128,16,256]{2,1,0:T(8,128)(2,1)} %bitcast.19), calls=%async_computation.1 | async-start | bytes 2097152 | tf_op jit(solution)/shard_map/all_to_all | solution.py:337
  103.2 77.0 %collective-permute-start = (bf16[512,1024]{1,0:T(8,128)(2,1)S(1)}, bf16[512,1024]{1,0:T(8,128)(2,1)S(1)}, u32[]{:S(2)}, u32[]{:S(2)}) collective-permute-start(bf16[512,1024]{1,0:T(8,128)(2,1)S(1)} %copy-done.2), channel_id=1, source_target_pairs={{0,6},{6,0},{2,4},{4,2},{1,7},{7,1},{3,5},{5,3},{8,14},{14,8},{10,... | collective-permute-start | bytes 3145736 | tf_op jit(solution)/shard_map/ppermute | solution.py:349
  126.5 18.5 %copy-start.4 = (bf16[1024,512]{1,0:T(8,128)(2,1)}, bf16[1024,512]{1,0:T(8,128)(2,1)S(1)}, u32[]{:S(2)}) copy-start(bf16[1024,512]{1,0:T(8,128)(2,1)S(1)} %collective-permute-done.1.far_up) | copy-start | bytes 3145732
  145.0 35.8 %all-to-all-start.2 = ((bf16[128,16,256]{2,1,0:T(8,128)(2,1)}), bf16[128,16,256]{2,1,0:T(8,128)(2,1)S(1)}, u32[]{:S(2)}, u32[]{:S(2)}) async-start(bf16[128,16,256]{2,1,0:T(8,128)(2,1)} %bitcast.20), calls=%async_computation.2 | async-start | bytes 2097152 | tf_op jit(solution)/shard_map/all_to_all | solution.py:337
  180.2 13.5 %copy-start.5 = (bf16[512,1024]{1,0:T(8,128)(2,1)}, bf16[512,1024]{1,0:T(8,128)(2,1)S(1)}, u32[]{:S(2)}) copy-start(bf16[512,1024]{1,0:T(8,128)(2,1)S(1)} %collective-permute-done.far_down) | copy-start | bytes 3145732
  180.8 1.0 copy-start.1
  193.7 4.9 %collective-permute-start.3 = (bf16[64,1024]{1,0:T(8,128)(2,1)}, bf16[64,1024]{1,0:T(8,128)(2,1)S(1)}, u32[]{:S(2)}, u32[]{:S(2)}) collective-permute-start(bf16[64,1024]{1,0:T(8,128)(2,1)} %get-tuple-element.24.own), channel_id=1, source_target_pairs={{0,2},{2,0},{4,6},{6,4},{1,3},{3,1},{5,7},{7,5},{8,10},{10,8},{12,... | collective-permute-start | bytes 393224 | tf_op jit(solution)/shard_map/ppermute | solution.py:345
  193.8 6.1 %collective-permute-start.4 = (bf16[64,1024]{1,0:T(8,128)(2,1)}, bf16[64,1024]{1,0:T(8,128)(2,1)S(1)}, u32[]{:S(2)}, u32[]{:S(2)}) collective-permute-start(bf16[64,1024]{1,0:T(8,128)(2,1)} %get-tuple-element.24.own), channel_id=1, source_target_pairs={{0,1},{1,0},{2,3},{3,2},{4,5},{5,4},{6,7},{7,6},{8,9},{9,8},{10,11... | collective-permute-start | bytes 393224 | tf_op jit(solution)/shard_map/ppermute | solution.py:341
  198.6 2.3 copy-start.7
  198.6 2.3 collective-permute-start.5
  199.9 1.0 copy-start.8
  200.9 0.7 copy-start.9
  218.7 1.8 collective-permute-start.6
  220.5 5.9 %copy-start.6 = (bf16[128,1024]{1,0:T(8,128)(2,1)}, bf16[128,1024]{1,0:T(8,128)(2,1)S(1)}, u32[]{:S(2)}) copy-start(bf16[128,1024]{1,0:T(8,128)(2,1)S(1)} %collective-permute-done.6.got) | copy-start | bytes 786436
  221.6 4.8 %collective-permute-start.7 = (bf16[64,1024]{1,0:T(8,128)(2,1)S(1)}, bf16[64,1024]{1,0:T(8,128)(2,1)S(1)}, u32[]{:S(2)}, u32[]{:S(2)}) collective-permute-start(bf16[64,1024]{1,0:T(8,128)(2,1)S(1)} %add_convert_fusion), channel_id=1, source_target_pairs={{0,2},{2,0},{4,6},{6,4},{1,3},{3,1},{5,7},{7,5},{8,10},{10,8},{12,... | collective-permute-start | bytes 393224 | tf_op jit(solution)/shard_map/ppermute | solution.py:345
  226.4 0.7 copy-start.10
Sparse Core Ops, SparseCore 0:
  10.4 169.8 all-gather.2

commit v6 on v4

--- a/solution.py
+++ b/solution.py
@@ -194,91 +194,76 @@
         coarse[...] = total[...].astype(BF16)
 
 
-def coarse_kernel(
-    own,
-    from_z,
-    pair,
-    pair_z,
-    gains,
-    heads,
-    own_gate_up,
-    own_down,
-    far_gate,
-    far_up,
-    far_down,
-    mid,
-    kept,
-    kept_z,
-    sent,
-    normed,
-    total,
-    out,
-):
+def attn_kernel(own, from_z, pair, pair_z, gains, heads, mid, normed, rows_16, total, out):
     step = pl.program_id(0)
-    sources = (own, from_z, pair, pair_z)
 
     @pl.when(step == 0)
     def _():
-        for at, ref in enumerate(sources):
+        for at, ref in enumerate((own, from_z, pair, pair_z)):
             values = ref[...].astype(F32)
-            normed[CROWS * at : CROWS * at + CROWS, :] = rms(values, gains[0:1, :])
+            rows_16[CROWS * at : CROWS * at + CROWS, :] = rms(values, gains[0:1, :])
             total[CROWS * at : CROWS * at + CROWS, :] = values
 
-    @pl.when(step < N_HID)
-    def _():
-        def weight(which):
-            rows = slice(16 * which, 16 * which + 16)
-            return jnp.stack(
-                [heads[:, 0, rows, 128 * part : 128 * part + 128] for part in range(4)], axis=1
-            ).reshape(CC, 128)
-
-        for ball in range(N_BALL):
-            lanes = slice(128 * (ball % 8), 128 * (ball % 8) + 128)
-            for part in range(4):
-                top = 64 * (ball // 8) + 16 * part
-                out[top : top + 16, lanes] = heads[ball, 0, 48:64, 128 * part : 128 * part + 128]
-
-        rows = normed[...]
-        q = mm(rows, weight(0)).astype(BF16)
-        k = mm(rows, weight(1)).astype(BF16)
-        v = mm(rows, weight(2)).astype(BF16)
-        head_of = iota((BALL, 128), 1) // 64
-        scale = LOG2E / math.sqrt(64)
-        mixed = jnp.zeros((BALL, 128), F32)
-        inverse = jnp.zeros((BALL, 128), F32)
-        zero = jnp.zeros((BALL, 128), BF16)
-        for head in range(2):
-            mine = head_of == head
-            scores = mm_nt(q, jnp.where(mine, k, zero))
-            top = jnp.max(scores, axis=-1, keepdims=True)
-            weights = jnp.exp2((scores - top) * scale)
-            sums = jnp.sum(weights, axis=-1, keepdims=True)
-            mixed = mixed + mm(weights.astype(BF16), jnp.where(mine, v, zero))
-            inverse = jnp.where(mine, 1.0 / sums, inverse)
-        total[...] += mm((mixed * inverse).astype(BF16), out[...])
-
-    @pl.when(step == N_HID)
+    def weight(which):
+        rows = slice(16 * which, 16 * which + 16)
+        return jnp.stack(
+            [heads[:, 0, rows, 128 * part : 128 * part + 128] for part in range(4)], axis=1
+        ).reshape(CC, 128)
+
+    for ball in range(N_BALL):
+        lanes = slice(128 * (ball % 8), 128 * (ball % 8) + 128)
+        for part in range(4):
+            top = 64 * (ball // 8) + 16 * part
+            out[top : top + 16, lanes] = heads[ball, 0, 48:64, 128 * part : 128 * part + 128]
+
+    rows = rows_16[...]
+    q = mm(rows, weight(0)).astype(BF16)
+    k = mm(rows, weight(1)).astype(BF16)
+    v = mm(rows, weight(2)).astype(BF16)
+    head_of = iota((BALL, 128), 1) // 64
+    scale = LOG2E / math.sqrt(64)
+    mixed = jnp.zeros((BALL, 128), F32)
+    inverse = jnp.zeros((BALL, 128), F32)
+    zero = jnp.zeros((BALL, 128), BF16)
+    for head in range(2):
+        mine = head_of == head
+        scores = mm_nt(q, jnp.where(mine, k, zero))
+        top = jnp.max(scores, axis=-1, keepdims=True)
+        weights = jnp.exp2((scores - top) * scale)
+        sums = jnp.sum(weights, axis=-1, keepdims=True)
+        mixed = mixed + mm(weights.astype(BF16), jnp.where(mine, v, zero))
+        inverse = jnp.where(mine, 1.0 / sums, inverse)
+    total[...] += mm((mixed * inverse).astype(BF16), out[...])
+
+    @pl.when(step == N_HID - 1)
     def _():
         values = total[...].astype(BF16)
         mid[...] = values[:CROWS]
         normed[...] = rms(values.astype(F32), gains[1:2, :])
-        total[...] = jnp.zeros_like(total)
+
+
+def mlp_kernel(normed, own_gate_up, own_down, far_gate, far_up, far_down, kept, kept_z, sent, total):
+    step = pl.program_id(0)
 
     def hidden_of(gate, up):
         rows = normed[...]
         return (silu(mm(rows, gate)) * mm(rows, up)).astype(BF16)
 
-    @pl.when((step >= N_HID) & (step < N_HID + 2))
+    @pl.when(step == 0)
+    def _():
+        total[...] = jnp.zeros_like(total)
+
+    @pl.when(step < 2)
     def _():
         total[...] += mm(hidden_of(own_gate_up[0], own_gate_up[1]), own_down[...])
 
-    @pl.when(step >= N_HID + 2)
+    @pl.when(step >= 2)
     def _():
         hidden = hidden_of(far_gate[...].reshape(CC, 256), far_up[...].reshape(CC, 256))
         total[:, :512] += mm(hidden, far_down[:, :32, :].reshape(256, 512))
         total[:, 512:] += mm(hidden, far_down[:, 32:, :].reshape(256, 512))
 
-    @pl.when(step == N_HID + 3)
+    @pl.when(step == 3)
     def _():
         kept[...] = total[:CROWS, :]
         kept_z[...] = total[CROWS : 2 * CROWS, :]
@@ -358,7 +343,7 @@
 
 
 def far_z(values):
-    return lax.ppermute(values, "z", [(0, 2), (2, 0), (1, 3), (3, 1)])
+    return lax.ppermute(values, "z", [(0, 3), (3, 0), (1, 2), (2, 1)])
 
 
 def fine(which, rows, place, slots, norm, qkv, out, gate_up, down):
@@ -457,47 +442,40 @@
 
     from_z = other_z(coarse)
     rows_64 = whole((CROWS, CC))
-    mid, kept, kept_z, sent = pl.pallas_call(
-        coarse_kernel,
-        grid=(N_HID + 4,),
+    mid, normed = pl.pallas_call(
+        attn_kernel,
+        grid=(N_HID,),
+        out_shape=(shape((CROWS, CC), BF16), shape((4 * CROWS, CC), BF16)),
+        in_specs=[rows_64, rows_64, rows_64, rows_64, whole((2, CC)), unit(2)],
+        out_specs=(rows_64, whole((4 * CROWS, CC))),
+        scratch_shapes=[
+            pltpu.VMEM((4 * CROWS, CC), BF16),
+            pltpu.VMEM((4 * CROWS, CC), F32),
+            pltpu.VMEM((128, CC), BF16),
+        ],
+        compiler_params=params(),
+        name="attn",
+    )(coarse, from_z, other_core(coarse), other_core(from_z), coarse_norm, weights)
+
+    kept, kept_z, sent = pl.pallas_call(
+        mlp_kernel,
+        grid=(4,),
         out_shape=(
-            shape((CROWS, CC), BF16),
             shape((CROWS, CC), F32),
             shape((CROWS, CC), F32),
             shape((2 * CROWS, CC), BF16),
         ),
         in_specs=[
-            rows_64,
-            rows_64,
-            rows_64,
-            rows_64,
-            whole((2, CC)),
-            unit(2),
-            hidden_half(N_HID, True),
-            hidden_half(N_HID, False),
-            *far_halves(N_HID + 2),
+            whole((4 * CROWS, CC)),
+            hidden_half(0, True),
+            hidden_half(0, False),
+            *far_halves(2),
         ],
-        out_specs=(rows_64, rows_64, rows_64, whole((2 * CROWS, CC))),
-        scratch_shapes=[
-            pltpu.VMEM((4 * CROWS, CC), BF16),
-            pltpu.VMEM((4 * CROWS, CC), F32),
-            pltpu.VMEM((128, CC), BF16),
-        ],
-        compiler_params=params(),
-        name="coarse",
-    )(
-        coarse,
-        from_z,
-        other_core(coarse),
-        other_core(from_z),
-        coarse_norm,
-        weights,
-        coarse_gate_up,
-        coarse_down,
-        far_mlp,
-        far_mlp,
-        far_mlp,
-    )
+        out_specs=(rows_64, rows_64, whole((2 * CROWS, CC))),
+        scratch_shapes=[pltpu.VMEM((4 * CROWS, CC), F32)],
+        compiler_params=params(),
+        name="mlp",
+    )(normed, coarse_gate_up, coarse_down, far_mlp, far_mlp, far_mlp)
 
     got = other_core(sent)
     got_z = other_z((kept_z + got[CROWS:].astype(F32)).astype(BF16))

time: 220 us -> 208 us (0.945)
  waiting for transfers between devices: 21.8 us -> 8.44 us
    all_gather x1, waiting for transfers between devices: 14.2 us -> 0.01 us  [body(): far_mlp = lax.all_gather(far_piece, 'ball')]
    pallas_call x1 -> x2, Pallas kernels: 17.2 us -> 18.5 us  [the longest x1 11.9 us: body(): pl.pallas_call(attn_kernel, grid=(N_HID,), out_shape=(shape((CROWS, CC),...]
  transfers between devices with their start and end apart: 8 -> 8, of which waited for: 4 -> 4; matrix products, arithmetic and copies ran while one was open for 0% -> 0% of each run, Pallas kernels for 23% -> 30%
where the time goes in v6:
time: 208 us; the launch traced here: 207 us
  blocking collectives  92.1 us (44%)
  Pallas kernels  79.9 us (38%)
  between operations  13.4 us (6%)
  starting transfers between devices  10.5 us (5%)
  waiting for transfers between devices  8.44 us (4%)
    all_to_all x3, blocking collectives, exchange(): return lax.all_to_all(values, ALL, split_axis=0, concat_axis=0, tiled=True)  92.1 us
    pallas_call x2, Pallas kernels, fine(): pl.pallas_call(functools.partial(fine_kernel, which), grid=(1,), out_shap...  32.9 us
    pallas_call x1, Pallas kernels, body(): pl.pallas_call(pool_kernel, grid=(N_HID,), out_shape=(shape((PTS, C), BF1...  12 us
    pallas_call x1, Pallas kernels, body(): pl.pallas_call(attn_kernel, grid=(N_HID,), out_shape=(shape((CROWS, CC),...  11.9 us
    pallas_call x1, Pallas kernels, body(): pl.pallas_call(unpool_kernel, grid=(N_HID,), out_shape=shape((PTS, C), BF...  8.56 us
    pallas_call x1, Pallas kernels, body(): pl.pallas_call(mlp_kernel, grid=(4,), out_shape=(shape((CROWS, CC), F32),...  6.58 us
    pallas_call x1, Pallas kernels, body(): pl.pallas_call(prep_kernel, out_shape=(shape((SLOTS, C + N_DEV), BF16), s...  6.22 us
    ppermute x2, waiting for transfers between devices, other_z(): return lax.ppermute(values, 'z', [(0, 1), (1, 0), (2, 3), (3, 2)])  6.04 us
  transfers between devices with their start and end apart: 8, of which 4 were waited for; matrix products, arithmetic and copies ran while one was open for 0% of the time, Pallas kernels for 30%

profile of v6, /device:TPU:1, one launch (start us, length us, event | category | flops | bytes accessed | tf_op | source)
XLA Modules:
  0.0 207.5 jit_solution(10062980487684881462)
XLA Ops:
  6.5 1.7 cut.1
  8.3 4.7 %collective-permute-start = (bf16[192,512]{1,0:T(8,128)(2,1)}, bf16[192,512]{1,0:T(8,128)(2,1)S(1)}, u32[]{:S(2)}, u32[]{:S(2)}) collective-permute-start(bf16[192,512]{1,0:T(8,128)(2,1)} %get-tuple-element.18), channel_id=1, source_target_pairs={{0,6},{6,0},{2,4},{4,2},{1,7},{7,1},{3,5},{5,3},{8,14},{14,8},{10,... | collective-permute-start | bytes 589832 | tf_op jit(solution)/shard_map/ppermute | solution.py:346
  13.0 6.2 %prep.1 = (bf16[2048,384]{1,0:T(8,128)(2,1)}, s32[2,1024]{1,0:T(2,128)}) custom-call(bf16[1024,256]{1,0:T(8,128)(2,1)} %points.1, s32[1,1024]{1,0:T(1,128)} %bitcast.25, s32[1,1024]{1,0:T(1,128)} %bitcast.26), custom_call_target="tpu_custom_call" | custom-call | flops 6000000000 | bytes 2097152 | tf_op jit(solution)/shard_map/prep/pallas_call | solution.py:418
  19.2 0.7 copy-done.1
  20.0 34.4 %all_to_all.33 = bf16[128,16,384]{2,1,0:T(8,128)(2,1)} all-to-all(bf16[128,16,384]{2,1,0:T(8,128)(2,1)} %bitcast.18), channel_id=1, replica_groups=mesh['ball'=16,'z'=4,'core'=2] {'ball','z','core'}, dimensions={0} | all-to-all | bytes 3145728 | tf_op jit(solution)/shard_map/all_to_all | solution.py:334
  54.3 16.3 %fine_block_0.1 = bf16[2048,256]{1,0:T(8,128)(2,1)} custom-call(bf16[2048,384]{1,0:T(8,128)(2,1)} %bitcast.19, bf16[2048,384]{1,0:T(8,128)(2,1)} %bitcast.20, s32[2,1024]{1,0:T(2,128)} %get-tuple-element.21.slots, f32[2,2,256]{2,1,0:T(2,128)} %gains.4, bf16[2,3,256,256]{3,2,1,0:T(8,128)(2,1)} %qkv.5, bf16[2,256,256]{2,1,0:T(8,128)(2,1)} %out.5, ...), custom_call_target="tpu_custom_call" | custom-call | flops 8000000000 | bytes 4194304 | tf_op jit(solution)/shard_map/fine_block_0/pallas_call | solution.py:350
  70.7 31.5 %all_to_all.34 = bf16[128,16,256]{2,1,0:T(8,128)(2,1)} all-to-all(bf16[128,16,256]{2,1,0:T(8,128)(2,1)} %bitcast.24), channel_id=1, replica_groups=mesh['ball'=16,'z'=4,'core'=2] {'ball','z','core'}, dimensions={0} | all-to-all | bytes 2097152 | tf_op jit(solution)/shard_map/all_to_all | solution.py:334
  102.1 16.6 %fine_block_1.1 = bf16[2048,256]{1,0:T(8,128)(2,1)} custom-call(bf16[2048,256]{1,0:T(8,128)(2,1)} %bitcast.22, bf16[2048,384]{1,0:T(8,128)(2,1)} %bitcast.21, s32[2,1024]{1,0:T(2,128)} %get-tuple-element.21.slots, f32[2,2,256]{2,1,0:T(2,128)} %gains.4, bf16[2,3,256,256]{3,2,1,0:T(8,128)(2,1)} %qkv.5, bf16[2,256,256]{2,1,0:T(8,128)(2,1)} %out.5, ...), custom_call_target="tpu_custom_call" | custom-call | flops 8000000000 | bytes 4194304 | tf_op jit(solution)/shard_map/fine_block_1/pallas_call | solution.py:350
  118.7 26.2 %all_to_all.35 = bf16[128,16,256]{2,1,0:T(8,128)(2,1)} all-to-all(bf16[128,16,256]{2,1,0:T(8,128)(2,1)} %bitcast.23), channel_id=1, replica_groups=mesh['ball'=16,'z'=4,'core'=2] {'ball','z','core'}, dimensions={0} | all-to-all | bytes 2097152 | tf_op jit(solution)/shard_map/all_to_all | solution.py:334
  145.0 12.0 %pool.3 = (bf16[1024,256]{1,0:T(8,128)(2,1)}, bf16[64,1024]{1,0:T(8,128)(2,1)}) custom-call(bf16[2048,256]{1,0:T(8,128)(2,1)} %bitcast.17, s32[2,1024]{1,0:T(2,128)} %get-tuple-element.21.slots, bf16[16,8,192,512]{3,2,1,0:T(8,128)(2,1)} %bitcast.11), custom_call_target="tpu_custom_call" | custom-call | tf_op jit(solution)/shard_map/pool/pallas_call | solution.py:432
  157.0 1.4 collective-permute-start.2
  158.4 2.6 %collective-permute-done.1.from_z = bf16[64,1024]{1,0:T(8,128)(2,1)S(1)} collective-permute-done((bf16[64,1024]{1,0:T(8,128)(2,1)}, bf16[64,1024]{1,0:T(8,128)(2,1)S(1)}, u32[]{:S(2)}, u32[]{:S(2)}) %collective-permute-start.1) | collective-permute-done | bytes 131104 | tf_op jit(solution)/shard_map/ppermute | solution.py:342
  161.0 2.3 %collective-permute-start.3 = (bf16[64,1024]{1,0:T(8,128)(2,1)S(1)}, bf16[64,1024]{1,0:T(8,128)(2,1)S(1)}, u32[]{:S(2)}, u32[]{:S(2)}) collective-permute-start(bf16[64,1024]{1,0:T(8,128)(2,1)S(1)} %collective-permute-done.1.from_z), channel_id=1, source_target_pairs={{0,1},{1,0},{2,3},{3,2},{4,5},{5,4},{6,7},{7,6},{8,9},{9,8},{10,11... | collective-permute-start | bytes 393224 | tf_op jit(solution)/shard_map/ppermute | solution.py:338
  163.3 1.0 collective-permute-done.3.pair_z
  164.3 0.6 copy-done.5
  164.9 11.9 %attn.1 = (bf16[64,1024]{1,0:T(8,128)(2,1)}, bf16[256,1024]{1,0:T(8,128)(2,1)}) custom-call(bf16[64,1024]{1,0:T(8,128)(2,1)} %get-tuple-element.23.own, bf16[64,1024]{1,0:T(8,128)(2,1)} %copy-done.2, bf16[64,1024]{1,0:T(8,128)(2,1)} %copy-done.3, bf16[64,1024]{1,0:T(8,128)(2,1)} %copy-done.5, f32[2,1024]{1,0:T(2,128)} %gains.5, ...), custom_call_target="tpu_custom_call" | custom-call | tf_op jit(solution)/shard_map/attn/pallas_call | solution.py:445
  176.9 6.6 %mlp.1 = (f32[64,1024]{1,0:T(8,128)}, f32[64,1024]{1,0:T(8,128)}, bf16[128,1024]{1,0:T(8,128)(2,1)}) custom-call(bf16[256,1024]{1,0:T(8,128)(2,1)} %get-tuple-element.25.normed, bf16[2,1024,512]{2,1,0:T(8,128)(2,1)} %own_gate_up.1, bf16[512,1024]{1,0:T(8,128)(2,1)} %own_down.1, bf16[16,192,512]{2,1,0:T(8,128)(2,1)} %bitcast.14, ...), custom_call_target="tpu_custom_call" | custom-call | tf_op jit(solution)/shard_map/mlp/pallas_call | solution.py:460
  183.4 0.8 collective-permute-start.4
  184.2 1.4 collective-permute-done.4.got
  185.6 1.1 add_convert_fusion
  186.7 1.4 collective-permute-start.5
  188.0 3.4 %collective-permute-done.5.got_z = bf16[64,1024]{1,0:T(8,128)(2,1)S(1)} collective-permute-done((bf16[64,1024]{1,0:T(8,128)(2,1)S(1)}, bf16[64,1024]{1,0:T(8,128)(2,1)S(1)}, u32[]{:S(2)}, u32[]{:S(2)}) %collective-permute-start.5) | collective-permute-done | bytes 131104 | tf_op jit(solution)/shard_map/ppermute | solution.py:342
  191.5 0.6 copy-done.4
  192.1 8.6 %unpool.3 = bf16[1024,256]{1,0:T(8,128)(2,1)} custom-call(bf16[64,1024]{1,0:T(8,128)(2,1)} %get-tuple-element.24.mid, f32[64,1024]{1,0:T(8,128)} %get-tuple-element.27.kept, bf16[128,1024]{1,0:T(8,128)(2,1)} %copy-done, bf16[64,1024]{1,0:T(8,128)(2,1)} %copy-done.4, bf16[16,8,192,512]{3,2,1,0:T(8,128)(2,1)} %bitcast.13, ...), custom_call_target="tpu_custom_call" | custom-call | tf_op jit(solution)/shard_map/unpool/pallas_call | solution.py:482
  (18 shorter events, 0.1 us)
Async XLA Ops:
  6.5 138.4 %all-gather.5.cloned.1.call-start = ((), (), s32[]{:S(2)}) async-start(), calls=%async_computation.3 | async-start | bytes 25362432 | tf_op jit(solution)/shard_map/all_gather | solution.py:416
  8.3 168.6 %all-gather.7.cloned.1.call-start = ((), (), s32[]{:S(2)}) async-start(), calls=%async_computation.4 | async-start | bytes 3342336 | tf_op jit(solution)/shard_map/all_gather | solution.py:426
  8.3 10.9 %collective-permute-start = (bf16[192,512]{1,0:T(8,128)(2,1)}, bf16[192,512]{1,0:T(8,128)(2,1)S(1)}, u32[]{:S(2)}, u32[]{:S(2)}) collective-permute-start(bf16[192,512]{1,0:T(8,128)(2,1)} %get-tuple-element.18), channel_id=1, source_target_pairs={{0,6},{6,0},{2,4},{4,2},{1,7},{7,1},{3,5},{5,3},{8,14},{14,8},{10,... | collective-permute-start | bytes 589832 | tf_op jit(solution)/shard_map/ppermute | solution.py:346
  19.2 0.7 copy-start.1
  157.0 4.0 %collective-permute-start.1 = (bf16[64,1024]{1,0:T(8,128)(2,1)}, bf16[64,1024]{1,0:T(8,128)(2,1)S(1)}, u32[]{:S(2)}, u32[]{:S(2)}) collective-permute-start(bf16[64,1024]{1,0:T(8,128)(2,1)} %get-tuple-element.23.own), channel_id=1, source_target_pairs={{0,2},{2,0},{4,6},{6,4},{1,3},{3,1},{5,7},{7,5},{8,10},{10,8},{12,... | collective-permute-start | bytes 393224 | tf_op jit(solution)/shard_map/ppermute | solution.py:342
  157.0 6.3 %collective-permute-start.2 = (bf16[64,1024]{1,0:T(8,128)(2,1)}, bf16[64,1024]{1,0:T(8,128)(2,1)S(1)}, u32[]{:S(2)}, u32[]{:S(2)}) collective-permute-start(bf16[64,1024]{1,0:T(8,128)(2,1)} %get-tuple-element.23.own), channel_id=1, source_target_pairs={{0,1},{1,0},{2,3},{3,2},{4,5},{5,4},{6,7},{7,6},{8,9},{9,8},{10,11... | collective-permute-start | bytes 393224 | tf_op jit(solution)/shard_map/ppermute | solution.py:338
  161.0 3.3 %copy-start.2 = (bf16[64,1024]{1,0:T(8,128)(2,1)}, bf16[64,1024]{1,0:T(8,128)(2,1)S(1)}, u32[]{:S(2)}) copy-start(bf16[64,1024]{1,0:T(8,128)(2,1)S(1)} %collective-permute-done.1.from_z) | copy-start | bytes 393220
  161.0 3.3 %collective-permute-start.3 = (bf16[64,1024]{1,0:T(8,128)(2,1)S(1)}, bf16[64,1024]{1,0:T(8,128)(2,1)S(1)}, u32[]{:S(2)}, u32[]{:S(2)}) collective-permute-start(bf16[64,1024]{1,0:T(8,128)(2,1)S(1)} %collective-permute-done.1.from_z), channel_id=1, source_target_pairs={{0,1},{1,0},{2,3},{3,2},{4,5},{5,4},{6,7},{7,6},{8,9},{9,8},{10,11... | collective-permute-start | bytes 393224 | tf_op jit(solution)/shard_map/ppermute | solution.py:338
  163.3 1.0 copy-start.3
  164.3 0.6 copy-start.5
  183.4 2.1 %collective-permute-start.4 = (bf16[128,1024]{1,0:T(8,128)(2,1)}, bf16[128,1024]{1,0:T(8,128)(2,1)S(1)}, u32[]{:S(2)}, u32[]{:S(2)}) collective-permute-start(bf16[128,1024]{1,0:T(8,128)(2,1)} %get-tuple-element.28), channel_id=1, source_target_pairs={{0,1},{1,0},{2,3},{3,2},{4,5},{5,4},{6,7},{7,6},{8,9},{9,8},{10,11... | collective-permute-start | bytes 786440 | tf_op jit(solution)/shard_map/ppermute | solution.py:338
  185.6 5.9 %copy-start = (bf16[128,1024]{1,0:T(8,128)(2,1)}, bf16[128,1024]{1,0:T(8,128)(2,1)S(1)}, u32[]{:S(2)}) copy-start(bf16[128,1024]{1,0:T(8,128)(2,1)S(1)} %collective-permute-done.4.got) | copy-start | bytes 786436
  186.7 4.8 %collective-permute-start.5 = (bf16[64,1024]{1,0:T(8,128)(2,1)S(1)}, bf16[64,1024]{1,0:T(8,128)(2,1)S(1)}, u32[]{:S(2)}, u32[]{:S(2)}) collective-permute-start(bf16[64,1024]{1,0:T(8,128)(2,1)S(1)} %add_convert_fusion), channel_id=1, source_target_pairs={{0,2},{2,0},{4,6},{6,4},{1,3},{3,1},{5,7},{7,5},{8,10},{10,8},{12,... | collective-permute-start | bytes 393224 | tf_op jit(solution)/shard_map/ppermute | solution.py:342
  191.4 0.7 copy-start.4
Sparse Core Ops, SparseCore 0:
  10.4 118.7 all-gather.4
  131.4 45.2 all-gather.6

commit v7 on v4

--- a/solution.py
+++ b/solution.py
@@ -152,7 +152,7 @@
         states[pl.ds(start, BALL), :] = fine_ball(x, gains, qkv, out, gate_up, down)
         return carry
 
-    lax.fori_loop(0, PTS // BALL, one_ball, 0)
+    lax.fori_loop(0, PTS // BALL, one_ball, 0, unroll=True)
 
     if which == 0:
         pack(slots[1:2, :], states, send)
@@ -194,34 +194,14 @@
         coarse[...] = total[...].astype(BF16)
 
 
-def coarse_kernel(
-    own,
-    from_z,
-    pair,
-    pair_z,
-    gains,
-    heads,
-    own_gate_up,
-    own_down,
-    far_gate,
-    far_up,
-    far_down,
-    mid,
-    kept,
-    kept_z,
-    sent,
-    normed,
-    total,
-    out,
-):
+def attn_kernel(own, from_z, pair, pair_z, gains, heads, gate_up, down, mid, normed, partial, rows_16, total, out):
     step = pl.program_id(0)
-    sources = (own, from_z, pair, pair_z)
 
     @pl.when(step == 0)
     def _():
-        for at, ref in enumerate(sources):
+        for at, ref in enumerate((own, from_z, pair, pair_z)):
             values = ref[...].astype(F32)
-            normed[CROWS * at : CROWS * at + CROWS, :] = rms(values, gains[0:1, :])
+            rows_16[CROWS * at : CROWS * at + CROWS, :] = rms(values, gains[0:1, :])
             total[CROWS * at : CROWS * at + CROWS, :] = values
 
     @pl.when(step < N_HID)
@@ -238,7 +218,7 @@
                 top = 64 * (ball // 8) + 16 * part
                 out[top : top + 16, lanes] = heads[ball, 0, 48:64, 128 * part : 128 * part + 128]
 
-        rows = normed[...]
+        rows = rows_16[...]
         q = mm(rows, weight(0)).astype(BF16)
         k = mm(rows, weight(1)).astype(BF16)
         v = mm(rows, weight(2)).astype(BF16)
@@ -262,23 +242,29 @@
         values = total[...].astype(BF16)
         mid[...] = values[:CROWS]
         normed[...] = rms(values.astype(F32), gains[1:2, :])
-        total[...] = jnp.zeros_like(total)
-
-    def hidden_of(gate, up):
-        rows = normed[...]
-        return (silu(mm(rows, gate)) * mm(rows, up)).astype(BF16)
-
-    @pl.when((step >= N_HID) & (step < N_HID + 2))
-    def _():
-        total[...] += mm(hidden_of(own_gate_up[0], own_gate_up[1]), own_down[...])
-
-    @pl.when(step >= N_HID + 2)
-    def _():
-        hidden = hidden_of(far_gate[...].reshape(CC, 256), far_up[...].reshape(CC, 256))
-        total[:, :512] += mm(hidden, far_down[:, :32, :].reshape(256, 512))
-        total[:, 512:] += mm(hidden, far_down[:, 32:, :].reshape(256, 512))
-
-    @pl.when(step == N_HID + 3)
+        partial[...] = jnp.zeros_like(partial)
+
+    @pl.when(step >= N_HID)
+    def _():
+        partial[...] += mm(hidden_of(normed[...], gate_up[0], gate_up[1]), down[...])
+
+
+def hidden_of(rows, gate, up):
+    return (silu(mm(rows, gate)) * mm(rows, up)).astype(BF16)
+
+
+def mlp_kernel(normed, partial, gate, up, down, kept, kept_z, sent, total):
+    step = pl.program_id(0)
+
+    @pl.when(step == 0)
+    def _():
+        total[...] = partial[...]
+
+    hidden = hidden_of(normed[...], gate[...].reshape(CC, 256), up[...].reshape(CC, 256))
+    total[:, :512] += mm(hidden, down[:, :32, :].reshape(256, 512))
+    total[:, 512:] += mm(hidden, down[:, 32:, :].reshape(256, 512))
+
+    @pl.when(step == 1)
     def _():
         kept[...] = total[:CROWS, :]
         kept_z[...] = total[CROWS : 2 * CROWS, :]
@@ -358,7 +344,7 @@
 
 
 def far_z(values):
-    return lax.ppermute(values, "z", [(0, 2), (2, 0), (1, 3), (3, 1)])
+    return lax.ppermute(values, "z", [(0, 3), (3, 0), (1, 2), (2, 1)])
 
 
 def fine(which, rows, place, slots, norm, qkv, out, gate_up, down):
@@ -437,12 +423,14 @@
         cost_estimate=pl.CostEstimate(flops=6 * 10**9, bytes_accessed=2 * 2**20, transcendentals=0),
         name="prep",
     )(points, tree_slot.reshape(1, PTS), rotated_slot.reshape(1, PTS))
-    far_piece, send = lax.optimization_barrier((far_z(mlp_piece), send))
-    far_mlp = lax.all_gather(far_piece, "ball")
     first = exchange(send)
     fine_weights = (fine_norm, fine_qkv, fine_out, fine_gate_up, fine_down)
     rows = exchange(fine(0, first, first, slots, *fine_weights))
-    returned = exchange(fine(1, rows, first, slots, *fine_weights))
+    mlp_piece, rows = lax.optimization_barrier((mlp_piece, rows))
+    answers = fine(1, rows, first, slots, *fine_weights)
+    far_piece, answers = lax.optimization_barrier((far_z(mlp_piece), answers))
+    far_mlp = lax.all_gather(far_piece, "ball")
+    returned = exchange(answers)
 
     block_two, coarse = pl.pallas_call(
         pool_kernel,
@@ -457,14 +445,14 @@
 
     from_z = other_z(coarse)
     rows_64 = whole((CROWS, CC))
-    mid, kept, kept_z, sent = pl.pallas_call(
-        coarse_kernel,
-        grid=(N_HID + 4,),
+    rows_256 = whole((4 * CROWS, CC))
+    mid, normed, partial = pl.pallas_call(
+        attn_kernel,
+        grid=(N_HID + 2,),
         out_shape=(
             shape((CROWS, CC), BF16),
-            shape((CROWS, CC), F32),
-            shape((CROWS, CC), F32),
-            shape((2 * CROWS, CC), BF16),
+            shape((4 * CROWS, CC), BF16),
+            shape((4 * CROWS, CC), F32),
         ),
         in_specs=[
             rows_64,
@@ -475,16 +463,15 @@
             unit(2),
             hidden_half(N_HID, True),
             hidden_half(N_HID, False),
-            *far_halves(N_HID + 2),
         ],
-        out_specs=(rows_64, rows_64, rows_64, whole((2 * CROWS, CC))),
+        out_specs=(rows_64, rows_256, rows_256),
         scratch_shapes=[
             pltpu.VMEM((4 * CROWS, CC), BF16),
             pltpu.VMEM((4 * CROWS, CC), F32),
             pltpu.VMEM((128, CC), BF16),
         ],
         compiler_params=params(),
-        name="coarse",
+        name="attn",
     )(
         coarse,
         from_z,
@@ -494,10 +481,22 @@
         weights,
         coarse_gate_up,
         coarse_down,
-        far_mlp,
-        far_mlp,
-        far_mlp,
     )
+
+    kept, kept_z, sent = pl.pallas_call(
+        mlp_kernel,
+        grid=(2,),
+        out_shape=(
+            shape((CROWS, CC), F32),
+            shape((CROWS, CC), F32),
+            shape((2 * CROWS, CC), BF16),
+        ),
+        in_specs=[rows_256, rows_256, *far_halves(0)],
+        out_specs=(rows_64, rows_64, whole((2 * CROWS, CC))),
+        scratch_shapes=[pltpu.VMEM((4 * CROWS, CC), F32)],
+        compiler_params=params(),
+        name="mlp",
+    )(normed, partial, far_mlp, far_mlp, far_mlp)
 
     got = other_core(sent)
     got_z = other_z((kept_z + got[CROWS:].astype(F32)).astype(BF16))

time: 220 us -> 217 us (0.986)
  starting transfers between devices: 10.6 us -> 4.29 us
  waiting for transfers between devices: 21.8 us -> 25.1 us
  blocking collectives: 91.6 us -> 94 us
  Pallas kernels: 78.8 us -> 76.6 us
    ppermute x1, starting transfers between devices: 4.51 us -> 0.01 us  [far_z(): return lax.ppermute(values, 'z', [(0, 3), (3, 0), (1, 2), (2, 1)])]
    pallas_call x2, Pallas kernels: 33 us -> 29.1 us  [fine(): pl.pallas_call(functools.partial(fine_kernel, which), grid=(1,), out_shap...]
    all_to_all x3, blocking collectives: 91.6 us -> 94 us  [exchange(): return lax.all_to_all(values, ALL, split_axis=0, concat_axis=0, tiled=True)]
    all_gather x1, waiting for transfers between devices: 0.01 us -> 2.44 us  [body(): weights = lax.all_gather(piece, ALL).reshape(N_BALL, N_HID, 192, 512)]
    ppermute x3, starting transfers between devices: 4.67 us -> 2.46 us  [other_core(): return lax.ppermute(values, 'core', [(0, 1), (1, 0)])]
    pallas_call x1 -> x2, Pallas kernels: 17.2 us -> 19 us  [the longest x1 14.7 us: body(): pl.pallas_call(attn_kernel, grid=(N_HID + 2,), out_shape=(shape((CROWS, C...]
  transfers between devices with their start and end apart: 8 -> 8, of which waited for: 4 -> 6; matrix products, arithmetic and copies ran while one was open for 0% -> 0% of each run, Pallas kernels for 23% -> 29%
where the time goes in v7:
time: 217 us
  blocking collectives  94 us (43%)
  Pallas kernels  76.6 us (35%)
  waiting for transfers between devices  25.1 us (12%)
  between operations  13.4 us (6%)
  starting transfers between devices  4.29 us (2%)
    all_to_all x3, blocking collectives, exchange(): return lax.all_to_all(values, ALL, split_axis=0, concat_axis=0, tiled=True)  94 us
    pallas_call x2, Pallas kernels, fine(): pl.pallas_call(functools.partial(fine_kernel, which), grid=(1,), out_shap...  29.1 us
    pallas_call x1, Pallas kernels, body(): pl.pallas_call(attn_kernel, grid=(N_HID + 2,), out_shape=(shape((CROWS, C...  14.7 us
    all_gather x1, waiting for transfers between devices, body(): far_mlp = lax.all_gather(far_piece, 'ball')  12.6 us
    pallas_call x1, Pallas kernels, body(): pl.pallas_call(pool_kernel, grid=(N_HID,), out_shape=(shape((PTS, C), BF1...  12 us
    pallas_call x1, Pallas kernels, body(): pl.pallas_call(unpool_kernel, grid=(N_HID,), out_shape=shape((PTS, C), BF...  8.56 us
    ppermute x2, waiting for transfers between devices, other_z(): return lax.ppermute(values, 'z', [(0, 1), (1, 0), (2, 3), (3, 2)])  7.65 us
    pallas_call x1, Pallas kernels, body(): pl.pallas_call(prep_kernel, out_shape=(shape((SLOTS, C + N_DEV), BF16), s...  6.24 us
  transfers between devices with their start and end apart: 8, of which 6 were waited for; matrix products, arithmetic and copies ran while one was open for 0% of the time, Pallas kernels for 29%

profile of v7, /device:TPU:1, one launch (start us, length us, event | category | flops | bytes accessed | tf_op | source)
XLA Modules:
  0.0 216.5 jit_solution(3820838434360477615)
XLA Ops:
  6.5 1.7 cut.1
  8.3 6.2 %prep.1 = (bf16[2048,384]{1,0:T(8,128)(2,1)}, s32[2,1024]{1,0:T(2,128)}) custom-call(bf16[1024,256]{1,0:T(8,128)(2,1)} %points.1, s32[1,1024]{1,0:T(1,128)} %bitcast.25, s32[1,1024]{1,0:T(1,128)} %bitcast.26), custom_call_target="tpu_custom_call" | custom-call | flops 6000000000 | bytes 2097152 | tf_op jit(solution)/shard_map/prep/pallas_call | solution.py:419
  14.6 38.0 %all_to_all.34 = bf16[128,16,384]{2,1,0:T(8,128)(2,1)} all-to-all(bf16[128,16,384]{2,1,0:T(8,128)(2,1)} %bitcast.21), channel_id=1, replica_groups=mesh['ball'=16,'z'=4,'core'=2] {'ball','z','core'}, dimensions={0} | all-to-all | bytes 3145728 | tf_op jit(solution)/shard_map/all_to_all | solution.py:335
  52.6 14.5 %fine_block_0.1 = bf16[2048,256]{1,0:T(8,128)(2,1)} custom-call(bf16[2048,384]{1,0:T(8,128)(2,1)} %bitcast.18, bf16[2048,384]{1,0:T(8,128)(2,1)} %bitcast.19, s32[2,1024]{1,0:T(2,128)} %get-tuple-element.23.slots, f32[2,2,256]{2,1,0:T(2,128)} %gains.4, bf16[2,3,256,256]{3,2,1,0:T(8,128)(2,1)} %qkv.5, bf16[2,256,256]{2,1,0:T(8,128)(2,1)} %out.5, ...), custom_call_target="tpu_custom_call" | custom-call | flops 8000000000 | bytes 4194304 | tf_op jit(solution)/shard_map/fine_block_0/pallas_call | solution.py:351
  67.1 29.7 %all_to_all.35 = bf16[128,16,256]{2,1,0:T(8,128)(2,1)} all-to-all(bf16[128,16,256]{2,1,0:T(8,128)(2,1)} %bitcast.24), channel_id=1, replica_groups=mesh['ball'=16,'z'=4,'core'=2] {'ball','z','core'}, dimensions={0} | all-to-all | bytes 2097152 | tf_op jit(solution)/shard_map/all_to_all | solution.py:335
  96.7 14.6 %fine_block_1.1 = bf16[2048,256]{1,0:T(8,128)(2,1)} custom-call(bf16[2048,256]{1,0:T(8,128)(2,1)} %bitcast.23, bf16[2048,384]{1,0:T(8,128)(2,1)} %bitcast.20, s32[2,1024]{1,0:T(2,128)} %get-tuple-element.23.slots, f32[2,2,256]{2,1,0:T(2,128)} %gains.4, bf16[2,3,256,256]{3,2,1,0:T(8,128)(2,1)} %qkv.5, bf16[2,256,256]{2,1,0:T(8,128)(2,1)} %out.5, ...), custom_call_target="tpu_custom_call" | custom-call | flops 8000000000 | bytes 4194304 | tf_op jit(solution)/shard_map/fine_block_1/pallas_call | solution.py:351
  111.4 0.7 copy-done.1
  112.1 26.4 %all_to_all.36 = bf16[128,16,256]{2,1,0:T(8,128)(2,1)} all-to-all(bf16[128,16,256]{2,1,0:T(8,128)(2,1)} %bitcast.22), channel_id=1, replica_groups=mesh['ball'=16,'z'=4,'core'=2] {'ball','z','core'}, dimensions={0} | all-to-all | bytes 2097152 | tf_op jit(solution)/shard_map/all_to_all | solution.py:335
  138.4 2.4 %all-gather.5.cloned.1.call-done = bf16[24576,512]{1,0:T(8,128)(2,1)} async-done(((bf16[192,512]{1,0:T(8,128)(2,1)}), bf16[24576,512]{1,0:T(8,128)(2,1)}) %all-gather.5.cloned.1.call-update) | async-done | bytes 25165840 | tf_op jit(solution)/shard_map/all_gather | solution.py:417
  140.9 12.0 %pool.3 = (bf16[1024,256]{1,0:T(8,128)(2,1)}, bf16[64,1024]{1,0:T(8,128)(2,1)}) custom-call(bf16[2048,256]{1,0:T(8,128)(2,1)} %bitcast.17, s32[2,1024]{1,0:T(2,128)} %get-tuple-element.23.slots, bf16[16,8,192,512]{3,2,1,0:T(8,128)(2,1)} %bitcast.11), custom_call_target="tpu_custom_call" | custom-call | tf_op jit(solution)/shard_map/pool/pallas_call | solution.py:435
  153.8 4.3 %collective-permute-done.1.from_z = bf16[64,1024]{1,0:T(8,128)(2,1)S(1)} collective-permute-done((bf16[64,1024]{1,0:T(8,128)(2,1)}, bf16[64,1024]{1,0:T(8,128)(2,1)S(1)}, u32[]{:S(2)}, u32[]{:S(2)}) %collective-permute-start.1) | collective-permute-done | bytes 131104 | tf_op jit(solution)/shard_map/ppermute | solution.py:343
  158.1 1.0 collective-permute-start.3
  159.0 1.0 collective-permute-done.3.pair_z
  160.0 0.7 copy-done.4
  160.7 14.7 %attn.1 = (bf16[64,1024]{1,0:T(8,128)(2,1)}, bf16[256,1024]{1,0:T(8,128)(2,1)}, f32[256,1024]{1,0:T(8,128)}) custom-call(bf16[64,1024]{1,0:T(8,128)(2,1)} %get-tuple-element.28.own, bf16[64,1024]{1,0:T(8,128)(2,1)} %copy-done.2, bf16[64,1024]{1,0:T(8,128)(2,1)} %copy-done.3, bf16[64,1024]{1,0:T(8,128)(2,1)} %copy-done.4, f32[2,1024]{1,0:T(2,128)} %gains.5, ...), custom_call_target="tpu_custom_call" | custom-call | tf_op jit(solution)/shard_map/attn/pallas_call | solution.py:449
  175.3 12.6 %all-gather.7.cloned.1.call-done = bf16[3072,512]{1,0:T(8,128)(2,1)} async-done(((bf16[192,512]{1,0:T(8,128)(2,1)}), bf16[3072,512]{1,0:T(8,128)(2,1)}) %all-gather.7.cloned.1.call-update) | async-done | bytes 3145744 | tf_op jit(solution)/shard_map/all_gather | solution.py:432
  188.0 4.3 %mlp.1 = (f32[64,1024]{1,0:T(8,128)}, f32[64,1024]{1,0:T(8,128)}, bf16[128,1024]{1,0:T(8,128)(2,1)}) custom-call(bf16[256,1024]{1,0:T(8,128)(2,1)} %get-tuple-element.30.normed, f32[256,1024]{1,0:T(8,128)} %get-tuple-element.31.partial, bf16[16,192,512]{2,1,0:T(8,128)(2,1)} %bitcast.14, bf16[16,192,512]{2,1,0:T(8,128)(2,1)} %bitcast.15, ...), custom_call_target="tpu_custom_call" | custom-call | tf_op jit(solution)/shard_map/mlp/pallas_call | solution.py:486
  192.2 1.0 collective-permute-start.4
  193.2 1.4 collective-permute-done.4.got
  194.6 1.1 add_convert_fusion
  195.7 1.4 collective-permute-start.5
  197.1 3.4 %collective-permute-done.5.got_z = bf16[64,1024]{1,0:T(8,128)(2,1)S(1)} collective-permute-done((bf16[64,1024]{1,0:T(8,128)(2,1)S(1)}, bf16[64,1024]{1,0:T(8,128)(2,1)S(1)}, u32[]{:S(2)}, u32[]{:S(2)}) %collective-permute-start.5) | collective-permute-done | bytes 131104 | tf_op jit(solution)/shard_map/ppermute | solution.py:343
  200.5 0.6 copy-done.5
  201.1 8.6 %unpool.3 = bf16[1024,256]{1,0:T(8,128)(2,1)} custom-call(bf16[64,1024]{1,0:T(8,128)(2,1)} %get-tuple-element.29.mid, f32[64,1024]{1,0:T(8,128)} %get-tuple-element.33.kept, bf16[128,1024]{1,0:T(8,128)(2,1)} %copy-done, bf16[64,1024]{1,0:T(8,128)(2,1)} %copy-done.5, bf16[16,8,192,512]{3,2,1,0:T(8,128)(2,1)} %bitcast.13, ...), custom_call_target="tpu_custom_call" | custom-call | tf_op jit(solution)/shard_map/unpool/pallas_call | solution.py:503
  (20 shorter events, 1.0 us)
Async XLA Ops:
  6.5 134.3 %all-gather.5.cloned.1.call-start = ((), (), s32[]{:S(2)}) async-start(), calls=%async_computation.3 | async-start | bytes 25362432 | tf_op jit(solution)/shard_map/all_gather | solution.py:417
  8.3 179.7 %all-gather.7.cloned.1.call-start = ((), (), s32[]{:S(2)}) async-start(), calls=%async_computation.4 | async-start | bytes 3342336 | tf_op jit(solution)/shard_map/all_gather | solution.py:432
  67.1 29.7 %copy-start.6 = (bf16[192,512]{1,0:T(8,128)(2,1)S(1)}, bf16[192,512]{1,0:T(8,128)(2,1)}, u32[]{:S(2)}) copy-start(bf16[192,512]{1,0:T(8,128)(2,1)} %get-tuple-element.24) | copy-start | bytes 589828
  96.7 14.6 %collective-permute-start = (bf16[192,512]{1,0:T(8,128)(2,1)S(1)}, bf16[192,512]{1,0:T(8,128)(2,1)S(1)}, u32[]{:S(2)}, u32[]{:S(2)}) collective-permute-start(bf16[192,512]{1,0:T(8,128)(2,1)S(1)} %copy-done.6), channel_id=1, source_target_pairs={{0,6},{6,0},{2,4},{4,2},{1,7},{7,1},{3,5},{5,3},{8,14},{14,8},{10,... | collective-permute-start | bytes 589832 | tf_op jit(solution)/shard_map/ppermute | solution.py:347
  111.4 0.7 copy-start.1
  152.9 5.2 %collective-permute-start.1 = (bf16[64,1024]{1,0:T(8,128)(2,1)}, bf16[64,1024]{1,0:T(8,128)(2,1)S(1)}, u32[]{:S(2)}, u32[]{:S(2)}) collective-permute-start(bf16[64,1024]{1,0:T(8,128)(2,1)} %get-tuple-element.28.own), channel_id=1, source_target_pairs={{0,2},{2,0},{4,6},{6,4},{1,3},{3,1},{5,7},{7,5},{8,10},{10,8},{12,... | collective-permute-start | bytes 393224 | tf_op jit(solution)/shard_map/ppermute | solution.py:343
  153.3 5.7 %collective-permute-start.2 = (bf16[64,1024]{1,0:T(8,128)(2,1)}, bf16[64,1024]{1,0:T(8,128)(2,1)S(1)}, u32[]{:S(2)}, u32[]{:S(2)}) collective-permute-start(bf16[64,1024]{1,0:T(8,128)(2,1)} %get-tuple-element.28.own), channel_id=1, source_target_pairs={{0,1},{1,0},{2,3},{3,2},{4,5},{5,4},{6,7},{7,6},{8,9},{9,8},{10,11... | collective-permute-start | bytes 393224 | tf_op jit(solution)/shard_map/ppermute | solution.py:339
  158.1 1.9 copy-start.2
  158.1 1.9 collective-permute-start.3
  159.0 1.0 copy-start.3
  160.0 0.7 copy-start.4
  192.2 2.4 %collective-permute-start.4 = (bf16[128,1024]{1,0:T(8,128)(2,1)}, bf16[128,1024]{1,0:T(8,128)(2,1)S(1)}, u32[]{:S(2)}, u32[]{:S(2)}) collective-permute-start(bf16[128,1024]{1,0:T(8,128)(2,1)} %get-tuple-element.34), channel_id=1, source_target_pairs={{0,1},{1,0},{2,3},{3,2},{4,5},{5,4},{6,7},{7,6},{8,9},{9,8},{10,11... | collective-permute-start | bytes 786440 | tf_op jit(solution)/shard_map/ppermute | solution.py:339
  194.6 5.9 %copy-start = (bf16[128,1024]{1,0:T(8,128)(2,1)}, bf16[128,1024]{1,0:T(8,128)(2,1)S(1)}, u32[]{:S(2)}) copy-start(bf16[128,1024]{1,0:T(8,128)(2,1)S(1)} %collective-permute-done.4.got) | copy-start | bytes 786436
  195.7 4.8 %collective-permute-start.5 = (bf16[64,1024]{1,0:T(8,128)(2,1)S(1)}, bf16[64,1024]{1,0:T(8,128)(2,1)S(1)}, u32[]{:S(2)}, u32[]{:S(2)}) collective-permute-start(bf16[64,1024]{1,0:T(8,128)(2,1)S(1)} %add_convert_fusion), channel_id=1, source_target_pairs={{0,2},{2,0},{4,6},{6,4},{1,3},{3,1},{5,7},{7,5},{8,10},{10,8},{12,... | collective-permute-start | bytes 393224 | tf_op jit(solution)/shard_map/ppermute | solution.py:343
  200.5 0.6 copy-start.5
Sparse Core Ops, SparseCore 0:
  10.4 130.4 all-gather.4
  143.1 44.8 all-gather.6

commit v8 on v7

--- a/solution.py
+++ b/solution.py
@@ -27,6 +27,7 @@
 N_BALL = 16
 N_Z = 4
 N_HID = 8
+STEPS = 4
 EPS = 1e-06
 LOG2E = 1.4426950408889634
 ALL = ("ball", "z", "core")
@@ -171,13 +172,14 @@
     low = (slot & 31).astype(F32)
     row = iota((8, PTS), 0)
     digits = jnp.where(row == 0, high, jnp.where(row == 1, low, 0.0)).astype(BF16)
-    child = iota((128, PTS), 0)
-    order = onehot(iota((128, PTS), 1) == POOL * (child & 63) + 2 * step + (child >> 6))
+    child = iota((256, PTS), 0)
+    order = onehot(iota((256, PTS), 1) == POOL * (child & 63) + 4 * step + (child >> 6))
     found = mm_nt(order, digits)
     at = (found[:, 0:1] * 32.0 + found[:, 1:2]).astype(I32)
-    pick = onehot(iota((128, SLOTS), 1) == at)
+    pick = onehot(iota((256, SLOTS), 1) == at)
     two = mm(pick, returned[...]).astype(BF16)
     block_two[...] = two
+    grouped = jnp.concatenate([two[64 * at : 64 * at + 64] for at in range(4)], axis=1)
 
     @pl.when(step == 0)
     def _():
@@ -186,10 +188,11 @@
     for half in range(2):
         rows = slice(32 * half, 32 * half + 32)
         lanes = slice(512 * half, 512 * half + 512)
-        weight = pool[:, 0, rows, :].reshape(512, 512)
-        total[:, lanes] += mm(two[:CROWS], weight[:C]) + mm(two[CROWS:], weight[C:])
-
-    @pl.when(step == N_HID - 1)
+        total[:, lanes] += mm(grouped[:, :512], pool[:, 0, rows, :].reshape(512, 512)) + mm(
+            grouped[:, 512:], pool[:, 1, rows, :].reshape(512, 512)
+        )
+
+    @pl.when(step == STEPS - 1)
     def _():
         coarse[...] = total[...].astype(BF16)
 
@@ -204,30 +207,40 @@
             rows_16[CROWS * at : CROWS * at + CROWS, :] = rms(values, gains[0:1, :])
             total[CROWS * at : CROWS * at + CROWS, :] = values
 
-    @pl.when(step < N_HID)
+    @pl.when(step < STEPS)
     def _():
         def weight(which):
             rows = slice(16 * which, 16 * which + 16)
-            return jnp.stack(
-                [heads[:, 0, rows, 128 * part : 128 * part + 128] for part in range(4)], axis=1
-            ).reshape(CC, 128)
-
-        for ball in range(N_BALL):
-            lanes = slice(128 * (ball % 8), 128 * (ball % 8) + 128)
-            for part in range(4):
-                top = 64 * (ball // 8) + 16 * part
-                out[top : top + 16, lanes] = heads[ball, 0, 48:64, 128 * part : 128 * part + 128]
+            return jnp.concatenate(
+                [
+                    jnp.stack(
+                        [heads[:, at, rows, 128 * part : 128 * part + 128] for part in range(4)],
+                        axis=1,
+                    ).reshape(CC, 128)
+                    for at in range(2)
+                ],
+                axis=1,
+            )
+
+        for at in range(2):
+            for ball in range(N_BALL):
+                lanes = slice(128 * (ball % 8), 128 * (ball % 8) + 128)
+                for part in range(4):
+                    top = 128 * at + 64 * (ball // 8) + 16 * part
+                    out[top : top + 16, lanes] = heads[
+                        ball, at, 48:64, 128 * part : 128 * part + 128
+                    ]
 
         rows = rows_16[...]
         q = mm(rows, weight(0)).astype(BF16)
         k = mm(rows, weight(1)).astype(BF16)
         v = mm(rows, weight(2)).astype(BF16)
-        head_of = iota((BALL, 128), 1) // 64
+        head_of = iota((BALL, 256), 1) // 64
         scale = LOG2E / math.sqrt(64)
-        mixed = jnp.zeros((BALL, 128), F32)
-        inverse = jnp.zeros((BALL, 128), F32)
-        zero = jnp.zeros((BALL, 128), BF16)
-        for head in range(2):
+        mixed = jnp.zeros((BALL, 256), F32)
+        inverse = jnp.zeros((BALL, 256), F32)
+        zero = jnp.zeros((BALL, 256), BF16)
+        for head in range(4):
             mine = head_of == head
             scores = mm_nt(q, jnp.where(mine, k, zero))
             top = jnp.max(scores, axis=-1, keepdims=True)
@@ -237,14 +250,14 @@
             inverse = jnp.where(mine, 1.0 / sums, inverse)
         total[...] += mm((mixed * inverse).astype(BF16), out[...])
 
-    @pl.when(step == N_HID)
+    @pl.when(step == STEPS)
     def _():
         values = total[...].astype(BF16)
         mid[...] = values[:CROWS]
         normed[...] = rms(values.astype(F32), gains[1:2, :])
         partial[...] = jnp.zeros_like(partial)
 
-    @pl.when(step >= N_HID)
+    @pl.when(step >= STEPS)
     def _():
         partial[...] += mm(hidden_of(normed[...], gate_up[0], gate_up[1]), down[...])
 
@@ -279,13 +292,16 @@
         parts = kept[...] + got[...].astype(F32) + got_z[...].astype(F32)
         done[...] = (mid[...].astype(F32) + parts).astype(BF16)
 
-    spread = mm(done[...], unpool[...].reshape(CC, 512)).astype(BF16).astype(F32)
-    start = pl.multiple_of(step * 128, 128)
     two = block_two[...].astype(F32)
-    children[pl.ds(start, CROWS), :] = (two[:CROWS] + spread[:, :C]).astype(BF16)
-    children[pl.ds(start + CROWS, CROWS), :] = (two[CROWS:] + spread[:, C:]).astype(BF16)
-
-    @pl.when(step == N_HID - 1)
+    for at in range(2):
+        spread = mm(done[...], unpool[:, at].reshape(CC, 512)).astype(BF16).astype(F32)
+        for half in range(2):
+            top = 128 * at + 64 * half
+            start = pl.multiple_of(step * 256 + top, 64)
+            added = two[top : top + CROWS] + spread[:, C * half : C * half + C]
+            children[pl.ds(start, CROWS), :] = added.astype(BF16)
+
+    @pl.when(step == STEPS - 1)
     def _():
         for chunk in range(4):
             point = iota((256, PTS), 0) + chunk * 256
@@ -310,7 +326,7 @@
 
 def unit(which):
     return pl.BlockSpec(
-        (N_BALL, 1, 64, 512), lambda i: (0, jnp.minimum(i, N_HID - 1), which, 0)
+        (N_BALL, 2, 64, 512), lambda i: (0, jnp.minimum(i, STEPS - 1), which, 0)
     )
 
 
@@ -423,21 +439,19 @@
         cost_estimate=pl.CostEstimate(flops=6 * 10**9, bytes_accessed=2 * 2**20, transcendentals=0),
         name="prep",
     )(points, tree_slot.reshape(1, PTS), rotated_slot.reshape(1, PTS))
+    far_piece, send = lax.optimization_barrier((far_z(mlp_piece), send))
+    far_mlp = lax.all_gather(far_piece, "ball")
     first = exchange(send)
     fine_weights = (fine_norm, fine_qkv, fine_out, fine_gate_up, fine_down)
     rows = exchange(fine(0, first, first, slots, *fine_weights))
-    mlp_piece, rows = lax.optimization_barrier((mlp_piece, rows))
-    answers = fine(1, rows, first, slots, *fine_weights)
-    far_piece, answers = lax.optimization_barrier((far_z(mlp_piece), answers))
-    far_mlp = lax.all_gather(far_piece, "ball")
-    returned = exchange(answers)
+    returned = exchange(fine(1, rows, first, slots, *fine_weights))
 
     block_two, coarse = pl.pallas_call(
         pool_kernel,
-        grid=(N_HID,),
+        grid=(STEPS,),
         out_shape=(shape((PTS, C), BF16), shape((CROWS, CC), BF16)),
         in_specs=[whole((SLOTS, C)), whole((2, PTS)), unit(0)],
-        out_specs=(pl.BlockSpec((128, C), lambda i: (i, 0)), whole((CROWS, CC))),
+        out_specs=(pl.BlockSpec((256, C), lambda i: (i, 0)), whole((CROWS, CC))),
         scratch_shapes=[pltpu.VMEM((CROWS, CC), F32)],
         compiler_params=params(),
         name="pool",
@@ -448,7 +462,7 @@
     rows_256 = whole((4 * CROWS, CC))
     mid, normed, partial = pl.pallas_call(
         attn_kernel,
-        grid=(N_HID + 2,),
+        grid=(STEPS + 2,),
         out_shape=(
             shape((CROWS, CC), BF16),
             shape((4 * CROWS, CC), BF16),
@@ -461,14 +475,14 @@
             rows_64,
             whole((2, CC)),
             unit(2),
-            hidden_half(N_HID, True),
-            hidden_half(N_HID, False),
+            hidden_half(STEPS, True),
+            hidden_half(STEPS, False),
         ],
         out_specs=(rows_64, rows_256, rows_256),
         scratch_shapes=[
             pltpu.VMEM((4 * CROWS, CC), BF16),
             pltpu.VMEM((4 * CROWS, CC), F32),
-            pltpu.VMEM((128, CC), BF16),
+            pltpu.VMEM((256, CC), BF16),
         ],
         compiler_params=params(),
         name="attn",
@@ -502,7 +516,7 @@
     got_z = other_z((kept_z + got[CROWS:].astype(F32)).astype(BF16))
     return pl.pallas_call(
         unpool_kernel,
-        grid=(N_HID,),
+        grid=(STEPS,),
         out_shape=shape((PTS, C), BF16),
         in_specs=[
             rows_64,
@@ -510,7 +524,7 @@
             rows_64,
             rows_64,
             unit(1),
-            pl.BlockSpec((128, C), lambda i: (i, 0)),
+            pl.BlockSpec((256, C), lambda i: (i, 0)),
         ],
         out_specs=whole((PTS, C)),
         scratch_shapes=[pltpu.VMEM((CROWS, CC), BF16), pltpu.VMEM((PTS, C), BF16)],

time: 217 us -> 203 us (0.935)
  waiting for transfers between devices: 25.1 us -> 15.6 us
  Pallas kernels: 76.6 us -> 69.8 us
  starting transfers between devices: 4.29 us -> 10.8 us
  blocking collectives: 94 us -> 90.1 us
    pallas_call x3, Pallas kernels: 35.2 us -> 28.5 us  [the longest x1 11.6 us: body(): pl.pallas_call(attn_kernel, grid=(STEPS + 2,), out_shape=(shape((CROWS, C...]
    all_gather x1, waiting for transfers between devices: 12.6 us -> 7.2 us  [body(): far_mlp = lax.all_gather(far_piece, 'ball')]
    ppermute x1, starting transfers between devices: 0.01 us -> 4.67 us  [far_z(): return lax.ppermute(values, 'z', [(0, 3), (3, 0), (1, 2), (2, 1)])]
    all_to_all x3, blocking collectives: 94 us -> 90.1 us  [exchange(): return lax.all_to_all(values, ALL, split_axis=0, concat_axis=0, tiled=True)]
    all_gather x1, waiting for transfers between devices: 2.44 us -> 0.01 us  [body(): weights = lax.all_gather(piece, ALL).reshape(N_BALL, N_HID, 192, 512)]
    ppermute x3, starting transfers between devices: 2.46 us -> 4.75 us  [other_core(): return lax.ppermute(values, 'core', [(0, 1), (1, 0)])]
  transfers between devices with their start and end apart: 8 -> 8, of which waited for: 6 -> 5; matrix products, arithmetic and copies ran while one was open for 0% -> 0% of each run, Pallas kernels for 29% -> 28%
where the time goes in v8:
time: 203 us
  blocking collectives  90.1 us (44%)
  Pallas kernels  69.8 us (34%)
  waiting for transfers between devices  15.6 us (8%)
  between operations  13.4 us (7%)
  starting transfers between devices  10.8 us (5%)
    all_to_all x3, blocking collectives, exchange(): return lax.all_to_all(values, ALL, split_axis=0, concat_axis=0, tiled=True)  90.1 us
    pallas_call x2, Pallas kernels, fine(): pl.pallas_call(functools.partial(fine_kernel, which), grid=(1,), out_shap...  29.1 us
    pallas_call x1, Pallas kernels, body(): pl.pallas_call(attn_kernel, grid=(STEPS + 2,), out_shape=(shape((CROWS, C...  11.6 us
    pallas_call x1, Pallas kernels, body(): pl.pallas_call(pool_kernel, grid=(STEPS,), out_shape=(shape((PTS, C), BF1...  10.2 us
    all_gather x1, waiting for transfers between devices, body(): far_mlp = lax.all_gather(far_piece, 'ball')  7.2 us
    pallas_call x1, Pallas kernels, body(): pl.pallas_call(unpool_kernel, grid=(STEPS,), out_shape=shape((PTS, C), BF...  6.73 us
    pallas_call x1, Pallas kernels, body(): pl.pallas_call(prep_kernel, out_shape=(shape((SLOTS, C + N_DEV), BF16), s...  6.22 us
    ppermute x2, waiting for transfers between devices, other_z(): return lax.ppermute(values, 'z', [(0, 1), (1, 0), (2, 3), (3, 2)])  6.01 us
  transfers between devices with their start and end apart: 8, of which 5 were waited for; matrix products, arithmetic and copies ran while one was open for 0% of the time, Pallas kernels for 28%

profile of v8, /device:TPU:1, one launch (start us, length us, event | category | flops | bytes accessed | tf_op | source)
XLA Modules:
  0.0 202.8 jit_solution(17540933364509285067)
XLA Ops:
  6.5 1.7 cut.1
  8.3 4.7 %collective-permute-start = (bf16[192,512]{1,0:T(8,128)(2,1)}, bf16[192,512]{1,0:T(8,128)(2,1)S(1)}, u32[]{:S(2)}, u32[]{:S(2)}) collective-permute-start(bf16[192,512]{1,0:T(8,128)(2,1)} %get-tuple-element.19), channel_id=1, source_target_pairs={{0,6},{6,0},{2,4},{4,2},{1,7},{7,1},{3,5},{5,3},{8,14},{14,8},{10,... | collective-permute-start | bytes 589832 | tf_op jit(solution)/shard_map/ppermute | solution.py:363
  13.0 6.2 %prep.1 = (bf16[2048,384]{1,0:T(8,128)(2,1)}, s32[2,1024]{1,0:T(2,128)}) custom-call(bf16[1024,256]{1,0:T(8,128)(2,1)} %points.1, s32[1,1024]{1,0:T(1,128)} %bitcast.25, s32[1,1024]{1,0:T(1,128)} %bitcast.26), custom_call_target="tpu_custom_call" | custom-call | flops 6000000000 | bytes 2097152 | tf_op jit(solution)/shard_map/prep/pallas_call | solution.py:435
  19.2 0.7 copy-done.1
  20.0 34.4 %all_to_all.33 = bf16[128,16,384]{2,1,0:T(8,128)(2,1)} all-to-all(bf16[128,16,384]{2,1,0:T(8,128)(2,1)} %bitcast.18), channel_id=1, replica_groups=mesh['ball'=16,'z'=4,'core'=2] {'ball','z','core'}, dimensions={0} | all-to-all | bytes 3145728 | tf_op jit(solution)/shard_map/all_to_all | solution.py:351
  54.3 14.5 %fine_block_0.1 = bf16[2048,256]{1,0:T(8,128)(2,1)} custom-call(bf16[2048,384]{1,0:T(8,128)(2,1)} %bitcast.19, bf16[2048,384]{1,0:T(8,128)(2,1)} %bitcast.20, s32[2,1024]{1,0:T(2,128)} %get-tuple-element.22.slots, f32[2,2,256]{2,1,0:T(2,128)} %gains.4, bf16[2,3,256,256]{3,2,1,0:T(8,128)(2,1)} %qkv.5, bf16[2,256,256]{2,1,0:T(8,128)(2,1)} %out.5, ...), custom_call_target="tpu_custom_call" | custom-call | flops 8000000000 | bytes 4194304 | tf_op jit(solution)/shard_map/fine_block_0/pallas_call | solution.py:367
  68.9 29.6 %all_to_all.34 = bf16[128,16,256]{2,1,0:T(8,128)(2,1)} all-to-all(bf16[128,16,256]{2,1,0:T(8,128)(2,1)} %bitcast.24), channel_id=1, replica_groups=mesh['ball'=16,'z'=4,'core'=2] {'ball','z','core'}, dimensions={0} | all-to-all | bytes 2097152 | tf_op jit(solution)/shard_map/all_to_all | solution.py:351
  98.5 14.6 %fine_block_1.1 = bf16[2048,256]{1,0:T(8,128)(2,1)} custom-call(bf16[2048,256]{1,0:T(8,128)(2,1)} %bitcast.22, bf16[2048,384]{1,0:T(8,128)(2,1)} %bitcast.21, s32[2,1024]{1,0:T(2,128)} %get-tuple-element.22.slots, f32[2,2,256]{2,1,0:T(2,128)} %gains.4, bf16[2,3,256,256]{3,2,1,0:T(8,128)(2,1)} %qkv.5, bf16[2,256,256]{2,1,0:T(8,128)(2,1)} %out.5, ...), custom_call_target="tpu_custom_call" | custom-call | flops 8000000000 | bytes 4194304 | tf_op jit(solution)/shard_map/fine_block_1/pallas_call | solution.py:367
  113.1 26.1 %all_to_all.35 = bf16[128,16,256]{2,1,0:T(8,128)(2,1)} all-to-all(bf16[128,16,256]{2,1,0:T(8,128)(2,1)} %bitcast.23), channel_id=1, replica_groups=mesh['ball'=16,'z'=4,'core'=2] {'ball','z','core'}, dimensions={0} | all-to-all | bytes 2097152 | tf_op jit(solution)/shard_map/all_to_all | solution.py:351
  139.2 10.2 %pool.3 = (bf16[1024,256]{1,0:T(8,128)(2,1)}, bf16[64,1024]{1,0:T(8,128)(2,1)}) custom-call(bf16[2048,256]{1,0:T(8,128)(2,1)} %bitcast.17, s32[2,1024]{1,0:T(2,128)} %get-tuple-element.22.slots, bf16[16,8,192,512]{3,2,1,0:T(8,128)(2,1)} %bitcast.11), custom_call_target="tpu_custom_call" | custom-call | tf_op jit(solution)/shard_map/pool/pallas_call | solution.py:449
  149.3 1.5 collective-permute-start.2
  150.8 2.6 %collective-permute-done.1.from_z = bf16[64,1024]{1,0:T(8,128)(2,1)S(1)} collective-permute-done((bf16[64,1024]{1,0:T(8,128)(2,1)}, bf16[64,1024]{1,0:T(8,128)(2,1)S(1)}, u32[]{:S(2)}, u32[]{:S(2)}) %collective-permute-start.1) | collective-permute-done | bytes 131104 | tf_op jit(solution)/shard_map/ppermute | solution.py:359
  153.4 2.3 %collective-permute-start.3 = (bf16[64,1024]{1,0:T(8,128)(2,1)S(1)}, bf16[64,1024]{1,0:T(8,128)(2,1)S(1)}, u32[]{:S(2)}, u32[]{:S(2)}) collective-permute-start(bf16[64,1024]{1,0:T(8,128)(2,1)S(1)} %collective-permute-done.1.from_z), channel_id=1, source_target_pairs={{0,1},{1,0},{2,3},{3,2},{4,5},{5,4},{6,7},{7,6},{8,9},{9,8},{10,11... | collective-permute-start | bytes 393224 | tf_op jit(solution)/shard_map/ppermute | solution.py:355
  155.7 1.0 collective-permute-done.3.pair_z
  157.3 11.6 %attn.1 = (bf16[64,1024]{1,0:T(8,128)(2,1)}, bf16[256,1024]{1,0:T(8,128)(2,1)}, f32[256,1024]{1,0:T(8,128)}) custom-call(bf16[64,1024]{1,0:T(8,128)(2,1)} %get-tuple-element.24.own, bf16[64,1024]{1,0:T(8,128)(2,1)} %copy-done.2, bf16[64,1024]{1,0:T(8,128)(2,1)} %copy-done.3, bf16[64,1024]{1,0:T(8,128)(2,1)} %copy-done.4, f32[2,1024]{1,0:T(2,128)} %gains.5, ...), custom_call_target="tpu_custom_call" | custom-call | tf_op jit(solution)/shard_map/attn/pallas_call | solution.py:463
  168.9 7.2 %all-gather.7.cloned.1.call-done = bf16[3072,512]{1,0:T(8,128)(2,1)} async-done(((bf16[192,512]{1,0:T(8,128)(2,1)}), bf16[3072,512]{1,0:T(8,128)(2,1)}) %all-gather.7.cloned.1.call-update) | async-done | bytes 3145744 | tf_op jit(solution)/shard_map/all_gather | solution.py:443
  176.1 4.3 %mlp.1 = (f32[64,1024]{1,0:T(8,128)}, f32[64,1024]{1,0:T(8,128)}, bf16[128,1024]{1,0:T(8,128)(2,1)}) custom-call(bf16[256,1024]{1,0:T(8,128)(2,1)} %get-tuple-element.26.normed, f32[256,1024]{1,0:T(8,128)} %get-tuple-element.27.partial, bf16[16,192,512]{2,1,0:T(8,128)(2,1)} %bitcast.14, bf16[16,192,512]{2,1,0:T(8,128)(2,1)} %bitcast.15, ...), custom_call_target="tpu_custom_call" | custom-call | tf_op jit(solution)/shard_map/mlp/pallas_call | solution.py:500
  180.3 1.0 collective-permute-start.4
  181.3 1.4 collective-permute-done.4.got
  182.7 1.1 add_convert_fusion
  183.8 1.3 collective-permute-start.5
  185.1 3.4 %collective-permute-done.5.got_z = bf16[64,1024]{1,0:T(8,128)(2,1)S(1)} collective-permute-done((bf16[64,1024]{1,0:T(8,128)(2,1)S(1)}, bf16[64,1024]{1,0:T(8,128)(2,1)S(1)}, u32[]{:S(2)}, u32[]{:S(2)}) %collective-permute-start.5) | collective-permute-done | bytes 131104 | tf_op jit(solution)/shard_map/ppermute | solution.py:359
  188.6 0.7 copy-done.5
  189.2 6.7 %unpool.3 = bf16[1024,256]{1,0:T(8,128)(2,1)} custom-call(bf16[64,1024]{1,0:T(8,128)(2,1)} %get-tuple-element.25.mid, f32[64,1024]{1,0:T(8,128)} %get-tuple-element.29.kept, bf16[128,1024]{1,0:T(8,128)(2,1)} %copy-done, bf16[64,1024]{1,0:T(8,128)(2,1)} %copy-done.5, bf16[16,8,192,512]{3,2,1,0:T(8,128)(2,1)} %bitcast.13, ...), custom_call_target="tpu_custom_call" | custom-call | tf_op jit(solution)/shard_map/unpool/pallas_call | solution.py:517
  (18 shorter events, 0.7 us)
Async XLA Ops:
  6.5 132.6 %all-gather.5.cloned.1.call-start = ((), (), s32[]{:S(2)}) async-start(), calls=%async_computation.3 | async-start | bytes 25362432 | tf_op jit(solution)/shard_map/all_gather | solution.py:433
  8.3 167.8 %all-gather.7.cloned.1.call-start = ((), (), s32[]{:S(2)}) async-start(), calls=%async_computation.4 | async-start | bytes 3342336 | tf_op jit(solution)/shard_map/all_gather | solution.py:443
  8.3 10.9 %collective-permute-start = (bf16[192,512]{1,0:T(8,128)(2,1)}, bf16[192,512]{1,0:T(8,128)(2,1)S(1)}, u32[]{:S(2)}, u32[]{:S(2)}) collective-permute-start(bf16[192,512]{1,0:T(8,128)(2,1)} %get-tuple-element.19), channel_id=1, source_target_pairs={{0,6},{6,0},{2,4},{4,2},{1,7},{7,1},{3,5},{5,3},{8,14},{14,8},{10,... | collective-permute-start | bytes 589832 | tf_op jit(solution)/shard_map/ppermute | solution.py:363
  19.2 0.7 copy-start.1
  149.3 4.0 %collective-permute-start.1 = (bf16[64,1024]{1,0:T(8,128)(2,1)}, bf16[64,1024]{1,0:T(8,128)(2,1)S(1)}, u32[]{:S(2)}, u32[]{:S(2)}) collective-permute-start(bf16[64,1024]{1,0:T(8,128)(2,1)} %get-tuple-element.24.own), channel_id=1, source_target_pairs={{0,2},{2,0},{4,6},{6,4},{1,3},{3,1},{5,7},{7,5},{8,10},{10,8},{12,... | collective-permute-start | bytes 393224 | tf_op jit(solution)/shard_map/ppermute | solution.py:359
  149.3 6.3 %collective-permute-start.2 = (bf16[64,1024]{1,0:T(8,128)(2,1)}, bf16[64,1024]{1,0:T(8,128)(2,1)S(1)}, u32[]{:S(2)}, u32[]{:S(2)}) collective-permute-start(bf16[64,1024]{1,0:T(8,128)(2,1)} %get-tuple-element.24.own), channel_id=1, source_target_pairs={{0,1},{1,0},{2,3},{3,2},{4,5},{5,4},{6,7},{7,6},{8,9},{9,8},{10,11... | collective-permute-start | bytes 393224 | tf_op jit(solution)/shard_map/ppermute | solution.py:355
  153.4 3.3 %copy-start.2 = (bf16[64,1024]{1,0:T(8,128)(2,1)}, bf16[64,1024]{1,0:T(8,128)(2,1)S(1)}, u32[]{:S(2)}) copy-start(bf16[64,1024]{1,0:T(8,128)(2,1)S(1)} %collective-permute-done.1.from_z) | copy-start | bytes 393220
  153.4 3.3 %collective-permute-start.3 = (bf16[64,1024]{1,0:T(8,128)(2,1)S(1)}, bf16[64,1024]{1,0:T(8,128)(2,1)S(1)}, u32[]{:S(2)}, u32[]{:S(2)}) collective-permute-start(bf16[64,1024]{1,0:T(8,128)(2,1)S(1)} %collective-permute-done.1.from_z), channel_id=1, source_target_pairs={{0,1},{1,0},{2,3},{3,2},{4,5},{5,4},{6,7},{7,6},{8,9},{9,8},{10,11... | collective-permute-start | bytes 393224 | tf_op jit(solution)/shard_map/ppermute | solution.py:355
  155.7 1.0 copy-start.3
  156.7 0.6 copy-start.4
  180.3 2.4 %collective-permute-start.4 = (bf16[128,1024]{1,0:T(8,128)(2,1)}, bf16[128,1024]{1,0:T(8,128)(2,1)S(1)}, u32[]{:S(2)}, u32[]{:S(2)}) collective-permute-start(bf16[128,1024]{1,0:T(8,128)(2,1)} %get-tuple-element.30), channel_id=1, source_target_pairs={{0,1},{1,0},{2,3},{3,2},{4,5},{5,4},{6,7},{7,6},{8,9},{9,8},{10,11... | collective-permute-start | bytes 786440 | tf_op jit(solution)/shard_map/ppermute | solution.py:355
  182.7 5.9 %copy-start = (bf16[128,1024]{1,0:T(8,128)(2,1)}, bf16[128,1024]{1,0:T(8,128)(2,1)S(1)}, u32[]{:S(2)}) copy-start(bf16[128,1024]{1,0:T(8,128)(2,1)S(1)} %collective-permute-done.4.got) | copy-start | bytes 786436
  183.8 4.8 %collective-permute-start.5 = (bf16[64,1024]{1,0:T(8,128)(2,1)S(1)}, bf16[64,1024]{1,0:T(8,128)(2,1)S(1)}, u32[]{:S(2)}, u32[]{:S(2)}) collective-permute-start(bf16[64,1024]{1,0:T(8,128)(2,1)S(1)} %add_convert_fusion), channel_id=1, source_target_pairs={{0,2},{2,0},{4,6},{6,4},{1,3},{3,1},{5,7},{7,5},{8,10},{10,8},{12,... | collective-permute-start | bytes 393224 | tf_op jit(solution)/shard_map/ppermute | solution.py:359
  188.6 0.7 copy-start.5
Sparse Core Ops, SparseCore 0:
  10.4 117.6 all-gather.4
  130.3 45.7 all-gather.6
